TPU v7x, 32 devices: a whole 2x2x4 slice. The times are simulated.
32 devices in a mesh: outer: 4 (over x, core), inner: 8 (over z, y).
Axes of the slice: x: 2, y: 2, z: 4, core: 2. Of those that a mesh axis runs over, the one named last changes fastest.
Arguments:
- queries: bfloat16 [4096, 4096], P(('outer', 'inner')), may hold values from -200 to 200
- keys: bfloat16 [4096, 1024], P(('outer', 'inner')), may hold values from -6 to 6
- values: bfloat16 [4096, 1024], P(('outer', 'inner')), may hold values from -6 to 6
- lengths: int32 [8], replicated, may hold values from 1 to 1024, as said below
- pack_order: int32 [8], replicated, may hold values from 0 to 7, as said below
Outputs:
- attended: bfloat16 [4096, 4096], P(('outer', 'inner'))
Inputs may be any that keep to these rules, and one draw needn't show every extreme that they name: 8 lengths that sum to 4096; the document packed first, lengths[pack_order[0]], has exactly 1024 tokens. `pack_order`: each of 0 to 7 exactly once.
All inputs are finite; a program needn't handle non-finite values.
Results may differ from a plain program's by a relative error of at most 0.0046.
Values may be sent and summed in bfloat16 or wider, within the bound.
No kernel may reach another device: no remote copies, remote signals or barrier semaphores. Data moves between devices by JAX's collectives and lax.ppermute only.
A program may use at most 64 MiB of HBM per device.

v0:
```python
import jax
import jax.numpy as jnp
from jax import lax
from jax.sharding import PartitionSpec as P

HD = 128
HOPS = 8


def shifted(block, axis, distance):
    devices = range(lax.axis_size(axis))
    route = [(i - distance, i) for i in devices if i - distance in devices]
    return lax.ppermute(block, axis, route)


def segment_ids(lengths, pack_order, positions):
    placed = jnp.take(lengths, pack_order)
    doc_starts = jnp.cumsum(placed) - placed
    counted = (doc_starts[None, :] <= positions[:, None]).astype(jnp.int32)
    return jnp.sum(counted, axis=1) - 1


def attend(queries, key_set, value_set, allowed):
    shard_rows = queries.shape[0]
    kv_heads = key_set.shape[1] // HD
    group_size = queries.shape[1] // key_set.shape[1]
    width = group_size * HD
    inv_root = jnp.sqrt(jnp.float32(HD))

    def per_group(head_group, output):
        query_part = lax.dynamic_slice_in_dim(queries, head_group * width, width, 1).reshape(
            shard_rows, group_size, HD
        )
        key_part = lax.dynamic_slice_in_dim(key_set, head_group * HD, HD, 1)
        value_part = lax.dynamic_slice_in_dim(value_set, head_group * HD, HD, 1)
        scores = (
            jnp.einsum("tjd,kd->jtk", query_part, key_part, preferred_element_type=jnp.float32)
            / inv_root
        )
        scores = jnp.where(allowed[None], scores, -jnp.inf)
        largest = jnp.max(scores, axis=-1, keepdims=True)
        exps = jnp.exp(scores - largest)
        weights = (exps / jnp.sum(exps, axis=-1, keepdims=True)).astype(jnp.bfloat16)
        mixed = jnp.einsum("jtk,kd->tjd", weights, value_part, preferred_element_type=jnp.float32)
        mixed = mixed.reshape(shard_rows, width).astype(jnp.bfloat16)
        return lax.dynamic_update_slice_in_dim(output, mixed, head_group * width, 1)

    initial = jnp.zeros(queries.shape, jnp.bfloat16)
    return lax.fori_loop(0, kv_heads, per_group, initial)


def shards(queries, keys, values, lengths, pack_order):
    shard_rows = queries.shape[0]
    device = lax.axis_index(("outer", "inner"))
    first_row = device * shard_rows
    received = []
    passed = (keys, values)
    for distance in range(1, HOPS + 1):
        passed = shifted((passed[0], passed[1]), ("outer", "inner"), 1)
        received.append(passed)
    ordered = received[::-1]
    key_all = jnp.concatenate([pair[0] for pair in ordered] + [keys], axis=0)
    value_all = jnp.concatenate([pair[1] for pair in ordered] + [values], axis=0)
    window = key_all.shape[0]
    query_pos = first_row + jnp.arange(shard_rows, dtype=jnp.int32)
    key_pos = first_row - HOPS * shard_rows + jnp.arange(window, dtype=jnp.int32)
    query_seg = segment_ids(lengths, pack_order, query_pos)
    key_seg = segment_ids(lengths, pack_order, key_pos)
    allowed = (
        (key_pos[None, :] >= 0)
        & (key_pos[None, :] <= query_pos[:, None])
        & (key_seg[None, :] == query_seg[:, None])
    )
    attended = attend(queries, key_all, value_all, allowed)
    return attended


def solution(mesh):
    in_specs = (
        P(("outer", "inner"), None),
        P(("outer", "inner"), None),
        P(("outer", "inner"), None),
        P(),
        P(),
    )
    out_specs = P(("outer", "inner"), None)
    return jax.shard_map(shards, mesh=mesh, in_specs=in_specs, out_specs=out_specs, check_vma=False)
```

profile of v0, /device:TPU:2, one launch (start us, length us, event | category | flops | bytes accessed | tf_op | source)
XLA Modules:
  0.0 176.3 jit_solution(834456888854591985)
XLA Ops:
  1.1 3.4 %collective-permute-start = (bf16[128,1024]{0,1:T(8,128)(2,1)S(1)}, bf16[128,1024]{0,1:T(8,128)(2,1)S(1)}, u32[]{:S(2)}, u32[]{:S(2)}) collective-permute-start(bf16[128,1024]{0,1:T(8,128)(2,1)S(1)} %copy.18), channel_id=1, source_target_pairs={{0,1},{1,2},{2,3},{3,4},{4,5},{5,6},{6,7},{7,8},{8,9},{9,10},{10,1... | collective-permute-start | bytes 786440 | tf_op jit(solution)/shard_map/ppermute | solution.py:13
  4.6 3.4 %collective-permute-start.8 = (bf16[128,1024]{1,0:T(8,128)(2,1)}, bf16[128,1024]{1,0:T(8,128)(2,1)S(1)}, u32[]{:S(2)}, u32[]{:S(2)}) collective-permute-start(bf16[128,1024]{1,0:T(8,128)(2,1)} %param.10), channel_id=1, source_target_pairs={{0,1},{1,2},{2,3},{3,4},{4,5},{5,6},{6,7},{7,8},{8,9},{9,10},{10,1... | collective-permute-start | bytes 786440 | tf_op jit(solution)/shard_map/ppermute | solution.py:13
  8.0 8.7 %collective-permute-done = bf16[128,1024]{0,1:T(8,128)(2,1)S(1)} collective-permute-done((bf16[128,1024]{0,1:T(8,128)(2,1)S(1)}, bf16[128,1024]{0,1:T(8,128)(2,1)S(1)}, u32[]{:S(2)}, u32[]{:S(2)}) %collective-permute-start) | collective-permute-done | bytes 262176 | tf_op jit(solution)/shard_map/ppermute | solution.py:13
  22.3 8.0 %collective-permute-done.1 = bf16[128,1024]{0,1:T(8,128)(2,1)S(1)} collective-permute-done((bf16[128,1024]{0,1:T(8,128)(2,1)S(1)}, bf16[128,1024]{0,1:T(8,128)(2,1)S(1)}, u32[]{:S(2)}, u32[]{:S(2)}) %collective-permute-start.1) | collective-permute-done | bytes 262176 | tf_op jit(solution)/shard_map/ppermute | solution.py:13
  32.2 3.7 %collective-permute-done.9 = bf16[128,1024]{1,0:T(8,128)(2,1)S(1)} collective-permute-done((bf16[128,1024]{1,0:T(8,128)(2,1)S(1)}, bf16[128,1024]{1,0:T(8,128)(2,1)S(1)}, u32[]{:S(2)}, u32[]{:S(2)}) %collective-permute-start.9) | collective-permute-done | bytes 262176 | tf_op jit(solution)/shard_map/ppermute | solution.py:13
  37.9 6.4 %collective-permute-done.2 = bf16[128,1024]{0,1:T(8,128)(2,1)S(1)} collective-permute-done((bf16[128,1024]{0,1:T(8,128)(2,1)S(1)}, bf16[128,1024]{0,1:T(8,128)(2,1)S(1)}, u32[]{:S(2)}, u32[]{:S(2)}) %collective-permute-start.2) | collective-permute-done | bytes 262176 | tf_op jit(solution)/shard_map/ppermute | solution.py:13
  47.5 2.5 %collective-permute-done.10 = bf16[128,1024]{1,0:T(8,128)(2,1)S(1)} collective-permute-done((bf16[128,1024]{1,0:T(8,128)(2,1)S(1)}, bf16[128,1024]{1,0:T(8,128)(2,1)S(1)}, u32[]{:S(2)}, u32[]{:S(2)}) %collective-permute-start.10) | collective-permute-done | bytes 262176 | tf_op jit(solution)/shard_map/ppermute | solution.py:13
  51.9 6.7 %collective-permute-done.3 = bf16[128,1024]{0,1:T(8,128)(2,1)S(1)} collective-permute-done((bf16[128,1024]{0,1:T(8,128)(2,1)S(1)}, bf16[128,1024]{0,1:T(8,128)(2,1)S(1)}, u32[]{:S(2)}, u32[]{:S(2)}) %collective-permute-start.3) | collective-permute-done | bytes 262176 | tf_op jit(solution)/shard_map/ppermute | solution.py:13
  65.8 6.4 %collective-permute-done.4 = bf16[128,1024]{0,1:T(8,128)(2,1)S(1)} collective-permute-done((bf16[128,1024]{0,1:T(8,128)(2,1)S(1)}, bf16[128,1024]{0,1:T(8,128)(2,1)S(1)}, u32[]{:S(2)}, u32[]{:S(2)}) %collective-permute-start.4) | collective-permute-done | bytes 262176 | tf_op jit(solution)/shard_map/ppermute | solution.py:13
  74.2 3.8 %collective-permute-done.12 = bf16[128,1024]{1,0:T(8,128)(2,1)S(1)} collective-permute-done((bf16[128,1024]{1,0:T(8,128)(2,1)S(1)}, bf16[128,1024]{1,0:T(8,128)(2,1)S(1)}, u32[]{:S(2)}, u32[]{:S(2)}) %collective-permute-start.12) | collective-permute-done | bytes 262176 | tf_op jit(solution)/shard_map/ppermute | solution.py:13
  79.9 6.5 %collective-permute-done.5 = bf16[128,1024]{0,1:T(8,128)(2,1)} collective-permute-done((bf16[128,1024]{0,1:T(8,128)(2,1)S(1)}, bf16[128,1024]{0,1:T(8,128)(2,1)}, u32[]{:S(2)}, u32[]{:S(2)}) %collective-permute-start.5) | collective-permute-done | bytes 262176 | tf_op jit(solution)/shard_map/ppermute | solution.py:13
  88.4 3.5 %collective-permute-done.13 = bf16[128,1024]{1,0:T(8,128)(2,1)S(1)} collective-permute-done((bf16[128,1024]{1,0:T(8,128)(2,1)S(1)}, bf16[128,1024]{1,0:T(8,128)(2,1)S(1)}, u32[]{:S(2)}, u32[]{:S(2)}) %collective-permute-start.13) | collective-permute-done | bytes 262176 | tf_op jit(solution)/shard_map/ppermute | solution.py:13
  93.8 7.3 %collective-permute-done.6 = bf16[128,1024]{0,1:T(8,128)(2,1)} collective-permute-done((bf16[128,1024]{0,1:T(8,128)(2,1)}, bf16[128,1024]{0,1:T(8,128)(2,1)}, u32[]{:S(2)}, u32[]{:S(2)}) %collective-permute-start.6) | collective-permute-done | bytes 262176 | tf_op jit(solution)/shard_map/ppermute | solution.py:13
  103.1 2.4 %collective-permute-done.14 = bf16[128,1024]{1,0:T(8,128)(2,1)} collective-permute-done((bf16[128,1024]{1,0:T(8,128)(2,1)S(1)}, bf16[128,1024]{1,0:T(8,128)(2,1)}, u32[]{:S(2)}, u32[]{:S(2)}) %collective-permute-start.14) | collective-permute-done | bytes 262176 | tf_op jit(solution)/shard_map/ppermute | solution.py:13
  107.4 5.3 %collective-permute-done.7 = bf16[128,1024]{0,1:T(8,128)(2,1)} collective-permute-done((bf16[128,1024]{0,1:T(8,128)(2,1)}, bf16[128,1024]{0,1:T(8,128)(2,1)}, u32[]{:S(2)}, u32[]{:S(2)}) %collective-permute-start.7) | collective-permute-done | bytes 262176 | tf_op jit(solution)/shard_map/ppermute | solution.py:13
  124.6 50.7 %while.14 = (s32[]{:T(128)}, bf16[128,4096]{1,0:T(8,128)(2,1)S(1)}, bf16[1152,1024]{0,1:T(8,128)(2,1)}, bf16[1152,1024]{1,0:T(8,128)(2,1)}, bf16[128,4096]{1,0:T...) while((s32[]{:T(128)}, bf16[128,4096]{1,0:T(8,128)(2,1)S(1)}, ...), condition=%wide.region_6.8_spmd.clone, body=%wide.region_3.7_spmd.clone.sunk | while | flops 458951424 | bytes 2785661 | solution.py:49
  128.5 2.2 %fusion.53 = bf16[128,4,128]{2,0,1:T(8,128)(2,1)S(1)} fusion(f32[4,128]{1,0:T(4,128)S(1)} %fusion.52, bf16[1152,1024]{0,1:T(8,128)(2,1)} %get-tuple-element.278, s32[]{:T(128)S(6)} %select_n.64, bf16[128,4,128]{0,2,1:T(8,128)(2,1)S(1)} %bitcast.59, pred[128,1152]{0,1:T(8,128)(4,1)S(1)} %compare_and_fusion.2, bf16[1152,1024]{1,0:T(8,128)(2,1)} %get-tuple-element.279), kind=kOutput, calls=%fused_computation.10.clone.1 | convolution fusion | flops 305006208 | bytes 1002496 | tf_op jit(solution)/shard_map/while/body/eval_jaxpr/jtk,kd->tjd/dot_general | solution.py:44
  134.9 2.2 %fusion.53 = bf16[128,4,128]{2,0,1:T(8,128)(2,1)S(1)} fusion(f32[4,128]{1,0:T(4,128)S(1)} %fusion.52, bf16[1152,1024]{0,1:T(8,128)(2,1)} %get-tuple-element.278, s32[]{:T(128)S(6)} %select_n.64, bf16[128,4,128]{0,2,1:T(8,128)(2,1)S(1)} %bitcast.59, pred[128,1152]{0,1:T(8,128)(4,1)S(1)} %compare_and_fusion.2, bf16[1152,1024]{1,0:T(8,128)(2,1)} %get-tuple-element.279), kind=kOutput, calls=%fused_computation.10.clone.1 | convolution fusion | flops 305006208 | bytes 1002496 | tf_op jit(solution)/shard_map/while/body/eval_jaxpr/jtk,kd->tjd/dot_general | solution.py:44
  141.2 2.2 %fusion.53 = bf16[128,4,128]{2,0,1:T(8,128)(2,1)S(1)} fusion(f32[4,128]{1,0:T(4,128)S(1)} %fusion.52, bf16[1152,1024]{0,1:T(8,128)(2,1)} %get-tuple-element.278, s32[]{:T(128)S(6)} %select_n.64, bf16[128,4,128]{0,2,1:T(8,128)(2,1)S(1)} %bitcast.59, pred[128,1152]{0,1:T(8,128)(4,1)S(1)} %compare_and_fusion.2, bf16[1152,1024]{1,0:T(8,128)(2,1)} %get-tuple-element.279), kind=kOutput, calls=%fused_computation.10.clone.1 | convolution fusion | flops 305006208 | bytes 1002496 | tf_op jit(solution)/shard_map/while/body/eval_jaxpr/jtk,kd->tjd/dot_general | solution.py:44
  147.6 2.2 %fusion.53 = bf16[128,4,128]{2,0,1:T(8,128)(2,1)S(1)} fusion(f32[4,128]{1,0:T(4,128)S(1)} %fusion.52, bf16[1152,1024]{0,1:T(8,128)(2,1)} %get-tuple-element.278, s32[]{:T(128)S(6)} %select_n.64, bf16[128,4,128]{0,2,1:T(8,128)(2,1)S(1)} %bitcast.59, pred[128,1152]{0,1:T(8,128)(4,1)S(1)} %compare_and_fusion.2, bf16[1152,1024]{1,0:T(8,128)(2,1)} %get-tuple-element.279), kind=kOutput, calls=%fused_computation.10.clone.1 | convolution fusion | flops 305006208 | bytes 1002496 | tf_op jit(solution)/shard_map/while/body/eval_jaxpr/jtk,kd->tjd/dot_general | solution.py:44
  153.9 2.2 %fusion.53 = bf16[128,4,128]{2,0,1:T(8,128)(2,1)S(1)} fusion(f32[4,128]{1,0:T(4,128)S(1)} %fusion.52, bf16[1152,1024]{0,1:T(8,128)(2,1)} %get-tuple-element.278, s32[]{:T(128)S(6)} %select_n.64, bf16[128,4,128]{0,2,1:T(8,128)(2,1)S(1)} %bitcast.59, pred[128,1152]{0,1:T(8,128)(4,1)S(1)} %compare_and_fusion.2, bf16[1152,1024]{1,0:T(8,128)(2,1)} %get-tuple-element.279), kind=kOutput, calls=%fused_computation.10.clone.1 | convolution fusion | flops 305006208 | bytes 1002496 | tf_op jit(solution)/shard_map/while/body/eval_jaxpr/jtk,kd->tjd/dot_general | solution.py:44
  160.2 2.2 %fusion.53 = bf16[128,4,128]{2,0,1:T(8,128)(2,1)S(1)} fusion(f32[4,128]{1,0:T(4,128)S(1)} %fusion.52, bf16[1152,1024]{0,1:T(8,128)(2,1)} %get-tuple-element.278, s32[]{:T(128)S(6)} %select_n.64, bf16[128,4,128]{0,2,1:T(8,128)(2,1)S(1)} %bitcast.59, pred[128,1152]{0,1:T(8,128)(4,1)S(1)} %compare_and_fusion.2, bf16[1152,1024]{1,0:T(8,128)(2,1)} %get-tuple-element.279), kind=kOutput, calls=%fused_computation.10.clone.1 | convolution fusion | flops 305006208 | bytes 1002496 | tf_op jit(solution)/shard_map/while/body/eval_jaxpr/jtk,kd->tjd/dot_general | solution.py:44
  166.6 2.2 %fusion.53 = bf16[128,4,128]{2,0,1:T(8,128)(2,1)S(1)} fusion(f32[4,128]{1,0:T(4,128)S(1)} %fusion.52, bf16[1152,1024]{0,1:T(8,128)(2,1)} %get-tuple-element.278, s32[]{:T(128)S(6)} %select_n.64, bf16[128,4,128]{0,2,1:T(8,128)(2,1)S(1)} %bitcast.59, pred[128,1152]{0,1:T(8,128)(4,1)S(1)} %compare_and_fusion.2, bf16[1152,1024]{1,0:T(8,128)(2,1)} %get-tuple-element.279), kind=kOutput, calls=%fused_computation.10.clone.1 | convolution fusion | flops 305006208 | bytes 1002496 | tf_op jit(solution)/shard_map/while/body/eval_jaxpr/jtk,kd->tjd/dot_general | solution.py:44
  172.9 2.2 %fusion.53 = bf16[128,4,128]{2,0,1:T(8,128)(2,1)S(1)} fusion(f32[4,128]{1,0:T(4,128)S(1)} %fusion.52, bf16[1152,1024]{0,1:T(8,128)(2,1)} %get-tuple-element.278, s32[]{:T(128)S(6)} %select_n.64, bf16[128,4,128]{0,2,1:T(8,128)(2,1)S(1)} %bitcast.59, pred[128,1152]{0,1:T(8,128)(4,1)S(1)} %compare_and_fusion.2, bf16[1152,1024]{1,0:T(8,128)(2,1)} %get-tuple-element.279), kind=kOutput, calls=%fused_computation.10.clone.1 | convolution fusion | flops 305006208 | bytes 1002496 | tf_op jit(solution)/shard_map/while/body/eval_jaxpr/jtk,kd->tjd/dot_general | solution.py:44
  (106 shorter events, 79.6 us)
Async XLA Ops:
  0.0 46.8 %copy-start = (s32[8]{0:T(128)S(1)}, s32[8]{0:T(128)}, u32[]{:S(2)}) copy-start(s32[8]{0:T(128)} %param.12) | copy-start | bytes 100
  1.1 15.6 %collective-permute-start = (bf16[128,1024]{0,1:T(8,128)(2,1)S(1)}, bf16[128,1024]{0,1:T(8,128)(2,1)S(1)}, u32[]{:S(2)}, u32[]{:S(2)}) collective-permute-start(bf16[128,1024]{0,1:T(8,128)(2,1)S(1)} %copy.18), channel_id=1, source_target_pairs={{0,1},{1,2},{2,3},{3,4},{4,5},{5,6},{6,7},{7,8},{8,9},{9,10},{10,1... | collective-permute-start | bytes 786440 | tf_op jit(solution)/shard_map/ppermute | solution.py:13
  4.6 15.8 %collective-permute-start.8 = (bf16[128,1024]{1,0:T(8,128)(2,1)}, bf16[128,1024]{1,0:T(8,128)(2,1)S(1)}, u32[]{:S(2)}, u32[]{:S(2)}) collective-permute-start(bf16[128,1024]{1,0:T(8,128)(2,1)} %param.10), channel_id=1, source_target_pairs={{0,1},{1,2},{2,3},{3,4},{4,5},{5,6},{6,7},{7,8},{8,9},{9,10},{10,1... | collective-permute-start | bytes 786440 | tf_op jit(solution)/shard_map/ppermute | solution.py:13
  16.7 13.6 %collective-permute-start.1 = (bf16[128,1024]{0,1:T(8,128)(2,1)S(1)}, bf16[128,1024]{0,1:T(8,128)(2,1)S(1)}, u32[]{:S(2)}, u32[]{:S(2)}) collective-permute-start(bf16[128,1024]{0,1:T(8,128)(2,1)S(1)} %collective-permute-done), channel_id=1, source_target_pairs={{0,1},{1,2},{2,3},{3,4},{4,5},{5,6},{6,7},{7,8},{8,9},{9,10},{10,1... | collective-permute-start | bytes 786440 | tf_op jit(solution)/shard_map/ppermute | solution.py:13
  20.4 15.6 %collective-permute-start.9 = (bf16[128,1024]{1,0:T(8,128)(2,1)S(1)}, bf16[128,1024]{1,0:T(8,128)(2,1)S(1)}, u32[]{:S(2)}, u32[]{:S(2)}) collective-permute-start(bf16[128,1024]{1,0:T(8,128)(2,1)S(1)} %collective-permute-done.8), channel_id=1, source_target_pairs={{0,1},{1,2},{2,3},{3,4},{4,5},{5,6},{6,7},{7,8},{8,9},{9,10},{10,1... | collective-permute-start | bytes 786440 | tf_op jit(solution)/shard_map/ppermute | solution.py:13
  30.3 13.9 %collective-permute-start.2 = (bf16[128,1024]{0,1:T(8,128)(2,1)S(1)}, bf16[128,1024]{0,1:T(8,128)(2,1)S(1)}, u32[]{:S(2)}, u32[]{:S(2)}) collective-permute-start(bf16[128,1024]{0,1:T(8,128)(2,1)S(1)} %collective-permute-done.1), channel_id=1, source_target_pairs={{0,1},{1,2},{2,3},{3,4},{4,5},{5,6},{6,7},{7,8},{8,9},{9,10},{10,1... | collective-permute-start | bytes 786440 | tf_op jit(solution)/shard_map/ppermute | solution.py:13
  36.0 14.1 %collective-permute-start.10 = (bf16[128,1024]{1,0:T(8,128)(2,1)S(1)}, bf16[128,1024]{1,0:T(8,128)(2,1)S(1)}, u32[]{:S(2)}, u32[]{:S(2)}) collective-permute-start(bf16[128,1024]{1,0:T(8,128)(2,1)S(1)} %collective-permute-done.9), channel_id=1, source_target_pairs={{0,1},{1,2},{2,3},{3,4},{4,5},{5,6},{6,7},{7,8},{8,9},{9,10},{10,1... | collective-permute-start | bytes 786440 | tf_op jit(solution)/shard_map/ppermute | solution.py:13
  44.2 14.4 %collective-permute-start.3 = (bf16[128,1024]{0,1:T(8,128)(2,1)S(1)}, bf16[128,1024]{0,1:T(8,128)(2,1)S(1)}, u32[]{:S(2)}, u32[]{:S(2)}) collective-permute-start(bf16[128,1024]{0,1:T(8,128)(2,1)S(1)} %collective-permute-done.2), channel_id=1, source_target_pairs={{0,1},{1,2},{2,3},{3,4},{4,5},{5,6},{6,7},{7,8},{8,9},{9,10},{10,1... | collective-permute-start | bytes 786440 | tf_op jit(solution)/shard_map/ppermute | solution.py:13
  50.0 13.8 %collective-permute-start.11 = (bf16[128,1024]{1,0:T(8,128)(2,1)S(1)}, bf16[128,1024]{1,0:T(8,128)(2,1)S(1)}, u32[]{:S(2)}, u32[]{:S(2)}) collective-permute-start(bf16[128,1024]{1,0:T(8,128)(2,1)S(1)} %collective-permute-done.10), channel_id=1, source_target_pairs={{0,1},{1,2},{2,3},{3,4},{4,5},{5,6},{6,7},{7,8},{8,9},{9,10},{10,1... | collective-permute-start | bytes 786440 | tf_op jit(solution)/shard_map/ppermute | solution.py:13
  58.6 13.6 %collective-permute-start.4 = (bf16[128,1024]{0,1:T(8,128)(2,1)S(1)}, bf16[128,1024]{0,1:T(8,128)(2,1)S(1)}, u32[]{:S(2)}, u32[]{:S(2)}) collective-permute-start(bf16[128,1024]{0,1:T(8,128)(2,1)S(1)} %collective-permute-done.3), channel_id=1, source_target_pairs={{0,1},{1,2},{2,3},{3,4},{4,5},{5,6},{6,7},{7,8},{8,9},{9,10},{10,1... | collective-permute-start | bytes 786440 | tf_op jit(solution)/shard_map/ppermute | solution.py:13
  63.9 14.2 %collective-permute-start.12 = (bf16[128,1024]{1,0:T(8,128)(2,1)S(1)}, bf16[128,1024]{1,0:T(8,128)(2,1)S(1)}, u32[]{:S(2)}, u32[]{:S(2)}) collective-permute-start(bf16[128,1024]{1,0:T(8,128)(2,1)S(1)} %collective-permute-done.11), channel_id=1, source_target_pairs={{0,1},{1,2},{2,3},{3,4},{4,5},{5,6},{6,7},{7,8},{8,9},{9,10},{10,1... | collective-permute-start | bytes 786440 | tf_op jit(solution)/shard_map/ppermute | solution.py:13
  72.2 14.2 %collective-permute-start.5 = (bf16[128,1024]{0,1:T(8,128)(2,1)S(1)}, bf16[128,1024]{0,1:T(8,128)(2,1)}, u32[]{:S(2)}, u32[]{:S(2)}) collective-permute-start(bf16[128,1024]{0,1:T(8,128)(2,1)S(1)} %collective-permute-done.4), channel_id=1, source_target_pairs={{0,1},{1,2},{2,3},{3,4},{4,5},{5,6},{6,7},{7,8},{8,9},{9,10},{10,1... | collective-permute-start | bytes 786440 | tf_op jit(solution)/shard_map/ppermute | solution.py:13
  78.0 13.9 %collective-permute-start.13 = (bf16[128,1024]{1,0:T(8,128)(2,1)S(1)}, bf16[128,1024]{1,0:T(8,128)(2,1)S(1)}, u32[]{:S(2)}, u32[]{:S(2)}) collective-permute-start(bf16[128,1024]{1,0:T(8,128)(2,1)S(1)} %collective-permute-done.12), channel_id=1, source_target_pairs={{0,1},{1,2},{2,3},{3,4},{4,5},{5,6},{6,7},{7,8},{8,9},{9,10},{10,1... | collective-permute-start | bytes 786440 | tf_op jit(solution)/shard_map/ppermute | solution.py:13
  86.4 14.7 %collective-permute-start.6 = (bf16[128,1024]{0,1:T(8,128)(2,1)}, bf16[128,1024]{0,1:T(8,128)(2,1)}, u32[]{:S(2)}, u32[]{:S(2)}) collective-permute-start(bf16[128,1024]{0,1:T(8,128)(2,1)} %collective-permute-done.5), channel_id=1, source_target_pairs={{0,1},{1,2},{2,3},{3,4},{4,5},{5,6},{6,7},{7,8},{8,9},{9,10},{10,1... | collective-permute-start | bytes 786440 | tf_op jit(solution)/shard_map/ppermute | solution.py:13
  91.9 13.6 %collective-permute-start.14 = (bf16[128,1024]{1,0:T(8,128)(2,1)S(1)}, bf16[128,1024]{1,0:T(8,128)(2,1)}, u32[]{:S(2)}, u32[]{:S(2)}) collective-permute-start(bf16[128,1024]{1,0:T(8,128)(2,1)S(1)} %collective-permute-done.13), channel_id=1, source_target_pairs={{0,1},{1,2},{2,3},{3,4},{4,5},{5,6},{6,7},{7,8},{8,9},{9,10},{10,1... | collective-permute-start | bytes 786440 | tf_op jit(solution)/shard_map/ppermute | solution.py:13
  101.1 11.6 %collective-permute-start.7 = (bf16[128,1024]{0,1:T(8,128)(2,1)}, bf16[128,1024]{0,1:T(8,128)(2,1)}, u32[]{:S(2)}, u32[]{:S(2)}) collective-permute-start(bf16[128,1024]{0,1:T(8,128)(2,1)} %collective-permute-done.6), channel_id=1, source_target_pairs={{0,1},{1,2},{2,3},{3,4},{4,5},{5,6},{6,7},{7,8},{8,9},{9,10},{10,1... | collective-permute-start | bytes 786440 | tf_op jit(solution)/shard_map/ppermute | solution.py:13
  105.5 11.5 %collective-permute-start.15 = (bf16[128,1024]{1,0:T(8,128)(2,1)}, bf16[128,1024]{1,0:T(8,128)(2,1)S(1)}, u32[]{:S(2)}, u32[]{:S(2)}) collective-permute-start(bf16[128,1024]{1,0:T(8,128)(2,1)} %collective-permute-done.14), channel_id=1, source_target_pairs={{0,1},{1,2},{2,3},{3,4},{4,5},{5,6},{6,7},{7,8},{8,9},{9,10},{10,1... | collective-permute-start | bytes 786440 | tf_op jit(solution)/shard_map/ppermute | solution.py:13
  116.1 7.6 %copy-start.2 = (bf16[128,1024]{1,0:T(8,128)(2,1)S(1)}, bf16[128,1024]{1,0:T(8,128)(2,1)}, u32[]{:S(2)}) copy-start(bf16[128,1024]{1,0:T(8,128)(2,1)} %param.10) | copy-start | bytes 786436
  116.2 7.5 %copy-start.3 = (bf16[1152,1024]{0,1:T(8,128)(2,1)}, bf16[1152,1024]{0,1:T(8,128)(2,1)S(1)}, u32[]{:S(2)}) copy-start(bf16[1152,1024]{0,1:T(8,128)(2,1)S(1)} %constant_dynamic-update-slice_fusion.1) | copy-start | bytes 7077892
  175.3 1.0 copy-start.1
where the time goes:
time: 178 us; the launch traced here: 176 us
  waiting for transfers between devices  75.6 us (42%)
  starting transfers between devices  33.6 us (19%)
  matrix products  32.4 us (18%)
  local copies, waits for them, and re-layouts  23 us (13%)
  other arithmetic  10.8 us (6%)
    ppermute x16, waiting for transfers between devices, shifted(): return lax.ppermute(block, axis, route)  75.6 us
    ppermute x16, starting transfers between devices, shifted(): return lax.ppermute(block, axis, route)  33.6 us
    dot_general x8, matrix products, per_group(): jnp.einsum('jtk,kd->tjd', weights, value_part, preferred_element_type=jnp...  17.7 us
    sub x8, matrix products, per_group(): exps = jnp.exp(scores - largest)  14.7 us
    unnamed x25, local copies, waits for them, and re-layouts  12.2 us
    and x8, other arithmetic, shards(): (key_pos[None, :] >= 0) & (key_pos[None, :] <= query_pos[:, None])  8.44 us
    dynamic_slice x16, local copies, waits for them, and re-layouts, per_group(): lax.dynamic_slice_in_dim(queries, head_group * width, width, 1)  8.29 us
  transfers between devices with their start and end apart: 16, of which 16 were waited for; matrix products, arithmetic and copies ran while one was open for 4% of the time, Pallas kernels for 0%

commit v1 on v0

v1 whole, which is shorter than its diff:
```python
import functools
import math

import jax
import jax.numpy as jnp
from jax import lax
from jax.experimental import pallas as pl
from jax.experimental.pallas import tpu as pltpu
from jax.sharding import PartitionSpec as P

HD = 128
HOPS = 8
FIRST = 1024
AXES = ("outer", "inner")
NEG = -1e30
SCALE = math.log2(math.e) / math.sqrt(HD)
RING = (0, 2, 4, 6, 7, 5, 3, 1)
OWN, MATE, NONE = 0, 1, 2
VMEM_LIMIT = 40 * 1024 * 1024
UNROLL = 4
FLOPS = 2_000_000_000


def make_plan(groups, first_blocks):
    m = len(RING)
    n = groups * m
    place = {j: p for p, j in enumerate(RING)}

    def held(d, j):
        o, i = divmod(d, m)
        if j == i:
            return d
        if o % 2 == 0 or j < i:
            return o * m + j
        return ((o + 2) % groups) * m + j

    def uses(q, b):
        return 0 < q - b <= HOPS and not (b < first_blocks <= q)

    def user(d, b):
        return d if uses(d, b) else d ^ m if uses(d ^ m, b) else None

    ops = [("A", 1), ("B", 1), ("A", 2), ("B", 2), ("A", 3), ("B", 3), ("A", 4)]
    route = {}
    for op, s in ops:
        route[op, s] = {}
        for d in range(n):
            o, i = divmod(d, m)
            way = 1 if (o % 2 == 0) == (op == "A") else -1
            j = RING[(place[i] - way * s) % m]
            b = held(d, j)
            behind = RING[(place[i] - way) % m]
            (source,) = [e for e in range(behind, n, m) if (e // m) % 2 == o % 2 and held(e, j) == b]
            route[op, s][d] = (source, b)
    for op, s in reversed(ops):
        sends_on = {e for e, _ in route.get((op, s + 1), {}).values()}
        route[op, s] = {d: r for d, r in route[op, s].items() if user(d, r[1]) is not None or d in sends_on}
    route["A", 4] = {user(d, b): (e, b) for d, (e, b) in route["A", 4].items()}
    return route, user


def block_table(route, user, groups):
    m = len(RING)
    n = groups * m
    rows = []
    for d in range(n):
        row = []
        for key in [("A", 1), ("B", 1), ("A", 2), ("B", 2), ("A", 3), ("B", 3), ("A", 4)]:
            if d not in route[key]:
                row += [0, NONE]
                continue
            b = route[key][d][1]
            u = d if key == ("A", 4) else user(d, b)
            row += [b, NONE if u is None else OWN if u == d else MATE]
        o = d // m
        row += [0, NONE] if o < 2 else [d if o % 2 == 0 else d - 2 * m, MATE]
        rows.append(row)
    return rows


def position(axes):
    outer, inner = axes
    return lax.axis_index(outer) * lax.axis_size(inner) + lax.axis_index(inner)


def doc_starts(lengths_ref, order_ref, fold, initial):
    def step(j, carry):
        start, value = carry
        value = fold(value, start)
        return start + lengths_ref[order_ref[j]], value

    return lax.fori_loop(0, order_ref.shape[0], step, (jnp.int32(0), initial), unroll=order_ref.shape[0] <= 8)[1]


def mask_bias(lengths_ref, order_ref, query_base, key_base, rows):
    query_pos = query_base + lax.broadcasted_iota(jnp.int32, (8, rows), 1)
    seen = doc_starts(
        lengths_ref,
        order_ref,
        lambda first, start: jnp.where(start <= query_pos, start, first),
        jnp.zeros((8, rows), jnp.int32),
    )
    seen, query_pos = (jnp.concatenate([x] * (rows // 8), axis=0) for x in (seen, query_pos))
    key_pos = key_base + lax.broadcasted_iota(jnp.int32, (rows, rows), 0)
    return jnp.where((key_pos >= seen) & (key_pos <= query_pos), 0.0, NEG).astype(jnp.float32)


def first_seen(lengths_ref, order_ref, query_base):
    return doc_starts(
        lengths_ref, order_ref, lambda first, start: jnp.where(start <= query_base, start, first), jnp.int32(0)
    )


def part_of(ref, g, width):
    return ref[:, pl.ds(pl.multiple_of(g * width, width), width)]


def attend_block(sizes, qt_of, kv_ref, bias, state, u, fresh):
    kv_heads, group_size, _ = sizes
    acc_ref, max_ref, sum_ref = state
    bias = jnp.concatenate([bias] * group_size, axis=1)

    def per_head(g, _):
        s = jnp.dot(part_of(kv_ref, g, HD), qt_of(g), preferred_element_type=jnp.float32)
        s = s * SCALE + bias
        top = jnp.max(s, axis=0, keepdims=True)
        if not fresh:
            old = max_ref[u, g]
            top = jnp.maximum(old, top)
            fade = jnp.exp2(old - top)
        p = jnp.exp2(s - top)
        total = jnp.sum(p, axis=0, keepdims=True)
        mixed = jnp.dot(part_of(kv_ref, kv_heads + g, HD), p.astype(jnp.bfloat16), preferred_element_type=jnp.float32)
        max_ref[u, g] = top
        sum_ref[u, g] = total if fresh else sum_ref[u, g] * fade + total
        acc_ref[u, g] = mixed if fresh else acc_ref[u, g] * fade + mixed
        return _

    lax.fori_loop(0, kv_heads, per_head, 0, unroll=UNROLL)


def pack_kv_kernel(k_ref, v_ref, kv_ref):
    width = k_ref.shape[1]
    kv_ref[:, :width] = k_ref[...]
    for g in range(width // HD):
        kv_ref[:, width + g * HD : width + (g + 1) * HD] = v_ref[:, g * HD : (g + 1) * HD].T


def own_kernel(sizes, mated, lengths_ref, order_ref, *refs):
    kv_heads, group_size, rows = sizes
    q_ref, kv_ref, qt_ref, *state = refs[1:] if mated else refs
    for h in range(kv_heads * group_size):
        qt_ref[:, h * HD : (h + 1) * HD] = q_ref[:, h * HD : (h + 1) * HD].T
    base = position(AXES) * rows
    bias = mask_bias(lengths_ref, order_ref, base, base, rows)
    attend_block(sizes, lambda g: part_of(qt_ref, g, group_size * HD), kv_ref, bias, state, OWN, True)


def block_of(table_ref, slot):
    device = position(AXES)
    if table_ref is None:
        block = device - 1 - slot
        return device, device, jnp.maximum(block, 0), jnp.where(block < 0, NONE, OWN)
    return device, table_ref[device, 0], table_ref[device, 1 + 2 * slot], table_ref[device, 2 + 2 * slot]


def back_kernel(sizes, slot, lengths_ref, order_ref, table_ref, qm_ref, kv_ref, *refs):
    kv_heads, group_size, rows = sizes
    state = refs[3:]
    _, mate, block, use = block_of(table_ref, slot)
    query_base, key_base = mate * rows, block * rows
    live = (use == MATE) & (key_base + rows > first_seen(lengths_ref, order_ref, query_base))

    @pl.when(live)
    def _():
        bias = mask_bias(lengths_ref, order_ref, query_base, key_base, rows)
        attend_block(sizes, lambda g: part_of(qm_ref, g, group_size * HD), kv_ref, bias, state, MATE, True)

    @pl.when(jnp.logical_not(live))
    def _():
        for g in range(kv_heads):
            for ref, value in zip(state, (0.0, NEG, 0.0)):
                ref[MATE, g] = jnp.full(ref.shape[2:], value, jnp.float32)


def add_block(sizes, slot, table_ref, lengths_ref, order_ref, q_ref, qm_ref, kv_ref, state):
    kv_heads, group_size, rows = sizes
    device, mate, block, use = block_of(table_ref, slot)
    mine = use == OWN
    query_base = jnp.where(mine, device, mate) * rows
    key_base = block * rows
    live = (use != NONE) & (key_base + rows > first_seen(lengths_ref, order_ref, query_base))

    @pl.when(live)
    def _():
        bias = mask_bias(lengths_ref, order_ref, query_base, key_base, rows)

        def qt_of(g):
            a = part_of(q_ref, g, group_size * HD)
            return a if qm_ref is None else jnp.where(mine, a, part_of(qm_ref, g, group_size * HD))

        attend_block(sizes, qt_of, kv_ref, bias, state, use, False)


def add_kernel(sizes, slot, mated, lengths_ref, order_ref, *refs):
    table_ref, refs = (refs[0], refs[1:]) if mated else (None, refs)
    q_ref, refs = refs[0], refs[1:]
    qm_ref, refs = (refs[0], refs[1:]) if mated else (None, refs)
    add_block(sizes, slot, table_ref, lengths_ref, order_ref, q_ref, qm_ref, refs[0], refs[4:])


def split3(x):
    a = x.astype(jnp.bfloat16)
    rest = x - a.astype(jnp.float32)
    b = rest.astype(jnp.bfloat16)
    return a, b, (rest - b.astype(jnp.float32)).astype(jnp.bfloat16)


def part_kernel(sizes, slot, lengths_ref, order_ref, table_ref, q_ref, qm_ref, kv_ref, a_in, m_in, s_in, part_ref, *state):
    kv_heads, group_size, rows = sizes
    add_block(sizes, slot, table_ref, lengths_ref, order_ref, q_ref, qm_ref, kv_ref, state)
    acc_ref, max_ref, sum_ref = state
    width = group_size * HD
    heads = kv_heads * group_size
    tops, sums = [], []
    for g in range(kv_heads):
        top, total = max_ref[MATE, g], sum_ref[MATE, g]
        share = 1.0 / jnp.where(total > 0, total, 1.0)
        part_ref[:, g * width : (g + 1) * width] = (acc_ref[MATE, g] * share).astype(jnp.bfloat16)
        for j in range(group_size):
            tops.append(top[:, j * HD : (j + 1) * HD])
            sums.append(total[:, j * HD : (j + 1) * HD])
    for column, stats in enumerate((tops, sums)):
        place = (heads + column) * HD
        for k, piece in enumerate(split3(jnp.concatenate(stats, axis=0))):
            part_ref[k * heads : (k + 1) * heads, place : place + HD] = piece


def last_kernel(sizes, slot, mated, lengths_ref, order_ref, *refs):
    table_ref, refs = (refs[0], refs[1:]) if mated else (None, refs)
    q_ref, refs = refs[0], refs[1:]
    kv_heads, group_size, rows = sizes
    heads = kv_heads * group_size
    part_ref, refs = (refs[0], refs[1:]) if mated else (None, refs)
    out_ref, state = refs[4], refs[5:]
    add_block(sizes, slot, table_ref, lengths_ref, order_ref, q_ref, None, refs[0], state)
    acc_ref, max_ref, sum_ref = state
    width = group_size * HD
    if mated:
        tops, sums = (
            sum(part_ref[k * heads : (k + 1) * heads, c * HD : (c + 1) * HD].astype(jnp.float32) for k in range(3))
            for c in (heads, heads + 1)
        )
        device = position(AXES)
        met = table_ref[device, 0] != device
        tops, sums = jnp.where(met, tops, NEG), jnp.where(met, sums, 0.0)
    for g in range(kv_heads):
        for j in range(group_size):
            h, mine = g * group_size + j, slice(j * HD, (j + 1) * HD)
            numer, top, total = acc_ref[OWN, g, :, mine], max_ref[OWN, g, :, mine], sum_ref[OWN, g, :, mine]
            if mated:
                both = jnp.maximum(top, tops[h : h + 1])
                weight, other = jnp.exp2(top - both), jnp.exp2(tops[h : h + 1] - both) * sums[h : h + 1]
                share = 1.0 / (total * weight + other)
                theirs = jnp.where(met, part_ref[:, h * HD : (h + 1) * HD].astype(jnp.float32), 0.0)
                out = numer * (weight * share) + theirs * (other * share)
            else:
                out = numer * (1.0 / total)
            out_ref[:, h * HD : (h + 1) * HD] = out.astype(jnp.bfloat16).T


def calls(sizes, scalars, mated):
    kv_heads, group_size, rows = sizes
    tall = group_size * rows
    sets = 2 if mated else 1
    state = [
        pltpu.VMEM((sets, kv_heads, HD, tall), jnp.float32),
        pltpu.VMEM((sets, kv_heads, 1, tall), jnp.float32),
        pltpu.VMEM((sets, kv_heads, 1, tall), jnp.float32),
    ]
    smem, vmem = pl.BlockSpec(memory_space=pltpu.SMEM), pl.BlockSpec(memory_space=pltpu.VMEM)
    held = []

    def call(kernel, arrays, out, name, keeps=True):
        n_in = len(scalars) + len(arrays)
        out = out + (state if keeps else [])
        result = pl.pallas_call(
            kernel,
            out_shape=out,
            in_specs=[smem] * len(scalars) + [vmem] * (len(arrays) + len(held)),
            out_specs=[vmem] * len(out),
            input_output_aliases={n_in + k: len(out) - 3 + k for k in range(len(held))},
            compiler_params=pltpu.CompilerParams(vmem_limit_bytes=VMEM_LIMIT),
            cost_estimate=pl.CostEstimate(flops=FLOPS, bytes_accessed=1 << 20, transcendentals=0),
            name=name,
        )(*scalars, *arrays, *held)
        held[:] = result[-3:]
        return result[:-3]

    def own(q, kv):
        qt = jax.ShapeDtypeStruct(q.shape, q.dtype)
        return call(functools.partial(own_kernel, sizes, mated), [q, kv], [qt], "own_block")[0]

    def back(slot, qm, kv):
        call(functools.partial(back_kernel, sizes, slot), [qm, kv], [], "mate_first_block")

    def add(slot, q, qm, kv):
        qs = [q] if qm is None else [q, qm]
        call(functools.partial(add_kernel, sizes, slot, qm is not None), qs + [kv], [], "add_block")

    def part(slot, q, qm, kv):
        out = jax.ShapeDtypeStruct((rows, (kv_heads * group_size + 2) * HD), jnp.bfloat16)
        return call(functools.partial(part_kernel, sizes, slot), [q, qm, kv], [out], "mate_part")[0]

    def last(slot, q, parts, kv):
        out = jax.ShapeDtypeStruct((rows, kv_heads * group_size * HD), jnp.bfloat16)
        return call(functools.partial(last_kernel, sizes, slot, mated), [q, *parts, kv], [out], "last_block")[0]

    return own, back, add, part, last


def pack_kv(keys, values):
    rows, width = keys.shape
    return pl.pallas_call(
        pack_kv_kernel, out_shape=jax.ShapeDtypeStruct((rows, 2 * width), keys.dtype), name="pack_keys_values"
    )(keys, values)


def ring_shards(groups, queries, keys, values, lengths, pack_order):
    rows, kv_heads = queries.shape[0], keys.shape[1] // HD
    m = len(RING)
    sizes = (kv_heads, queries.shape[1] // keys.shape[1], rows)
    route, user = make_plan(groups, FIRST // rows)
    mate_of = [d if d < 2 * m else d ^ m for d in range(groups * m)]
    table = jnp.array([[mate] + row for mate, row in zip(mate_of, block_table(route, user, groups))], jnp.int32)
    own, back, add, part, last = calls(sizes, (lengths, pack_order, table), True)

    def send(block, op, step):
        return lax.ppermute(block, AXES, sorted((e, d) for d, (e, _) in route[op, step].items()))

    mates = [(d, d ^ m) for d in range(2 * m, groups * m)]
    eight_back = [(m + i, 3 * m + i) for i in range(m)] + [(2 * m + i, 2 * m + i) for i in range(m)]
    kv = pack_kv(keys, values)
    a1 = send(kv, "A", 1)
    q = own(queries, kv)
    b1 = send(kv, "B", 1)
    qm = lax.ppermute(q, AXES, mates)
    kv8 = lax.ppermute(kv, AXES, eight_back)
    a2 = send(a1, "A", 2)
    back(7, qm, kv8)
    add(0, q, qm, a1)
    b2 = send(b1, "B", 2)
    add(1, q, qm, b1)
    a3 = send(a2, "A", 3)
    add(2, q, qm, a2)
    b3 = send(b2, "B", 3)
    add(3, q, qm, b2)
    a4 = send(a3, "A", 4)
    add(4, q, qm, a3)
    mine = part(5, q, qm, b3)
    theirs = lax.ppermute(mine, AXES, mates)
    return last(6, q, [theirs], a4)


def chain_shards(queries, keys, values, lengths, pack_order):
    rows, kv_heads = queries.shape[0], keys.shape[1] // HD
    sizes = (kv_heads, queries.shape[1] // keys.shape[1], rows)
    n = lax.axis_size(AXES)
    own, back, add, part, last = calls(sizes, (lengths, pack_order), False)
    kv = pack_kv(keys, values)
    q = own(queries, kv)
    for hop in range(HOPS):
        kv = lax.ppermute(kv, AXES, [(d, d + 1) for d in range(n - 1)])
        if hop < HOPS - 1:
            add(hop, q, None, kv)
    return last(HOPS - 1, q, [], kv)


def solution(mesh):
    spec, whole = P(AXES, None), P()
    outer, inner = mesh.shape["outer"], mesh.shape["inner"]
    ring = outer == 4 and inner == len(RING) == HOPS
    shards = functools.partial(ring_shards, outer) if ring else chain_shards
    return jax.shard_map(
        shards, mesh=mesh, in_specs=(spec, spec, spec, whole, whole), out_specs=spec, check_vma=False
    )
```

time: 178 us -> 76.8 us (0.43)
  the two profiles are of different devices: /device:TPU:2 before, /device:TPU:28 now
where the time goes in v1:
time: 76.8 us; the launch traced here: 75.8 us
  Pallas kernels  30.7 us (40%)
  waiting for transfers between devices  22.3 us (29%)
  starting transfers between devices  18.3 us (24%)
  local copies, waits for them, and re-layouts  4.31 us (6%)
    pallas_call x9, Pallas kernels, call(): pl.pallas_call(kernel, out_shape=out, in_specs=[smem] * len(scalars) + [v...  28.7 us
    ppermute x7, waiting for transfers between devices, send(): lax.ppermute(block, AXES, sorted(((e, d) for d, (e, _) in route[op, step]...  22.3 us
    ppermute x7, starting transfers between devices, send(): lax.ppermute(block, AXES, sorted(((e, d) for d, (e, _) in route[op, step]...  16.2 us
    unnamed x16, local copies, waits for them, and re-layouts  4.31 us
    pallas_call x1, Pallas kernels, pack_kv(): pl.pallas_call(pack_kv_kernel, out_shape=jax.ShapeDtypeStruct((rows, 2 *...  1.94 us
  transfers between devices with their start and end apart: 10, of which 3 were waited for; matrix products, arithmetic and copies ran while one was open for 0% of the time, Pallas kernels for 27%

profile of v1, /device:TPU:28, one launch (start us, length us, event | category | flops | bytes accessed | tf_op | source)
XLA Modules:
  0.0 75.8 jit_solution(10587146619384285346)
XLA Ops:
  0.0 1.9 %pack_keys_values.1.refs_2_ = bf16[128,2048]{1,0:T(8,128)(2,1)} custom-call(bf16[128,1024]{1,0:T(8,128)(2,1)} %k_ref.1, bf16[128,1024]{1,0:T(8,128)(2,1)} %v_ref.1), custom_call_target="tpu_custom_call" | custom-call | tf_op jit(solution)/shard_map/pack_keys_values/pallas_call | solution.py:324
  1.9 1.3 %collective-permute-start.4 = (bf16[128,2048]{1,0:T(8,128)(2,1)}, bf16[128,2048]{1,0:T(8,128)(2,1)S(1)}, u32[]{:S(2)}, u32[]{:S(2)}) collective-permute-start(bf16[128,2048]{1,0:T(8,128)(2,1)} %pack_keys_values.1.refs_2_), channel_id=1, source_target_pairs={{0,2},{1,0},{2,4},{3,1},{4,6},{6,7},{8,9},{9,11},{10,24},{11,13},{... | collective-permute-start | bytes 1572872 | tf_op jit(solution)/shard_map/ppermute | solution.py:339
  3.2 1.3 %collective-permute-start.1 = (bf16[128,2048]{1,0:T(8,128)(2,1)}, bf16[128,2048]{1,0:T(8,128)(2,1)S(1)}, u32[]{:S(2)}, u32[]{:S(2)}) collective-permute-start(bf16[128,2048]{1,0:T(8,128)(2,1)} %pack_keys_values.1.refs_2_), channel_id=1, source_target_pairs={{0,1},{1,3},{2,0},{3,5},{5,7},{8,10},{9,24},{10,12},{11,25},{12,14... | collective-permute-start | bytes 1572872 | tf_op jit(solution)/shard_map/ppermute | solution.py:339
  4.5 1.0 %copy-done = bf16[128,2048]{1,0:T(8,128)(2,1)S(1)} copy-done((bf16[128,2048]{1,0:T(8,128)(2,1)S(1)}, bf16[128,2048]{1,0:T(8,128)(2,1)}, u32[]{:S(2)}) %copy-start) | copy-done | bytes 524312
  5.6 1.2 %copy-done.1 = bf16[128,4096]{1,0:T(8,128)(2,1)S(1)} copy-done((bf16[128,4096]{1,0:T(8,128)(2,1)S(1)}, bf16[128,4096]{1,0:T(8,128)(2,1)}, u32[]{:S(2)}) %copy-start.1) | copy-done | bytes 1048600
  8.8 3.4 %own_block.1 = (bf16[128,4096]{1,0:T(8,128)(2,1)S(1)}, f32[2,8,128,512]{3,2,1,0:T(8,128)S(1)}, f32[2,8,1,512]{3,2,1,0:T(1,128)S(1)}, f32[2,8,1,512]{3,2,1,0:T(1,128)S(1)}) custom-call(s32[8]{0:T(128)S(1)} %copy-done.2, s32[8]{0:T(128)S(1)} %copy-done.4, s32[32,17]{1,0:T(8,128)S(1)} %copy-done.6, bf16[128,4096]{1,0:T(8,128)(2,1)S(1)} %copy-done.1, ...), custom_call_target="tpu_custom_call" | custom-call | flops 2000000000 | bytes 1048576 | tf_op jit(solution)/shard_map/own_block/pallas_call | solution.py:287
  12.3 0.7 collective-permute-start
  13.0 3.8 %collective-permute-done.4.refs_3_ = bf16[128,2048]{1,0:T(8,128)(2,1)S(1)} collective-permute-done((bf16[128,2048]{1,0:T(8,128)(2,1)}, bf16[128,2048]{1,0:T(8,128)(2,1)S(1)}, u32[]{:S(2)}, u32[]{:S(2)}) %collective-permute-start.4) | collective-permute-done | bytes 524320 | tf_op jit(solution)/shard_map/ppermute | solution.py:339
  16.8 1.3 %collective-permute-start.5 = (bf16[128,2048]{1,0:T(8,128)(2,1)S(1)}, bf16[128,2048]{1,0:T(8,128)(2,1)S(1)}, u32[]{:S(2)}, u32[]{:S(2)}) collective-permute-start(bf16[128,2048]{1,0:T(8,128)(2,1)S(1)} %collective-permute-done.4.refs_3_), channel_id=1, source_target_pairs={{0,2},{1,0},{2,4},{4,6},{6,7},{8,9},{9,11},{11,13},{13,15},{15,14}... | collective-permute-start | bytes 1572872 | tf_op jit(solution)/shard_map/ppermute | solution.py:339
  18.1 4.6 %collective-permute-start.2 = (bf16[128,2048]{1,0:T(8,128)(2,1)S(1)}, bf16[128,2048]{1,0:T(8,128)(2,1)S(1)}, u32[]{:S(2)}, u32[]{:S(2)}) collective-permute-start(bf16[128,2048]{1,0:T(8,128)(2,1)S(1)} %collective-permute-done.1.refs_3_), channel_id=1, source_target_pairs={{0,1},{1,3},{3,5},{5,7},{7,6},{8,26},{10,12},{12,14},{14,15},{15,2... | collective-permute-start | bytes 1572872 | tf_op jit(solution)/shard_map/ppermute | solution.py:339
  23.4 9.3 %collective-permute-done.5.refs_3_ = bf16[128,2048]{1,0:T(8,128)(2,1)S(1)} collective-permute-done((bf16[128,2048]{1,0:T(8,128)(2,1)S(1)}, bf16[128,2048]{1,0:T(8,128)(2,1)S(1)}, u32[]{:S(2)}, u32[]{:S(2)}) %collective-permute-start.5) | collective-permute-done | bytes 524320 | tf_op jit(solution)/shard_map/ppermute | solution.py:339
  32.7 1.9 %collective-permute-start.6 = (bf16[128,2048]{1,0:T(8,128)(2,1)S(1)}, bf16[128,2048]{1,0:T(8,128)(2,1)S(1)}, u32[]{:S(2)}, u32[]{:S(2)}) collective-permute-start(bf16[128,2048]{1,0:T(8,128)(2,1)S(1)} %collective-permute-done.5.refs_3_), channel_id=1, source_target_pairs={{0,2},{2,4},{4,6},{6,7},{7,5},{9,27},{11,13},{13,15},{14,28},{15,1... | collective-permute-start | bytes 1572872 | tf_op jit(solution)/shard_map/ppermute | solution.py:339
  34.6 3.9 %collective-permute-start.3 = (bf16[128,2048]{1,0:T(8,128)(2,1)S(1)}, bf16[128,2048]{1,0:T(8,128)(2,1)S(1)}, u32[]{:S(2)}, u32[]{:S(2)}) collective-permute-start(bf16[128,2048]{1,0:T(8,128)(2,1)S(1)} %collective-permute-done.2.refs_3_), channel_id=1, source_target_pairs={{1,3},{3,5},{5,7},{7,6},{10,12},{12,14},{14,15},{15,13},{16,17},{1... | collective-permute-start | bytes 1572872 | tf_op jit(solution)/shard_map/ppermute | solution.py:339
  38.5 1.0 %mate_first_block.1 = (f32[2,8,128,512]{3,2,1,0:T(8,128)S(1)}, f32[2,8,1,512]{3,2,1,0:T(1,128)S(1)}, f32[2,8,1,512]{3,2,1,0:T(1,128)S(1)}) custom-call(s32[8]{0:T(128)S(1)} %copy-done.2, s32[8]{0:T(128)S(1)} %copy-done.4, s32[32,17]{1,0:T(8,128)S(1)} %copy-done.6, ...), custom_call_target="tpu_custom_call", output_to_operand_aliasing={{0}: (5, {}), {1}: (6, {}), {2}: (7, {})} | custom-call | flops 2000000000 | bytes 1048576 | tf_op jit(solution)/shard_map/mate_first_block/pallas_call | solution.py:287
  39.5 3.2 %add_block.5 = (f32[2,8,128,512]{3,2,1,0:T(8,128)S(1)}, f32[2,8,1,512]{3,2,1,0:T(1,128)S(1)}, f32[2,8,1,512]{3,2,1,0:T(1,128)S(1)}) custom-call(s32[8]{0:T(128)S(1)} %copy-done.2, s32[8]{0:T(128)S(1)} %copy-done.4, s32[32,17]{1,0:T(8,128)S(1)} %copy-done.6, ...), custom_call_target="tpu_custom_call", output_to_operand_aliasing={{0}: (6, {}), {1}: (7, {}), {2}: (8, {})} | custom-call | flops 2000000000 | bytes 1048576 | tf_op jit(solution)/shard_map/add_block/pallas_call | solution.py:287
  42.8 3.2 %add_block.6 = (f32[2,8,128,512]{3,2,1,0:T(8,128)S(1)}, f32[2,8,1,512]{3,2,1,0:T(1,128)S(1)}, f32[2,8,1,512]{3,2,1,0:T(1,128)S(1)}) custom-call(s32[8]{0:T(128)S(1)} %copy-done.2, s32[8]{0:T(128)S(1)} %copy-done.4, s32[32,17]{1,0:T(8,128)S(1)} %copy-done.6, ...), custom_call_target="tpu_custom_call", output_to_operand_aliasing={{0}: (6, {}), {1}: (7, {}), {2}: (8, {})} | custom-call | flops 2000000000 | bytes 1048576 | tf_op jit(solution)/shard_map/add_block/pallas_call | solution.py:287
  46.0 3.2 %add_block.7 = (f32[2,8,128,512]{3,2,1,0:T(8,128)S(1)}, f32[2,8,1,512]{3,2,1,0:T(1,128)S(1)}, f32[2,8,1,512]{3,2,1,0:T(1,128)S(1)}) custom-call(s32[8]{0:T(128)S(1)} %copy-done.2, s32[8]{0:T(128)S(1)} %copy-done.4, s32[32,17]{1,0:T(8,128)S(1)} %copy-done.6, ...), custom_call_target="tpu_custom_call", output_to_operand_aliasing={{0}: (6, {}), {1}: (7, {}), {2}: (8, {})} | custom-call | flops 2000000000 | bytes 1048576 | tf_op jit(solution)/shard_map/add_block/pallas_call | solution.py:287
  49.2 3.2 %add_block.8 = (f32[2,8,128,512]{3,2,1,0:T(8,128)S(1)}, f32[2,8,1,512]{3,2,1,0:T(1,128)S(1)}, f32[2,8,1,512]{3,2,1,0:T(1,128)S(1)}) custom-call(s32[8]{0:T(128)S(1)} %copy-done.2, s32[8]{0:T(128)S(1)} %copy-done.4, s32[32,17]{1,0:T(8,128)S(1)} %copy-done.6, ...), custom_call_target="tpu_custom_call", output_to_operand_aliasing={{0}: (6, {}), {1}: (7, {}), {2}: (8, {})} | custom-call | flops 2000000000 | bytes 1048576 | tf_op jit(solution)/shard_map/add_block/pallas_call | solution.py:287
  52.5 3.2 %add_block.9 = (f32[2,8,128,512]{3,2,1,0:T(8,128)S(1)}, f32[2,8,1,512]{3,2,1,0:T(1,128)S(1)}, f32[2,8,1,512]{3,2,1,0:T(1,128)S(1)}) custom-call(s32[8]{0:T(128)S(1)} %copy-done.2, s32[8]{0:T(128)S(1)} %copy-done.4, s32[32,17]{1,0:T(8,128)S(1)} %copy-done.6, ...), custom_call_target="tpu_custom_call", output_to_operand_aliasing={{0}: (6, {}), {1}: (7, {}), {2}: (8, {})} | custom-call | flops 2000000000 | bytes 1048576 | tf_op jit(solution)/shard_map/add_block/pallas_call | solution.py:287
  55.8 3.4 %mate_part.1 = (bf16[128,4352]{1,0:T(8,128)(2,1)S(1)}, f32[2,8,128,512]{3,2,1,0:T(8,128)S(1)}, f32[2,8,1,512]{3,2,1,0:T(1,128)S(1)}, f32[2,8,1,512]{3,2,1,0:T(1,128)S(1)}) custom-call(s32[8]{0:T(128)S(1)} %copy-done.2, s32[8]{0:T(128)S(1)} %copy-done.4, s32[32,17]{1,0:T(8,128)S(1)} %copy-done.6, ...), custom_call_target="tpu_custom_call", output_to_operand_aliasing={{1}: (6, {}), {2}: (7, {}), {3}: (8, {})} | custom-call | flops 2000000000 | bytes 1048576 | tf_op jit(solution)/shard_map/mate_part/pallas_call | solution.py:287
  59.2 0.7 collective-permute-start.8
  59.9 1.9 %collective-permute-start.9 = (bf16[128,2048]{1,0:T(8,128)(2,1)S(1)}, bf16[128,2048]{1,0:T(8,128)(2,1)S(1)}, u32[]{:S(2)}, u32[]{:S(2)}) collective-permute-start(bf16[128,2048]{1,0:T(8,128)(2,1)S(1)} %collective-permute-done.6.refs_3_), channel_id=1, source_target_pairs={{2,4},{4,6},{6,7},{7,5},{11,13},{13,15},{14,12},{15,14},{16,26},{1... | collective-permute-start | bytes 1572872 | tf_op jit(solution)/shard_map/ppermute | solution.py:339
  61.8 9.1 %collective-permute-done.9.refs_3_ = bf16[128,2048]{1,0:T(8,128)(2,1)S(1)} collective-permute-done((bf16[128,2048]{1,0:T(8,128)(2,1)S(1)}, bf16[128,2048]{1,0:T(8,128)(2,1)S(1)}, u32[]{:S(2)}, u32[]{:S(2)}) %collective-permute-start.9) | collective-permute-done | bytes 524320 | tf_op jit(solution)/shard_map/ppermute | solution.py:339
  71.0 4.8 %last_block.1 = (bf16[128,4096]{1,0:T(8,128)(2,1)}, f32[2,8,128,512]{3,2,1,0:T(8,128)S(1)}, f32[2,8,1,512]{3,2,1,0:T(1,128)S(1)}, f32[2,8,1,512]{3,2,1,0:T(1,128)S(1)}) custom-call(s32[8]{0:T(128)S(1)} %copy-done.3, s32[8]{0:T(128)S(1)} %copy-done.5, s32[32,17]{1,0:T(8,128)S(1)} %copy-done.7, ...), custom_call_target="tpu_custom_call", output_to_operand_aliasing={{1}: (6, {}), {2}: (7, {}), {3}: (8, {})} | custom-call | flops 2000000000 | bytes 1048576 | tf_op jit(solution)/shard_map/last_block/pallas_call | solution.py:287
  (22 shorter events, 2.8 us)
Async XLA Ops:
  1.9 14.9 %collective-permute-start.4 = (bf16[128,2048]{1,0:T(8,128)(2,1)}, bf16[128,2048]{1,0:T(8,128)(2,1)S(1)}, u32[]{:S(2)}, u32[]{:S(2)}) collective-permute-start(bf16[128,2048]{1,0:T(8,128)(2,1)} %pack_keys_values.1.refs_2_), channel_id=1, source_target_pairs={{0,2},{1,0},{2,4},{3,1},{4,6},{6,7},{8,9},{9,11},{10,24},{11,13},{... | collective-permute-start | bytes 1572872 | tf_op jit(solution)/shard_map/ppermute | solution.py:339
  3.2 14.9 %collective-permute-start.1 = (bf16[128,2048]{1,0:T(8,128)(2,1)}, bf16[128,2048]{1,0:T(8,128)(2,1)S(1)}, u32[]{:S(2)}, u32[]{:S(2)}) collective-permute-start(bf16[128,2048]{1,0:T(8,128)(2,1)} %pack_keys_values.1.refs_2_), channel_id=1, source_target_pairs={{0,1},{1,3},{2,0},{3,5},{5,7},{8,10},{9,24},{10,12},{11,25},{12,14... | collective-permute-start | bytes 1572872 | tf_op jit(solution)/shard_map/ppermute | solution.py:339
  4.5 1.0 %copy-start = (bf16[128,2048]{1,0:T(8,128)(2,1)S(1)}, bf16[128,2048]{1,0:T(8,128)(2,1)}, u32[]{:S(2)}) copy-start(bf16[128,2048]{1,0:T(8,128)(2,1)} %pack_keys_values.1.refs_2_) | copy-start | bytes 1572868
  5.6 1.2 %copy-start.1 = (bf16[128,4096]{1,0:T(8,128)(2,1)S(1)}, bf16[128,4096]{1,0:T(8,128)(2,1)}, u32[]{:S(2)}) copy-start(bf16[128,4096]{1,0:T(8,128)(2,1)} %refs_1_.1) | copy-start | bytes 3145732
  6.8 0.7 copy-start.2
  7.5 0.7 copy-start.4
  8.1 0.7 copy-start.6
  12.3 26.3 %collective-permute-start = (bf16[128,4096]{1,0:T(8,128)(2,1)S(1)}, bf16[128,4096]{1,0:T(8,128)(2,1)S(1)}, u32[]{:S(2)}, u32[]{:S(2)}) collective-permute-start(bf16[128,4096]{1,0:T(8,128)(2,1)S(1)} %get-tuple-element.32.refs_1_.q_ref), channel_id=1, source_target_pairs={{16,24},{17,25},{18,26},{19,27},{20,28},{21,29},{22,30},{23,31},{2... | collective-permute-start | bytes 3145736 | tf_op jit(solution)/shard_map/ppermute | solution.py:347
  16.8 15.8 %collective-permute-start.5 = (bf16[128,2048]{1,0:T(8,128)(2,1)S(1)}, bf16[128,2048]{1,0:T(8,128)(2,1)S(1)}, u32[]{:S(2)}, u32[]{:S(2)}) collective-permute-start(bf16[128,2048]{1,0:T(8,128)(2,1)S(1)} %collective-permute-done.4.refs_3_), channel_id=1, source_target_pairs={{0,2},{1,0},{2,4},{4,6},{6,7},{8,9},{9,11},{11,13},{13,15},{15,14}... | collective-permute-start | bytes 1572872 | tf_op jit(solution)/shard_map/ppermute | solution.py:339
  18.1 16.5 %collective-permute-start.2 = (bf16[128,2048]{1,0:T(8,128)(2,1)S(1)}, bf16[128,2048]{1,0:T(8,128)(2,1)S(1)}, u32[]{:S(2)}, u32[]{:S(2)}) collective-permute-start(bf16[128,2048]{1,0:T(8,128)(2,1)S(1)} %collective-permute-done.1.refs_3_), channel_id=1, source_target_pairs={{0,1},{1,3},{3,5},{5,7},{7,6},{8,26},{10,12},{12,14},{14,15},{15,2... | collective-permute-start | bytes 1572872 | tf_op jit(solution)/shard_map/ppermute | solution.py:339
  22.7 15.8 %collective-permute-start.7 = (bf16[128,2048]{1,0:T(8,128)(2,1)S(1)}, bf16[128,2048]{1,0:T(8,128)(2,1)S(1)}, u32[]{:S(2)}, u32[]{:S(2)}) collective-permute-start(bf16[128,2048]{1,0:T(8,128)(2,1)S(1)} %copy-done), channel_id=1, source_target_pairs={{8,24},{9,25},{10,26},{11,27},{12,28},{13,29},{14,30},{15,31},{16,... | collective-permute-start | bytes 1572872 | tf_op jit(solution)/shard_map/ppermute | solution.py:348
  32.7 19.8 %collective-permute-start.6 = (bf16[128,2048]{1,0:T(8,128)(2,1)S(1)}, bf16[128,2048]{1,0:T(8,128)(2,1)S(1)}, u32[]{:S(2)}, u32[]{:S(2)}) collective-permute-start(bf16[128,2048]{1,0:T(8,128)(2,1)S(1)} %collective-permute-done.5.refs_3_), channel_id=1, source_target_pairs={{0,2},{2,4},{4,6},{6,7},{7,5},{9,27},{11,13},{13,15},{14,28},{15,1... | collective-permute-start | bytes 1572872 | tf_op jit(solution)/shard_map/ppermute | solution.py:339
  34.6 21.2 %collective-permute-start.3 = (bf16[128,2048]{1,0:T(8,128)(2,1)S(1)}, bf16[128,2048]{1,0:T(8,128)(2,1)S(1)}, u32[]{:S(2)}, u32[]{:S(2)}) collective-permute-start(bf16[128,2048]{1,0:T(8,128)(2,1)S(1)} %collective-permute-done.2.refs_3_), channel_id=1, source_target_pairs={{1,3},{3,5},{5,7},{7,6},{10,12},{12,14},{14,15},{15,13},{16,17},{1... | collective-permute-start | bytes 1572872 | tf_op jit(solution)/shard_map/ppermute | solution.py:339
  55.7 15.3 %copy-start.3 = (s32[8]{0:T(128)S(1)}, s32[8]{0:T(128)}, u32[]{:S(2)}) copy-start(s32[8]{0:T(128)} %lengths_ref.17) | copy-start | bytes 100
  55.7 15.2 %copy-start.5 = (s32[8]{0:T(128)S(1)}, s32[8]{0:T(128)}, u32[]{:S(2)}) copy-start(s32[8]{0:T(128)} %order_ref.17) | copy-start | bytes 100
  55.7 15.2 %copy-start.7 = (s32[32,17]{1,0:T(8,128)S(1)}, s32[32,17]{1,0:T(8,128)}, u32[]{:S(2)}) copy-start(s32[32,17]{1,0:T(8,128)} %constant.2.clone.refs_0_.table_ref) | copy-start | bytes 6532
  59.2 11.8 %collective-permute-start.8 = (bf16[128,4352]{1,0:T(8,128)(2,1)S(1)}, bf16[128,4352]{1,0:T(8,128)(2,1)S(1)}, u32[]{:S(2)}, u32[]{:S(2)}) collective-permute-start(bf16[128,4352]{1,0:T(8,128)(2,1)S(1)} %get-tuple-element.54), channel_id=1, source_target_pairs={{16,24},{17,25},{18,26},{19,27},{20,28},{21,29},{22,30},{23,31},{2... | collective-permute-start | bytes 3342344 | tf_op jit(solution)/shard_map/ppermute | solution.py:361
  59.9 11.1 %collective-permute-start.9 = (bf16[128,2048]{1,0:T(8,128)(2,1)S(1)}, bf16[128,2048]{1,0:T(8,128)(2,1)S(1)}, u32[]{:S(2)}, u32[]{:S(2)}) collective-permute-start(bf16[128,2048]{1,0:T(8,128)(2,1)S(1)} %collective-permute-done.6.refs_3_), channel_id=1, source_target_pairs={{2,4},{4,6},{6,7},{7,5},{11,13},{13,15},{14,12},{15,14},{16,26},{1... | collective-permute-start | bytes 1572872 | tf_op jit(solution)/shard_map/ppermute | solution.py:339

commit v2 on v1

v2 whole, which is shorter than its diff:
```python
import functools
import math

import jax
import jax.numpy as jnp
from jax import lax
from jax.experimental import pallas as pl
from jax.experimental.pallas import tpu as pltpu
from jax.sharding import PartitionSpec as P

HD = 128
HOPS = 8
FIRST = 1024
AXES = ("outer", "inner")
NEG = -1e30
SCALE = math.log2(math.e) / math.sqrt(HD)
RING = (0, 2, 4, 6, 7, 5, 3, 1)
OWN, MATE, NONE = 0, 1, 2
VMEM_LIMIT = 40 * 1024 * 1024
SLOTS = 8
STARTS = 2 + 2 * SLOTS
INFO_SPACE = pltpu.SMEM
FLOPS = 800_000_000
LAST_FLOPS = 50_000_000_000


def make_plan(groups, first_blocks):
    m = len(RING)
    n = groups * m
    place = {j: p for p, j in enumerate(RING)}

    def held(d, j):
        o, i = divmod(d, m)
        if j == i:
            return d
        if o % 2 == 0 or j < i:
            return o * m + j
        return ((o + 2) % groups) * m + j

    def uses(q, b):
        return 0 < q - b <= HOPS and not (b < first_blocks <= q)

    def user(d, b):
        return d if uses(d, b) else d ^ m if uses(d ^ m, b) else None

    ops = [("A", 1), ("B", 1), ("A", 2), ("B", 2), ("A", 3), ("B", 3), ("A", 4)]
    route = {}
    for op, s in ops:
        route[op, s] = {}
        for d in range(n):
            o, i = divmod(d, m)
            way = 1 if (o % 2 == 0) == (op == "A") else -1
            j = RING[(place[i] - way * s) % m]
            b = held(d, j)
            behind = RING[(place[i] - way) % m]
            (source,) = [e for e in range(behind, n, m) if (e // m) % 2 == o % 2 and held(e, j) == b]
            route[op, s][d] = (source, b)
    for op, s in reversed(ops):
        sends_on = {e for e, _ in route.get((op, s + 1), {}).values()}
        route[op, s] = {d: r for d, r in route[op, s].items() if user(d, r[1]) is not None or d in sends_on}
    route["A", 4] = {user(d, b): (e, b) for d, (e, b) in route["A", 4].items()}
    return route, user


def block_table(route, user, groups):
    m = len(RING)
    n = groups * m
    rows = []
    for d in range(n):
        row = []
        for key in [("A", 1), ("B", 1), ("A", 2), ("B", 2), ("A", 3), ("B", 3), ("A", 4)]:
            if d not in route[key]:
                row += [0, NONE]
                continue
            b = route[key][d][1]
            u = d if key == ("A", 4) else user(d, b)
            row += [b, NONE if u is None else OWN if u == d else MATE]
        o = d // m
        row += [0, NONE] if o < 2 else [d if o % 2 == 0 else d - 2 * m, MATE]
        rows.append(row)
    return rows


def position(axes):
    outer, inner = axes
    return lax.axis_index(outer) * lax.axis_size(inner) + lax.axis_index(inner)


def attend_block(sizes, q_of, kv_ref, bias, state, u, fresh):
    kv_heads, group_size, _ = sizes
    acc_ref, max_ref, sum_ref = state
    tile = 2 if group_size % 2 == 0 else 1
    bias = jnp.concatenate([bias] * tile, axis=1)
    for g in range(kv_heads):
        keys = kv_ref[:, g * HD : (g + 1) * HD]
        values = kv_ref[:, (kv_heads + g) * HD : (kv_heads + g + 1) * HD]
        for j in range(0, group_size, tile):
            columns = slice(j * HD, (j + tile) * HD)
            queries = jnp.concatenate([q_of(g * group_size + j + k) for k in range(tile)], axis=0)
            s = lax.dot_general(keys, queries, (((1,), (1,)), ((), ())), preferred_element_type=jnp.float32)
            s = s * SCALE + bias
            top = jnp.max(s, axis=0, keepdims=True)
            if not fresh:
                old = max_ref[u, g, :, columns]
                top = jnp.maximum(old, top)
                fade = jnp.exp2(old - top)
            p = jnp.exp2(s - top)
            total = jnp.sum(p, axis=0, keepdims=True)
            mixed = jnp.dot(values, p.astype(jnp.bfloat16), preferred_element_type=jnp.float32)
            max_ref[u, g, :, columns] = top
            sum_ref[u, g, :, columns] = total if fresh else sum_ref[u, g, :, columns] * fade + total
            acc_ref[u, g, :, columns] = mixed if fresh else acc_ref[u, g, :, columns] * fade + mixed


def head_of(ref):
    return lambda h: ref[:, h * HD : (h + 1) * HD]


def mask_bias(info_ref, n_docs, query_base, key_base, rows):
    query_pos = query_base + lax.broadcasted_iota(jnp.int32, (8, rows), 1)

    def latest(j, seen):
        start = info_ref[STARTS + j]
        return jnp.where(start <= query_pos, start, seen)

    seen = lax.fori_loop(0, n_docs, latest, jnp.zeros((8, rows), jnp.int32), unroll=n_docs <= 8)
    seen, query_pos = (jnp.concatenate([x] * (rows // 8), axis=0) for x in (seen, query_pos))
    key_pos = key_base + lax.broadcasted_iota(jnp.int32, (rows, rows), 0)
    return jnp.where((key_pos >= seen) & (key_pos <= query_pos), 0.0, NEG).astype(jnp.float32)


def pack_kernel(rows, n_docs, table, *refs):
    *far, k_ref, v_ref, kv_ref, info_ref, v_here, lengths_ref, order_ref, row_ref, sems = refs
    width = k_ref.shape[1]
    device = position(AXES)
    fetch_v = pltpu.make_async_copy(v_ref, v_here, sems.at[0])
    fetch_k = pltpu.make_async_copy(k_ref, kv_ref.at[:, pl.ds(0, width)], sems.at[1])
    small = [(far[0], lengths_ref), (far[1], order_ref)] + ([(far[2].at[device], row_ref)] if table else [])
    fetches = [pltpu.make_async_copy(a, b, sems.at[2 + k]) for k, (a, b) in enumerate(small)]
    for fetch in [fetch_v, fetch_k, *fetches]:
        fetch.start()
    for fetch in fetches:
        fetch.wait()

    mate = row_ref[0] if table else device
    info_ref[0] = device
    info_ref[1] = mate
    own_first, mate_first = device * rows, mate * rows

    def document(j, carry):
        start, own_seen, mate_seen = carry
        info_ref[STARTS + j] = start
        own_seen = jnp.where(start <= own_first, start, own_seen)
        mate_seen = jnp.where(start <= mate_first, start, mate_seen)
        return start + lengths_ref[order_ref[j]], own_seen, mate_seen

    zero = jnp.int32(0)
    _, own_seen, mate_seen = lax.fori_loop(0, n_docs, document, (zero, zero, zero), unroll=n_docs <= 8)
    for slot in range(SLOTS):
        if table:
            block, use = row_ref[1 + 2 * slot], row_ref[2 + 2 * slot]
        else:
            block, use = device - 1 - slot, OWN
        seen = jnp.where(use == OWN, own_seen, mate_seen)
        shown = (block >= 0) & (block * rows + rows > seen)
        info_ref[2 + 2 * slot] = block
        info_ref[3 + 2 * slot] = jnp.where(shown, use, NONE)

    fetch_v.wait()
    for g in range(width // HD):
        kv_ref[:, width + g * HD : width + (g + 1) * HD] = v_here[:, g * HD : (g + 1) * HD].T
    fetch_k.wait()


def own_kernel(sizes, n_docs, info_ref, q_ref, kv_ref, *state):
    rows = sizes[2]
    base = info_ref[0] * rows
    bias = mask_bias(info_ref, n_docs, base, base, rows)
    attend_block(sizes, head_of(q_ref), kv_ref, bias, state, OWN, True)


def back_kernel(sizes, n_docs, slot, info_ref, qm_ref, kv_ref, *refs):
    kv_heads, group_size, rows = sizes
    state = refs[3:]
    live = info_ref[3 + 2 * slot] == MATE

    @pl.when(live)
    def _():
        bias = mask_bias(info_ref, n_docs, info_ref[1] * rows, info_ref[2 + 2 * slot] * rows, rows)
        attend_block(sizes, head_of(qm_ref), kv_ref, bias, state, MATE, True)

    @pl.when(jnp.logical_not(live))
    def _():
        for g in range(kv_heads):
            for ref, value in zip(state, (0.0, NEG, 0.0)):
                ref[MATE, g] = jnp.full(ref.shape[2:], value, jnp.float32)


def add_block(sizes, n_docs, slot, info_ref, q_ref, qm_ref, kv_ref, state):
    rows = sizes[2]
    use = info_ref[3 + 2 * slot]

    @pl.when(use != NONE)
    def _():
        mine = use == OWN
        query_base = jnp.where(mine, info_ref[0], info_ref[1]) * rows
        bias = mask_bias(info_ref, n_docs, query_base, info_ref[2 + 2 * slot] * rows, rows)
        q_of = head_of(q_ref)
        if qm_ref is not None:
            q_own, q_mate = q_of, head_of(qm_ref)
            q_of = lambda h: jnp.where(mine, q_own(h), q_mate(h))
        attend_block(sizes, q_of, kv_ref, bias, state, use, False)


def add_kernel(sizes, n_docs, slot, mated, info_ref, q_ref, *refs):
    qm_ref, refs = (refs[0], refs[1:]) if mated else (None, refs)
    add_block(sizes, n_docs, slot, info_ref, q_ref, qm_ref, refs[0], refs[4:])


def split3(x):
    a = x.astype(jnp.bfloat16)
    rest = x - a.astype(jnp.float32)
    b = rest.astype(jnp.bfloat16)
    return a, b, (rest - b.astype(jnp.float32)).astype(jnp.bfloat16)


def part_kernel(sizes, n_docs, slot, info_ref, q_ref, qm_ref, kv_ref, a_in, m_in, s_in, part_ref, *state):
    kv_heads, group_size, rows = sizes
    add_block(sizes, n_docs, slot, info_ref, q_ref, qm_ref, kv_ref, state)
    acc_ref, max_ref, sum_ref = state
    width = group_size * HD
    heads = kv_heads * group_size
    tops, sums = [], []
    for g in range(kv_heads):
        top, total = max_ref[MATE, g], sum_ref[MATE, g]
        share = 1.0 / jnp.where(total > 0, total, 1.0)
        part_ref[:, g * width : (g + 1) * width] = (acc_ref[MATE, g] * share).astype(jnp.bfloat16)
        for j in range(group_size):
            tops.append(top[:, j * HD : (j + 1) * HD])
            sums.append(total[:, j * HD : (j + 1) * HD])
    for column, stats in enumerate((tops, sums)):
        place = (heads + column) * HD
        for k, piece in enumerate(split3(jnp.concatenate(stats, axis=0))):
            part_ref[k * heads : (k + 1) * heads, place : place + HD] = piece


def merge_kernel(sizes, mated, info_ref, *refs):
    kv_heads, group_size, rows = sizes
    heads = kv_heads * group_size
    part_ref, refs = (refs[0], refs[1:]) if mated else (None, refs)
    acc_ref, max_ref, sum_ref, out_ref = refs
    if mated:
        tops, sums = (
            sum(part_ref[k * heads : (k + 1) * heads, c * HD : (c + 1) * HD].astype(jnp.float32) for k in range(3))
            for c in (heads, heads + 1)
        )
        met = info_ref[1] != info_ref[0]
        tops, sums = jnp.where(met, tops, NEG), jnp.where(met, sums, 0.0)
    for g in range(kv_heads):
        for j in range(group_size):
            h, mine = g * group_size + j, slice(j * HD, (j + 1) * HD)
            numer, top, total = acc_ref[OWN, g, :, mine], max_ref[OWN, g, :, mine], sum_ref[OWN, g, :, mine]
            if mated:
                both = jnp.maximum(top, tops[h : h + 1])
                weight, other = jnp.exp2(top - both), jnp.exp2(tops[h : h + 1] - both) * sums[h : h + 1]
                share = 1.0 / (total * weight + other)
                theirs = jnp.where(met, part_ref[:, h * HD : (h + 1) * HD].astype(jnp.float32), 0.0)
                out = numer * (weight * share) + theirs * (other * share)
            else:
                out = numer * (1.0 / total)
            out_ref[:, h * HD : (h + 1) * HD] = out.astype(jnp.bfloat16).T


def calls(sizes, n_docs, info, mated):
    kv_heads, group_size, rows = sizes
    tall = group_size * rows
    sets = 2 if mated else 1
    state = [
        pltpu.VMEM((sets, kv_heads, HD, tall), jnp.float32),
        pltpu.VMEM((sets, kv_heads, 1, tall), jnp.float32),
        pltpu.VMEM((sets, kv_heads, 1, tall), jnp.float32),
    ]
    smem, vmem = pl.BlockSpec(memory_space=pltpu.SMEM), pl.BlockSpec(memory_space=pltpu.VMEM)
    held = []

    def call(kernel, arrays, out, name, keeps=True, flops=FLOPS):
        n_in = 1 + len(arrays)
        out = out + (state if keeps else [])
        result = pl.pallas_call(
            kernel,
            out_shape=out,
            in_specs=[smem] + [vmem] * (len(arrays) + len(held)),
            out_specs=[vmem] * len(out),
            input_output_aliases={n_in + k: len(out) - 3 + k for k in range(len(held))} if keeps else {},
            compiler_params=pltpu.CompilerParams(vmem_limit_bytes=VMEM_LIMIT),
            cost_estimate=pl.CostEstimate(flops=flops, bytes_accessed=1 << 20, transcendentals=0),
            name=name,
        )(info, *arrays, *held)
        if not keeps:
            return result
        held[:] = result[-3:]
        return result[:-3]

    def own(q, kv):
        call(functools.partial(own_kernel, sizes, n_docs), [q, kv], [], "own_block")

    def back(slot, qm, kv):
        call(functools.partial(back_kernel, sizes, n_docs, slot), [qm, kv], [], "mate_first_block")

    def add(slot, q, qm, kv, flops=FLOPS):
        qs = [q] if qm is None else [q, qm]
        kernel = functools.partial(add_kernel, sizes, n_docs, slot, qm is not None)
        call(kernel, qs + [kv], [], "add_block", flops=flops)

    def part(slot, q, qm, kv):
        out = jax.ShapeDtypeStruct((rows, (kv_heads * group_size + 2) * HD), jnp.bfloat16)
        return call(functools.partial(part_kernel, sizes, n_docs, slot), [q, qm, kv], [out], "mate_part")[0]

    def merge(parts):
        out = jax.ShapeDtypeStruct((rows, kv_heads * group_size * HD), jnp.bfloat16)
        return call(functools.partial(merge_kernel, sizes, mated), parts, [out], "merge", keeps=False)[0]

    def after(block):
        block, held[-1] = lax.optimization_barrier((block, held[-1]))
        return block

    return own, back, add, part, merge, after


def pack(keys, values, lengths, pack_order, table):
    rows, width = keys.shape
    n_docs = lengths.shape[0]
    hbm = pl.BlockSpec(memory_space=pltpu.HBM)
    scalars = [lengths, pack_order] + ([] if table is None else [table])
    return pl.pallas_call(
        functools.partial(pack_kernel, rows, n_docs, table is not None),
        out_shape=[
            jax.ShapeDtypeStruct((rows, 2 * width), keys.dtype),
            INFO_SPACE((STARTS + n_docs,), jnp.int32),
        ],
        in_specs=[hbm] * (len(scalars) + 2),
        out_specs=[pl.BlockSpec(memory_space=pltpu.VMEM), pl.BlockSpec(memory_space=pltpu.SMEM)],
        scratch_shapes=[
            pltpu.VMEM((rows, width), values.dtype),
            pltpu.SMEM((n_docs,), jnp.int32),
            pltpu.SMEM((n_docs,), jnp.int32),
            pltpu.SMEM((1 + 2 * SLOTS,), jnp.int32),
            pltpu.SemaphoreType.DMA((5,)),
        ],
        name="pack_keys_values",
    )(*scalars, keys, values)


def ring_shards(groups, queries, keys, values, lengths, pack_order):
    rows, kv_heads = queries.shape[0], keys.shape[1] // HD
    m = len(RING)
    sizes = (kv_heads, queries.shape[1] // keys.shape[1], rows)
    route, user = make_plan(groups, FIRST // rows)
    mate_of = [d if d < 2 * m else d ^ m for d in range(groups * m)]
    table = jnp.array([[mate] + row for mate, row in zip(mate_of, block_table(route, user, groups))], jnp.int32)
    kv, info = pack(keys, values, lengths, pack_order, table)
    own, back, add, part, merge, after = calls(sizes, lengths.shape[0], info, True)

    def send(block, op, step):
        return lax.ppermute(block, AXES, sorted((e, d) for d, (e, _) in route[op, step].items()))

    mates = [(d, d ^ m) for d in range(2 * m, groups * m)]
    eight_back = [(m + i, 3 * m + i) for i in range(m)] + [(2 * m + i, 2 * m + i) for i in range(m)]
    a1 = send(kv, "A", 1)
    q = queries
    own(q, kv)
    b1 = send(kv, "B", 1)
    qm = lax.ppermute(q, AXES, mates)
    kv8 = lax.ppermute(kv, AXES, eight_back)
    a2 = send(after(a1), "A", 2)
    back(7, qm, kv8)
    add(0, q, qm, a1)
    b2 = send(after(b1), "B", 2)
    add(1, q, qm, b1)
    a3 = send(after(a2), "A", 3)
    add(2, q, qm, a2)
    b3 = send(after(b2), "B", 3)
    add(3, q, qm, b2)
    a4 = send(after(a3), "A", 4)
    add(4, q, qm, a3)
    mine = part(5, q, qm, b3)
    theirs = lax.ppermute(mine, AXES, mates)
    add(6, q, None, a4, LAST_FLOPS)
    return merge([theirs])


def chain_shards(queries, keys, values, lengths, pack_order):
    rows, kv_heads = queries.shape[0], keys.shape[1] // HD
    sizes = (kv_heads, queries.shape[1] // keys.shape[1], rows)
    n = lax.axis_size(AXES)
    kv, info = pack(keys, values, lengths, pack_order, None)
    own, back, add, part, merge, after = calls(sizes, lengths.shape[0], info, False)
    q = queries
    own(q, kv)
    for hop in range(HOPS):
        kv = lax.ppermute(kv, AXES, [(d, d + 1) for d in range(n - 1)])
        add(hop, q, None, kv)
    return merge([])


def solution(mesh):
    spec, whole = P(AXES, None), P()
    outer, inner = mesh.shape["outer"], mesh.shape["inner"]
    ring = outer == 4 and inner == len(RING) == HOPS
    shards = functools.partial(ring_shards, outer) if ring else chain_shards
    return jax.shard_map(
        shards, mesh=mesh, in_specs=(spec, spec, spec, whole, whole), out_specs=spec, check_vma=False
    )
```

time: 76.8 us -> 64.4 us (0.84)
  the two profiles are of different devices: /device:TPU:28 before, /device:TPU:26 now
where the time goes in v2:
time: 64.4 us; the launch traced here: 63.9 us
  waiting for transfers between devices  26.6 us (41%)
  starting transfers between devices  23.7 us (37%)
  Pallas kernels  11.2 us (17%)
  local copies, waits for them, and re-layouts  2.26 us (4%)
    ppermute x7, waiting for transfers between devices, send(): lax.ppermute(block, AXES, sorted(((e, d) for d, (e, _) in route[op, step]...  26.6 us
    ppermute x7, starting transfers between devices, send(): lax.ppermute(block, AXES, sorted(((e, d) for d, (e, _) in route[op, step]...  18.1 us
    pallas_call x10, Pallas kernels, call(): pl.pallas_call(kernel, out_shape=out, in_specs=[smem] + [vmem] * (len(arr...  9.28 us
    unnamed x6, local copies, waits for them, and re-layouts  2.26 us
    ppermute x1, starting transfers between devices, ring_shards(): theirs = lax.ppermute(mine, AXES, mates)  1.92 us
    pallas_call x1, Pallas kernels, pack(): pl.pallas_call(functools.partial(pack_kernel, rows, n_docs, table is not...  1.91 us
    ppermute x1, starting transfers between devices, ring_shards(): qm = lax.ppermute(q, AXES, mates)  1.91 us
    ppermute x1, starting transfers between devices, ring_shards(): kv8 = lax.ppermute(kv, AXES, eight_back)  1.7 us
  transfers between devices with their start and end apart: 10, of which 4 were waited for; matrix products, arithmetic and copies ran while one was open for 0% of the time, Pallas kernels for 15%

profile of v2, /device:TPU:26, one launch (start us, length us, event | category | flops | bytes accessed | tf_op | source)
XLA Modules:
  0.0 63.9 jit_solution(3458686569599562026)
XLA Ops:
  0.0 1.9 %collective-permute-start = (bf16[128,4096]{1,0:T(8,128)(2,1)}, bf16[128,4096]{1,0:T(8,128)(2,1)S(1)}, u32[]{:S(2)}, u32[]{:S(2)}) collective-permute-start(bf16[128,4096]{1,0:T(8,128)(2,1)} %q_ref.15), channel_id=1, source_target_pairs={{16,24},{17,25},{18,26},{19,27},{20,28},{21,29},{22,30},{23,31},{2... | collective-permute-start | bytes 3145736 | tf_op jit(solution)/shard_map/ppermute | solution.py:373
  1.9 1.9 %pack_keys_values.1 = (bf16[128,2048]{1,0:T(8,128)(2,1)}, s32[26]{0:T(128)S(4)}) custom-call(s32[8]{0:T(128)} %refs_0_.1, s32[8]{0:T(128)} %refs_1_.1, s32[32,17]{1,0:T(8,128)} %constant.2.clone.refs_2_, bf16[128,1024]{1,0:T(8,128)(2,1)} %refs_3_.1, bf16[128,1024]{1,0:T(8,128)(2,1)} %refs_4_.1), custom_call_target="tpu_custom_call" | custom-call | tf_op jit(solution)/shard_map/pack_keys_values/pallas_call | solution.py:335
  3.8 3.4 %collective-permute-start.2 = (bf16[128,2048]{1,0:T(8,128)(2,1)}, bf16[128,2048]{1,0:T(8,128)(2,1)S(1)}, u32[]{:S(2)}, u32[]{:S(2)}) collective-permute-start(bf16[128,2048]{1,0:T(8,128)(2,1)} %get-tuple-element.46.kv_ref), channel_id=1, source_target_pairs={{0,2},{1,0},{2,4},{3,1},{4,6},{6,7},{8,9},{9,11},{10,24},{11,13},{... | collective-permute-start | bytes 1572872 | tf_op jit(solution)/shard_map/ppermute | solution.py:365
  7.3 1.7 %collective-permute-start.3 = (bf16[128,2048]{1,0:T(8,128)(2,1)}, bf16[128,2048]{1,0:T(8,128)(2,1)S(1)}, u32[]{:S(2)}, u32[]{:S(2)}) collective-permute-start(bf16[128,2048]{1,0:T(8,128)(2,1)} %get-tuple-element.46.kv_ref), channel_id=1, source_target_pairs={{8,24},{9,25},{10,26},{11,27},{12,28},{13,29},{14,30},{15,31},{16,... | collective-permute-start | bytes 1572872 | tf_op jit(solution)/shard_map/ppermute | solution.py:374
  9.0 2.4 %collective-permute-start.1 = (bf16[128,2048]{1,0:T(8,128)(2,1)}, bf16[128,2048]{1,0:T(8,128)(2,1)S(1)}, u32[]{:S(2)}, u32[]{:S(2)}) collective-permute-start(bf16[128,2048]{1,0:T(8,128)(2,1)} %get-tuple-element.46.kv_ref), channel_id=1, source_target_pairs={{0,1},{1,3},{2,0},{3,5},{5,7},{8,10},{9,24},{10,12},{11,25},{12,14... | collective-permute-start | bytes 1572872 | tf_op jit(solution)/shard_map/ppermute | solution.py:365
  11.4 1.2 %copy-done = bf16[128,4096]{1,0:T(8,128)(2,1)S(1)} copy-done((bf16[128,4096]{1,0:T(8,128)(2,1)S(1)}, bf16[128,4096]{1,0:T(8,128)(2,1)}, u32[]{:S(2)}) %copy-start) | copy-done | bytes 1048600
  12.6 1.0 %copy-done.2 = bf16[128,2048]{1,0:T(8,128)(2,1)S(1)} copy-done((bf16[128,2048]{1,0:T(8,128)(2,1)S(1)}, bf16[128,2048]{1,0:T(8,128)(2,1)}, u32[]{:S(2)}) %copy-start.2) | copy-done | bytes 524312
  13.7 1.1 %own_block.1 = (f32[2,8,128,512]{3,2,1,0:T(8,128)S(1)}, f32[2,8,1,512]{3,2,1,0:T(1,128)S(1)}, f32[2,8,1,512]{3,2,1,0:T(1,128)S(1)}) custom-call(s32[26]{0:T(128)S(4)} %get-tuple-element.45.info_ref, bf16[128,4096]{1,0:T(8,128)(2,1)S(1)} %copy-done, bf16[128,2048]{1,0:T(8,128)(2,1)S(1)} %copy-done.2), custom_call_target="tpu_custom_call" | custom-call | flops 800000000 | bytes 1048576 | tf_op jit(solution)/shard_map/own_block/pallas_call | solution.py:289
  14.8 3.8 %collective-permute-done.2.refs_1_ = bf16[128,2048]{1,0:T(8,128)(2,1)S(1)} collective-permute-done((bf16[128,2048]{1,0:T(8,128)(2,1)}, bf16[128,2048]{1,0:T(8,128)(2,1)S(1)}, u32[]{:S(2)}, u32[]{:S(2)}) %collective-permute-start.2) | collective-permute-done | bytes 524320 | tf_op jit(solution)/shard_map/ppermute | solution.py:365
  18.6 3.4 %collective-permute-start.5 = (bf16[128,2048]{1,0:T(8,128)(2,1)S(1)}, bf16[128,2048]{1,0:T(8,128)(2,1)S(1)}, u32[]{:S(2)}, u32[]{:S(2)}) collective-permute-start(bf16[128,2048]{1,0:T(8,128)(2,1)S(1)} %collective-permute-done.2.refs_1_), channel_id=1, source_target_pairs={{0,2},{1,0},{2,4},{4,6},{6,7},{8,9},{9,11},{11,13},{13,15},{15,14}... | collective-permute-start | bytes 1572872 | tf_op jit(solution)/shard_map/ppermute | solution.py:365
  22.2 1.3 %add_block.6 = (f32[2,8,128,512]{3,2,1,0:T(8,128)S(1)}, f32[2,8,1,512]{3,2,1,0:T(1,128)S(1)}, f32[2,8,1,512]{3,2,1,0:T(1,128)S(1)}) custom-call(s32[26]{0:T(128)S(4)} %get-tuple-element.45.info_ref, bf16[128,4096]{1,0:T(8,128)(2,1)S(1)} %copy-done.1, ...), custom_call_target="tpu_custom_call", output_to_operand_aliasing={{0}: (4, {}), {1}: (5, {}), {2}: (6, {})} | custom-call | flops 800000000 | bytes 1048576 | tf_op jit(solution)/shard_map/add_block/pallas_call | solution.py:289
  23.5 2.4 %collective-permute-start.4 = (bf16[128,2048]{1,0:T(8,128)(2,1)S(1)}, bf16[128,2048]{1,0:T(8,128)(2,1)S(1)}, u32[]{:S(2)}, u32[]{:S(2)}) collective-permute-start(bf16[128,2048]{1,0:T(8,128)(2,1)S(1)} %collective-permute-done.1.refs_1_), channel_id=1, source_target_pairs={{0,1},{1,3},{3,5},{5,7},{7,6},{8,26},{10,12},{12,14},{14,15},{15,2... | collective-permute-start | bytes 1572872 | tf_op jit(solution)/shard_map/ppermute | solution.py:365
  25.9 7.9 %collective-permute-done.5.refs_1_ = bf16[128,2048]{1,0:T(8,128)(2,1)S(1)} collective-permute-done((bf16[128,2048]{1,0:T(8,128)(2,1)S(1)}, bf16[128,2048]{1,0:T(8,128)(2,1)S(1)}, u32[]{:S(2)}, u32[]{:S(2)}) %collective-permute-start.5) | collective-permute-done | bytes 524320 | tf_op jit(solution)/shard_map/ppermute | solution.py:365
  33.8 2.5 %collective-permute-start.7 = (bf16[128,2048]{1,0:T(8,128)(2,1)S(1)}, bf16[128,2048]{1,0:T(8,128)(2,1)S(1)}, u32[]{:S(2)}, u32[]{:S(2)}) collective-permute-start(bf16[128,2048]{1,0:T(8,128)(2,1)S(1)} %collective-permute-done.5.refs_1_), channel_id=1, source_target_pairs={{0,2},{2,4},{4,6},{6,7},{7,5},{9,27},{11,13},{13,15},{14,28},{15,1... | collective-permute-start | bytes 1572872 | tf_op jit(solution)/shard_map/ppermute | solution.py:365
  36.3 1.3 %add_block.8 = (f32[2,8,128,512]{3,2,1,0:T(8,128)S(1)}, f32[2,8,1,512]{3,2,1,0:T(1,128)S(1)}, f32[2,8,1,512]{3,2,1,0:T(1,128)S(1)}) custom-call(s32[26]{0:T(128)S(4)} %get-tuple-element.45.info_ref, bf16[128,4096]{1,0:T(8,128)(2,1)S(1)} %copy-done.1, ...), custom_call_target="tpu_custom_call", output_to_operand_aliasing={{0}: (4, {}), {1}: (5, {}), {2}: (6, {})} | custom-call | flops 800000000 | bytes 1048576 | tf_op jit(solution)/shard_map/add_block/pallas_call | solution.py:289
  37.6 2.1 %collective-permute-start.6 = (bf16[128,2048]{1,0:T(8,128)(2,1)S(1)}, bf16[128,2048]{1,0:T(8,128)(2,1)S(1)}, u32[]{:S(2)}, u32[]{:S(2)}) collective-permute-start(bf16[128,2048]{1,0:T(8,128)(2,1)S(1)} %collective-permute-done.4.refs_1_), channel_id=1, source_target_pairs={{1,3},{3,5},{5,7},{7,6},{10,12},{12,14},{14,15},{15,13},{16,17},{1... | collective-permute-start | bytes 1572872 | tf_op jit(solution)/shard_map/ppermute | solution.py:365
  39.7 1.3 %add_block.9 = (f32[2,8,128,512]{3,2,1,0:T(8,128)S(1)}, f32[2,8,1,512]{3,2,1,0:T(1,128)S(1)}, f32[2,8,1,512]{3,2,1,0:T(1,128)S(1)}) custom-call(s32[26]{0:T(128)S(4)} %get-tuple-element.45.info_ref, bf16[128,4096]{1,0:T(8,128)(2,1)S(1)} %copy-done.1, ...), custom_call_target="tpu_custom_call", output_to_operand_aliasing={{0}: (4, {}), {1}: (5, {}), {2}: (6, {})} | custom-call | flops 800000000 | bytes 1048576 | tf_op jit(solution)/shard_map/add_block/pallas_call | solution.py:289
  41.0 9.1 %collective-permute-done.7.refs_1_ = bf16[128,2048]{1,0:T(8,128)(2,1)S(1)} collective-permute-done((bf16[128,2048]{1,0:T(8,128)(2,1)S(1)}, bf16[128,2048]{1,0:T(8,128)(2,1)S(1)}, u32[]{:S(2)}, u32[]{:S(2)}) %collective-permute-start.7) | collective-permute-done | bytes 524320 | tf_op jit(solution)/shard_map/ppermute | solution.py:365
  50.1 1.9 %collective-permute-start.9 = (bf16[128,2048]{1,0:T(8,128)(2,1)S(1)}, bf16[128,2048]{1,0:T(8,128)(2,1)S(1)}, u32[]{:S(2)}, u32[]{:S(2)}) collective-permute-start(bf16[128,2048]{1,0:T(8,128)(2,1)S(1)} %collective-permute-done.7.refs_1_), channel_id=1, source_target_pairs={{2,4},{4,6},{6,7},{7,5},{11,13},{13,15},{14,12},{15,14},{16,26},{1... | collective-permute-start | bytes 1572872 | tf_op jit(solution)/shard_map/ppermute | solution.py:365
  52.0 1.4 %mate_part.1 = (bf16[128,4352]{1,0:T(8,128)(2,1)S(1)}, f32[2,8,128,512]{3,2,1,0:T(8,128)S(1)}, f32[2,8,1,512]{3,2,1,0:T(1,128)S(1)}, f32[2,8,1,512]{3,2,1,0:T(1,128)S(1)}) custom-call(s32[26]{0:T(128)S(4)} %get-tuple-element.45.info_ref, bf16[128,4096]{1,0:T(8,128)(2,1)S(1)} %copy-done.1, ...), custom_call_target="tpu_custom_call", output_to_operand_aliasing={{1}: (4, {}), {2}: (5, {}), {3}: (6, {})} | custom-call | flops 800000000 | bytes 1048576 | tf_op jit(solution)/shard_map/mate_part/pallas_call | solution.py:289
  53.4 1.9 %collective-permute-start.8 = (bf16[128,4352]{1,0:T(8,128)(2,1)S(1)}, bf16[128,4352]{1,0:T(8,128)(2,1)S(1)}, u32[]{:S(2)}, u32[]{:S(2)}) collective-permute-start(bf16[128,4352]{1,0:T(8,128)(2,1)S(1)} %get-tuple-element.77), channel_id=1, source_target_pairs={{16,24},{17,25},{18,26},{19,27},{20,28},{21,29},{22,30},{23,31},{2... | collective-permute-start | bytes 3342344 | tf_op jit(solution)/shard_map/ppermute | solution.py:387
  55.4 5.8 %collective-permute-done.9.refs_0_ = bf16[128,2048]{1,0:T(8,128)(2,1)S(1)} collective-permute-done((bf16[128,2048]{1,0:T(8,128)(2,1)S(1)}, bf16[128,2048]{1,0:T(8,128)(2,1)S(1)}, u32[]{:S(2)}, u32[]{:S(2)}) %collective-permute-start.9) | collective-permute-done | bytes 524320 | tf_op jit(solution)/shard_map/ppermute | solution.py:365
  61.1 1.2 %add_block.11 = (f32[2,8,128,512]{3,2,1,0:T(8,128)S(1)}, f32[2,8,1,512]{3,2,1,0:T(1,128)S(1)}, f32[2,8,1,512]{3,2,1,0:T(1,128)S(1)}) custom-call(s32[26]{0:T(128)S(4)} %get-tuple-element.45.info_ref, bf16[128,4096]{1,0:T(8,128)(2,1)S(1)} %copy-done.1, ...), custom_call_target="tpu_custom_call", output_to_operand_aliasing={{0}: (3, {}), {1}: (4, {}), {2}: (5, {})} | custom-call | flops 49999998976 | bytes 1048576 | tf_op jit(solution)/shard_map/add_block/pallas_call | solution.py:289
  62.3 1.6 %merge.1 = bf16[128,4096]{1,0:T(8,128)(2,1)} custom-call(s32[26]{0:T(128)S(4)} %get-tuple-element.45.info_ref, bf16[128,4352]{1,0:T(8,128)(2,1)S(1)} %collective-permute-done.8.refs_0_, f32[2,8,128,512]{3,2,1,0:T(8,128)S(1)} %get-tuple-element.82.refs_1_, f32[2,8,1,512]{3,2,1,0:T(1,128)S(1)} %get-tuple-element.83.refs_2_, ...), custom_call_target="tpu_custom_call" | custom-call | flops 800000000 | bytes 1048576 | tf_op jit(solution)/shard_map/merge/pallas_call | solution.py:289
  (13 shorter events, 0.2 us)
Async XLA Ops:
  0.0 22.0 %collective-permute-start = (bf16[128,4096]{1,0:T(8,128)(2,1)}, bf16[128,4096]{1,0:T(8,128)(2,1)S(1)}, u32[]{:S(2)}, u32[]{:S(2)}) collective-permute-start(bf16[128,4096]{1,0:T(8,128)(2,1)} %q_ref.15), channel_id=1, source_target_pairs={{16,24},{17,25},{18,26},{19,27},{20,28},{21,29},{22,30},{23,31},{2... | collective-permute-start | bytes 3145736 | tf_op jit(solution)/shard_map/ppermute | solution.py:373
  3.8 14.7 %collective-permute-start.2 = (bf16[128,2048]{1,0:T(8,128)(2,1)}, bf16[128,2048]{1,0:T(8,128)(2,1)S(1)}, u32[]{:S(2)}, u32[]{:S(2)}) collective-permute-start(bf16[128,2048]{1,0:T(8,128)(2,1)} %get-tuple-element.46.kv_ref), channel_id=1, source_target_pairs={{0,2},{1,0},{2,4},{3,1},{4,6},{6,7},{8,9},{9,11},{10,24},{11,13},{... | collective-permute-start | bytes 1572872 | tf_op jit(solution)/shard_map/ppermute | solution.py:365
  7.3 14.7 %collective-permute-start.3 = (bf16[128,2048]{1,0:T(8,128)(2,1)}, bf16[128,2048]{1,0:T(8,128)(2,1)S(1)}, u32[]{:S(2)}, u32[]{:S(2)}) collective-permute-start(bf16[128,2048]{1,0:T(8,128)(2,1)} %get-tuple-element.46.kv_ref), channel_id=1, source_target_pairs={{8,24},{9,25},{10,26},{11,27},{12,28},{13,29},{14,30},{15,31},{16,... | collective-permute-start | bytes 1572872 | tf_op jit(solution)/shard_map/ppermute | solution.py:374
  9.0 14.5 %collective-permute-start.1 = (bf16[128,2048]{1,0:T(8,128)(2,1)}, bf16[128,2048]{1,0:T(8,128)(2,1)S(1)}, u32[]{:S(2)}, u32[]{:S(2)}) collective-permute-start(bf16[128,2048]{1,0:T(8,128)(2,1)} %get-tuple-element.46.kv_ref), channel_id=1, source_target_pairs={{0,1},{1,3},{2,0},{3,5},{5,7},{8,10},{9,24},{10,12},{11,25},{12,14... | collective-permute-start | bytes 1572872 | tf_op jit(solution)/shard_map/ppermute | solution.py:365
  11.4 1.2 %copy-start = (bf16[128,4096]{1,0:T(8,128)(2,1)S(1)}, bf16[128,4096]{1,0:T(8,128)(2,1)}, u32[]{:S(2)}) copy-start(bf16[128,4096]{1,0:T(8,128)(2,1)} %q_ref.15) | copy-start | bytes 3145732
  12.6 1.0 %copy-start.2 = (bf16[128,2048]{1,0:T(8,128)(2,1)S(1)}, bf16[128,2048]{1,0:T(8,128)(2,1)}, u32[]{:S(2)}) copy-start(bf16[128,2048]{1,0:T(8,128)(2,1)} %get-tuple-element.46.kv_ref) | copy-start | bytes 1572868
  13.7 8.5 %copy-start.1 = (bf16[128,4096]{1,0:T(8,128)(2,1)S(1)}, bf16[128,4096]{1,0:T(8,128)(2,1)}, u32[]{:S(2)}) copy-start(bf16[128,4096]{1,0:T(8,128)(2,1)} %q_ref.15) | copy-start | bytes 3145732
  18.6 15.3 %collective-permute-start.5 = (bf16[128,2048]{1,0:T(8,128)(2,1)S(1)}, bf16[128,2048]{1,0:T(8,128)(2,1)S(1)}, u32[]{:S(2)}, u32[]{:S(2)}) collective-permute-start(bf16[128,2048]{1,0:T(8,128)(2,1)S(1)} %collective-permute-done.2.refs_1_), channel_id=1, source_target_pairs={{0,2},{1,0},{2,4},{4,6},{6,7},{8,9},{9,11},{11,13},{13,15},{15,14}... | collective-permute-start | bytes 1572872 | tf_op jit(solution)/shard_map/ppermute | solution.py:365
  23.5 14.2 %collective-permute-start.4 = (bf16[128,2048]{1,0:T(8,128)(2,1)S(1)}, bf16[128,2048]{1,0:T(8,128)(2,1)S(1)}, u32[]{:S(2)}, u32[]{:S(2)}) collective-permute-start(bf16[128,2048]{1,0:T(8,128)(2,1)S(1)} %collective-permute-done.1.refs_1_), channel_id=1, source_target_pairs={{0,1},{1,3},{3,5},{5,7},{7,6},{8,26},{10,12},{12,14},{14,15},{15,2... | collective-permute-start | bytes 1572872 | tf_op jit(solution)/shard_map/ppermute | solution.py:365
  33.8 16.2 %collective-permute-start.7 = (bf16[128,2048]{1,0:T(8,128)(2,1)S(1)}, bf16[128,2048]{1,0:T(8,128)(2,1)S(1)}, u32[]{:S(2)}, u32[]{:S(2)}) collective-permute-start(bf16[128,2048]{1,0:T(8,128)(2,1)S(1)} %collective-permute-done.5.refs_1_), channel_id=1, source_target_pairs={{0,2},{2,4},{4,6},{6,7},{7,5},{9,27},{11,13},{13,15},{14,28},{15,1... | collective-permute-start | bytes 1572872 | tf_op jit(solution)/shard_map/ppermute | solution.py:365
  37.6 14.4 %collective-permute-start.6 = (bf16[128,2048]{1,0:T(8,128)(2,1)S(1)}, bf16[128,2048]{1,0:T(8,128)(2,1)S(1)}, u32[]{:S(2)}, u32[]{:S(2)}) collective-permute-start(bf16[128,2048]{1,0:T(8,128)(2,1)S(1)} %collective-permute-done.4.refs_1_), channel_id=1, source_target_pairs={{1,3},{3,5},{5,7},{7,6},{10,12},{12,14},{14,15},{15,13},{16,17},{1... | collective-permute-start | bytes 1572872 | tf_op jit(solution)/shard_map/ppermute | solution.py:365
  50.1 11.1 %collective-permute-start.9 = (bf16[128,2048]{1,0:T(8,128)(2,1)S(1)}, bf16[128,2048]{1,0:T(8,128)(2,1)S(1)}, u32[]{:S(2)}, u32[]{:S(2)}) collective-permute-start(bf16[128,2048]{1,0:T(8,128)(2,1)S(1)} %collective-permute-done.7.refs_1_), channel_id=1, source_target_pairs={{2,4},{4,6},{6,7},{7,5},{11,13},{13,15},{14,12},{15,14},{16,26},{1... | collective-permute-start | bytes 1572872 | tf_op jit(solution)/shard_map/ppermute | solution.py:365
  53.4 8.9 %collective-permute-start.8 = (bf16[128,4352]{1,0:T(8,128)(2,1)S(1)}, bf16[128,4352]{1,0:T(8,128)(2,1)S(1)}, u32[]{:S(2)}, u32[]{:S(2)}) collective-permute-start(bf16[128,4352]{1,0:T(8,128)(2,1)S(1)} %get-tuple-element.77), channel_id=1, source_target_pairs={{16,24},{17,25},{18,26},{19,27},{20,28},{21,29},{22,30},{23,31},{2... | collective-permute-start | bytes 3342344 | tf_op jit(solution)/shard_map/ppermute | solution.py:387

commit v3 on v2

--- a/solution.py
+++ b/solution.py
@@ -17,10 +17,9 @@
 RING = (0, 2, 4, 6, 7, 5, 3, 1)
 OWN, MATE, NONE = 0, 1, 2
 VMEM_LIMIT = 40 * 1024 * 1024
-SLOTS = 8
+SLOTS = 10
 STARTS = 2 + 2 * SLOTS
-INFO_SPACE = pltpu.SMEM
-FLOPS = 800_000_000
+FLOPS = 1000
 LAST_FLOPS = 50_000_000_000
 
 
@@ -29,54 +28,60 @@
     n = groups * m
     place = {j: p for p, j in enumerate(RING)}
 
-    def held(d, j):
-        o, i = divmod(d, m)
-        if j == i:
-            return d
-        if o % 2 == 0 or j < i:
-            return o * m + j
-        return ((o + 2) % groups) * m + j
+    def held(chip, odd, j):
+        x, i = divmod(chip, m)
+        o = 2 * x + odd
+        if odd and j > i and (i, j) != (0, 1):
+            o = (o + 2) % groups
+        return o * m + j
+
+    straight = [(n - m + 2, n - m + 3), (n - m + 3, n - m + 4), (n - 3 * m + 1, n - 2 * m)]
 
     def uses(q, b):
-        return 0 < q - b <= HOPS and not (b < first_blocks <= q)
+        return 0 < q - b <= HOPS and not (b < first_blocks <= q) and (b, q) not in straight
 
     def user(d, b):
         return d if uses(d, b) else d ^ m if uses(d ^ m, b) else None
 
-    ops = [("A", 1), ("B", 1), ("A", 2), ("B", 2), ("A", 3), ("B", 3), ("A", 4)]
+    ops = [("own", 1), ("mate", 1), ("own", 2), ("mate", 2), ("own", 3), ("mate", 3), ("own", 4)]
     route = {}
     for op, s in ops:
         route[op, s] = {}
         for d in range(n):
             o, i = divmod(d, m)
-            way = 1 if (o % 2 == 0) == (op == "A") else -1
+            x, core = divmod(o, 2)
+            odd = core if op == "own" else 1 - core
+            way = 1 if core else -1
             j = RING[(place[i] - way * s) % m]
-            b = held(d, j)
+            b = held(x * m + i, odd, j)
             behind = RING[(place[i] - way) % m]
-            (source,) = [e for e in range(behind, n, m) if (e // m) % 2 == o % 2 and held(e, j) == b]
+            (source,) = [
+                (2 * y + core) * m + behind for y in range(groups // 2) if held(y * m + behind, odd, j) == b
+            ]
             route[op, s][d] = (source, b)
     for op, s in reversed(ops):
         sends_on = {e for e, _ in route.get((op, s + 1), {}).values()}
         route[op, s] = {d: r for d, r in route[op, s].items() if user(d, r[1]) is not None or d in sends_on}
-    route["A", 4] = {user(d, b): (e, b) for d, (e, b) in route["A", 4].items()}
-    return route, user
-
-
-def block_table(route, user, groups):
+    route["own", 4] = {user(d, b): (e, b) for d, (e, b) in route["own", 4].items()}
+    return route, user, straight
+
+
+def block_table(route, user, straight, groups):
     m = len(RING)
-    n = groups * m
     rows = []
-    for d in range(n):
-        row = []
-        for key in [("A", 1), ("B", 1), ("A", 2), ("B", 2), ("A", 3), ("B", 3), ("A", 4)]:
+    for d in range(groups * m):
+        row = [d ^ m]
+        for key in [("own", 1), ("mate", 1), ("own", 2), ("mate", 2), ("own", 3), ("mate", 3), ("own", 4)]:
             if d not in route[key]:
                 row += [0, NONE]
                 continue
             b = route[key][d][1]
-            u = d if key == ("A", 4) else user(d, b)
+            u = d if key == ("own", 4) else user(d, b)
             row += [b, NONE if u is None else OWN if u == d else MATE]
+        row += [d ^ m, OWN if user(d, d ^ m) == d else NONE]
         o = d // m
-        row += [0, NONE] if o < 2 else [d if o % 2 == 0 else d - 2 * m, MATE]
+        row += [d - m, OWN] if o % 2 == 0 and o > 0 else [0, NONE]
+        row += [x for b, q in straight if q == d for x in (b, OWN)] or [0, NONE]
         rows.append(row)
     return rows
 
@@ -172,28 +177,31 @@
     fetch_k.wait()
 
 
+def fetch_kernel(q_ref, here_ref, sem):
+    fetch = pltpu.make_async_copy(q_ref, here_ref, sem)
+    fetch.start()
+    fetch.wait()
+
+
+def fetched(queries):
+    return pl.pallas_call(
+        fetch_kernel,
+        out_shape=pltpu.VMEM(queries.shape, queries.dtype),
+        in_specs=[pl.BlockSpec(memory_space=pltpu.HBM)],
+        out_specs=pl.BlockSpec(memory_space=pltpu.VMEM),
+        scratch_shapes=[pltpu.SemaphoreType.DMA],
+        name="fetch_queries",
+    )(queries)
+
+
 def own_kernel(sizes, n_docs, info_ref, q_ref, kv_ref, *state):
     rows = sizes[2]
     base = info_ref[0] * rows
     bias = mask_bias(info_ref, n_docs, base, base, rows)
     attend_block(sizes, head_of(q_ref), kv_ref, bias, state, OWN, True)
-
-
-def back_kernel(sizes, n_docs, slot, info_ref, qm_ref, kv_ref, *refs):
-    kv_heads, group_size, rows = sizes
-    state = refs[3:]
-    live = info_ref[3 + 2 * slot] == MATE
-
-    @pl.when(live)
-    def _():
-        bias = mask_bias(info_ref, n_docs, info_ref[1] * rows, info_ref[2 + 2 * slot] * rows, rows)
-        attend_block(sizes, head_of(qm_ref), kv_ref, bias, state, MATE, True)
-
-    @pl.when(jnp.logical_not(live))
-    def _():
-        for g in range(kv_heads):
-            for ref, value in zip(state, (0.0, NEG, 0.0)):
-                ref[MATE, g] = jnp.full(ref.shape[2:], value, jnp.float32)
+    if state[0].shape[0] > 1:
+        for ref, value in zip(state, (0.0, NEG, 0.0)):
+            ref[MATE] = jnp.full(ref.shape[1:], value, jnp.float32)
 
 
 def add_block(sizes, n_docs, slot, info_ref, q_ref, qm_ref, kv_ref, state):
@@ -293,7 +301,7 @@
             out_specs=[vmem] * len(out),
             input_output_aliases={n_in + k: len(out) - 3 + k for k in range(len(held))} if keeps else {},
             compiler_params=pltpu.CompilerParams(vmem_limit_bytes=VMEM_LIMIT),
-            cost_estimate=pl.CostEstimate(flops=flops, bytes_accessed=1 << 20, transcendentals=0),
+            cost_estimate=pl.CostEstimate(flops=flops, bytes_accessed=1024, transcendentals=0),
             name=name,
         )(info, *arrays, *held)
         if not keeps:
@@ -304,9 +312,6 @@
     def own(q, kv):
         call(functools.partial(own_kernel, sizes, n_docs), [q, kv], [], "own_block")
 
-    def back(slot, qm, kv):
-        call(functools.partial(back_kernel, sizes, n_docs, slot), [qm, kv], [], "mate_first_block")
-
     def add(slot, q, qm, kv, flops=FLOPS):
         qs = [q] if qm is None else [q, qm]
         kernel = functools.partial(add_kernel, sizes, n_docs, slot, qm is not None)
@@ -324,7 +329,7 @@
         block, held[-1] = lax.optimization_barrier((block, held[-1]))
         return block
 
-    return own, back, add, part, merge, after
+    return own, add, part, merge, after
 
 
 def pack(keys, values, lengths, pack_order, table):
@@ -335,8 +340,8 @@
     return pl.pallas_call(
         functools.partial(pack_kernel, rows, n_docs, table is not None),
         out_shape=[
-            jax.ShapeDtypeStruct((rows, 2 * width), keys.dtype),
-            INFO_SPACE((STARTS + n_docs,), jnp.int32),
+            pltpu.VMEM((rows, 2 * width), keys.dtype),
+            pltpu.SMEM((STARTS + n_docs,), jnp.int32),
         ],
         in_specs=[hbm] * (len(scalars) + 2),
         out_specs=[pl.BlockSpec(memory_space=pltpu.VMEM), pl.BlockSpec(memory_space=pltpu.SMEM)],
@@ -355,37 +360,40 @@
     rows, kv_heads = queries.shape[0], keys.shape[1] // HD
     m = len(RING)
     sizes = (kv_heads, queries.shape[1] // keys.shape[1], rows)
-    route, user = make_plan(groups, FIRST // rows)
-    mate_of = [d if d < 2 * m else d ^ m for d in range(groups * m)]
-    table = jnp.array([[mate] + row for mate, row in zip(mate_of, block_table(route, user, groups))], jnp.int32)
+    route, user, straight = make_plan(groups, FIRST // rows)
+    table = jnp.array(block_table(route, user, straight, groups), jnp.int32)
     kv, info = pack(keys, values, lengths, pack_order, table)
-    own, back, add, part, merge, after = calls(sizes, lengths.shape[0], info, True)
+    own, add, part, merge, after = calls(sizes, lengths.shape[0], info, True)
 
     def send(block, op, step):
         return lax.ppermute(block, AXES, sorted((e, d) for d, (e, _) in route[op, step].items()))
 
-    mates = [(d, d ^ m) for d in range(2 * m, groups * m)]
-    eight_back = [(m + i, 3 * m + i) for i in range(m)] + [(2 * m + i, 2 * m + i) for i in range(m)]
-    a1 = send(kv, "A", 1)
-    q = queries
+    mates = [(d, d ^ m) for d in range(groups * m)]
+    eight_back = [(d - m, d) for o in range(2, groups, 2) for d in range(o * m, (o + 1) * m)]
+    u1 = send(kv, "own", 1)
+    kvm = lax.ppermute(kv, AXES, mates)
+    q = fetched(queries)
     own(q, kv)
-    b1 = send(kv, "B", 1)
-    qm = lax.ppermute(q, AXES, mates)
-    kv8 = lax.ppermute(kv, AXES, eight_back)
-    a2 = send(after(a1), "A", 2)
-    back(7, qm, kv8)
-    add(0, q, qm, a1)
-    b2 = send(after(b1), "B", 2)
-    add(1, q, qm, b1)
-    a3 = send(after(a2), "A", 3)
-    add(2, q, qm, a2)
-    b3 = send(after(b2), "B", 3)
-    add(3, q, qm, b2)
-    a4 = send(after(a3), "A", 4)
-    add(4, q, qm, a3)
-    mine = part(5, q, qm, b3)
+    w1 = send(after(kvm), "mate", 1)
+    qm = lax.ppermute(queries, AXES, mates)
+    kv1 = lax.ppermute(kv, AXES, straight)
+    u2 = send(after(u1), "own", 2)
+    add(7, q, None, kvm)
+    add(0, q, qm, u1)
+    w2 = send(after(w1), "mate", 2)
+    add(1, q, qm, w1)
+    add(9, q, None, kv1)
+    kv8 = lax.ppermute(after(kv), AXES, eight_back)
+    u3 = send(after(u2), "own", 3)
+    add(2, q, qm, u2)
+    w3 = send(after(w2), "mate", 3)
+    add(3, q, qm, w2)
+    add(8, q, None, kv8)
+    u4 = send(after(u3), "own", 4)
+    add(4, q, qm, u3)
+    mine = part(5, q, qm, w3)
     theirs = lax.ppermute(mine, AXES, mates)
-    add(6, q, None, a4, LAST_FLOPS)
+    add(6, q, None, u4, LAST_FLOPS)
     return merge([theirs])
 
 
@@ -394,7 +402,7 @@
     sizes = (kv_heads, queries.shape[1] // keys.shape[1], rows)
     n = lax.axis_size(AXES)
     kv, info = pack(keys, values, lengths, pack_order, None)
-    own, back, add, part, merge, after = calls(sizes, lengths.shape[0], info, False)
+    own, add, part, merge, after = calls(sizes, lengths.shape[0], info, False)
     q = queries
     own(q, kv)
     for hop in range(HOPS):

time: 64.4 us -> 54.9 us (0.85)
  the two profiles are of different devices: /device:TPU:26 before, /device:TPU:22 now
where the time goes in v3:
time: 54.9 us; the launch traced here: 53.9 us
  waiting for transfers between devices  26.5 us (48%)
  starting transfers between devices  19.6 us (36%)
  Pallas kernels  7.58 us (14%)
    ppermute x7, waiting for transfers between devices, send(): lax.ppermute(block, AXES, sorted(((e, d) for d, (e, _) in route[op, step]...  26.5 us
    ppermute x7, starting transfers between devices, send(): lax.ppermute(block, AXES, sorted(((e, d) for d, (e, _) in route[op, step]...  17 us
    pallas_call x12, Pallas kernels, call(): pl.pallas_call(kernel, out_shape=out, in_specs=[smem] + [vmem] * (len(arr...  5.22 us
    ppermute x1, starting transfers between devices, ring_shards(): kv8 = lax.ppermute(after(kv), AXES, eight_back)  1.29 us
    pallas_call x1, Pallas kernels, fetched(): pl.pallas_call(fetch_kernel, out_shape=pltpu.VMEM(queries.shape, queries....  1.24 us
    pallas_call x1, Pallas kernels, pack(): pl.pallas_call(functools.partial(pack_kernel, rows, n_docs, table is not...  1.12 us
  transfers between devices with their start and end apart: 12, of which 7 were waited for; matrix products, arithmetic and copies ran while one was open for 0% of the time, Pallas kernels for 9%

profile of v3, /device:TPU:22, one launch (start us, length us, event | category | flops | bytes accessed | tf_op | source)
XLA Modules:
  0.0 53.9 jit_solution(7741877810740800857)
XLA Ops:
  0.0 1.1 %pack_keys_values.1 = (bf16[128,2048]{1,0:T(8,128)(2,1)S(1)}, s32[30]{0:T(128)S(4)}) custom-call(s32[8]{0:T(128)} %refs_0_.1, s32[8]{0:T(128)} %refs_1_.1, s32[32,21]{1,0:T(8,128)} %constant.2.clone.refs_2_, bf16[128,1024]{1,0:T(8,128)(2,1)} %refs_3_.1, bf16[128,1024]{1,0:T(8,128)(2,1)} %refs_4_.1), custom_call_target="tpu_custom_call" | custom-call | tf_op jit(solution)/shard_map/pack_keys_values/pallas_call | solution.py:340
  1.2 0.5 collective-permute-start
  1.7 3.5 %collective-permute-start.3 = (bf16[128,2048]{1,0:T(8,128)(2,1)S(1)}, bf16[128,2048]{1,0:T(8,128)(2,1)}, u32[]{:S(2)}, u32[]{:S(2)}) collective-permute-start(bf16[128,2048]{1,0:T(8,128)(2,1)S(1)} %get-tuple-element.83.kv_ref), channel_id=1, source_target_pairs={{0,1},{1,3},{2,0},{3,5},{5,7},{8,10},{9,8},{10,12},{11,25},{12,14}... | collective-permute-start | bytes 1572872 | tf_op jit(solution)/shard_map/ppermute | solution.py:369
  5.2 1.2 %fetch_queries.1.q_ref = bf16[128,4096]{1,0:T(8,128)(2,1)S(1)} custom-call(bf16[128,4096]{1,0:T(8,128)(2,1)} %q_ref.1), custom_call_target="tpu_custom_call" | custom-call | tf_op jit(solution)/shard_map/fetch_queries/pallas_call | solution.py:187
  6.4 1.1 %own_block.1 = (f32[2,8,128,512]{3,2,1,0:T(8,128)S(1)}, f32[2,8,1,512]{3,2,1,0:T(1,128)S(1)}, f32[2,8,1,512]{3,2,1,0:T(1,128)S(1)}) custom-call(s32[30]{0:T(128)S(4)} %get-tuple-element.55.info_ref, bf16[128,4096]{1,0:T(8,128)(2,1)S(1)} %fetch_queries.1.q_ref, bf16[128,2048]{1,0:T(8,128)(2,1)S(1)} %get-tuple-element.83.kv_ref), custom_call_target="tpu_custom_call" | custom-call | flops 1000 | bytes 1024 | tf_op jit(solution)/shard_map/own_block/pallas_call | solution.py:297
  7.5 2.4 %collective-permute-start.2 = (bf16[128,2048]{1,0:T(8,128)(2,1)S(1)}, bf16[128,2048]{1,0:T(8,128)(2,1)S(1)}, u32[]{:S(2)}, u32[]{:S(2)}) collective-permute-start(bf16[128,2048]{1,0:T(8,128)(2,1)S(1)} %collective-permute-done.1.refs_0_), channel_id=1, source_target_pairs={{0,1},{1,3},{2,16},{3,5},{4,18},{5,7},{6,20},{7,22},{8,10},{9,8},{... | collective-permute-start | bytes 1572872 | tf_op jit(solution)/shard_map/ppermute | solution.py:369
  10.0 0.7 %collective-permute-start.6 = (bf16[128,2048]{1,0:T(8,128)(2,1)S(1)}, bf16[128,2048]{1,0:T(8,128)(2,1)S(1)}, u32[]{:S(2)}, u32[]{:S(2)}) collective-permute-start(bf16[128,2048]{1,0:T(8,128)(2,1)S(1)} %get-tuple-element.83.kv_ref), channel_id=1, source_target_pairs={{26,27},{27,28},{9,16}} | collective-permute-start | bytes 1572872 | tf_op jit(solution)/shard_map/ppermute | solution.py:379
  10.7 2.2 %collective-permute-done.3.refs_1_ = bf16[128,2048]{1,0:T(8,128)(2,1)} collective-permute-done((bf16[128,2048]{1,0:T(8,128)(2,1)S(1)}, bf16[128,2048]{1,0:T(8,128)(2,1)}, u32[]{:S(2)}, u32[]{:S(2)}) %collective-permute-start.3) | collective-permute-done | bytes 524320 | tf_op jit(solution)/shard_map/ppermute | solution.py:369
  12.9 3.5 %collective-permute-start.5 = (bf16[128,2048]{1,0:T(8,128)(2,1)}, bf16[128,2048]{1,0:T(8,128)(2,1)S(1)}, u32[]{:S(2)}, u32[]{:S(2)}) collective-permute-start(bf16[128,2048]{1,0:T(8,128)(2,1)} %collective-permute-done.3.refs_1_), channel_id=1, source_target_pairs={{0,1},{1,3},{3,5},{5,7},{7,6},{8,10},{10,12},{12,14},{14,15},{15,2... | collective-permute-start | bytes 1572872 | tf_op jit(solution)/shard_map/ppermute | solution.py:369
  16.4 2.3 %add_block.10 = (f32[2,8,128,512]{3,2,1,0:T(8,128)S(1)}, f32[2,8,1,512]{3,2,1,0:T(1,128)S(1)}, f32[2,8,1,512]{3,2,1,0:T(1,128)S(1)}) custom-call(s32[30]{0:T(128)S(4)} %get-tuple-element.55.info_ref, bf16[128,4096]{1,0:T(8,128)(2,1)S(1)} %fetch_queries.1.q_ref, ...), custom_call_target="tpu_custom_call", output_to_operand_aliasing={{0}: (4, {}), {1}: (5, {}), {2}: (6, {})} | custom-call | flops 1000 | bytes 1024 | tf_op jit(solution)/shard_map/add_block/pallas_call | solution.py:297
  18.7 3.5 %collective-permute-done.2.refs_1_ = bf16[128,2048]{1,0:T(8,128)(2,1)S(1)} collective-permute-done((bf16[128,2048]{1,0:T(8,128)(2,1)S(1)}, bf16[128,2048]{1,0:T(8,128)(2,1)S(1)}, u32[]{:S(2)}, u32[]{:S(2)}) %collective-permute-start.2) | collective-permute-done | bytes 524320 | tf_op jit(solution)/shard_map/ppermute | solution.py:369
  22.2 1.9 %collective-permute-start.4 = (bf16[128,2048]{1,0:T(8,128)(2,1)S(1)}, bf16[128,2048]{1,0:T(8,128)(2,1)S(1)}, u32[]{:S(2)}, u32[]{:S(2)}) collective-permute-start(bf16[128,2048]{1,0:T(8,128)(2,1)S(1)} %collective-permute-done.2.refs_1_), channel_id=1, source_target_pairs={{1,3},{3,5},{5,7},{7,6},{8,10},{10,12},{12,14},{14,15},{16,17},{17... | collective-permute-start | bytes 1572872 | tf_op jit(solution)/shard_map/ppermute | solution.py:369
  24.2 1.3 %collective-permute-start.9 = (bf16[128,2048]{1,0:T(8,128)(2,1)S(1)}, bf16[128,2048]{1,0:T(8,128)(2,1)S(1)}, u32[]{:S(2)}, u32[]{:S(2)}) collective-permute-start(bf16[128,2048]{1,0:T(8,128)(2,1)S(1)} %get-tuple-element.83.kv_ref), channel_id=1, source_target_pairs={{8,16},{9,17},{10,18},{11,19},{12,20},{13,21},{14,22},{15,23}} | collective-permute-start | bytes 1572872 | tf_op jit(solution)/shard_map/ppermute | solution.py:386
  25.5 4.3 %collective-permute-done.5.refs_1_ = bf16[128,2048]{1,0:T(8,128)(2,1)S(1)} collective-permute-done((bf16[128,2048]{1,0:T(8,128)(2,1)}, bf16[128,2048]{1,0:T(8,128)(2,1)S(1)}, u32[]{:S(2)}, u32[]{:S(2)}) %collective-permute-start.5) | collective-permute-done | bytes 524320 | tf_op jit(solution)/shard_map/ppermute | solution.py:369
  29.9 1.9 %collective-permute-start.8 = (bf16[128,2048]{1,0:T(8,128)(2,1)S(1)}, bf16[128,2048]{1,0:T(8,128)(2,1)S(1)}, u32[]{:S(2)}, u32[]{:S(2)}) collective-permute-start(bf16[128,2048]{1,0:T(8,128)(2,1)S(1)} %collective-permute-done.5.refs_1_), channel_id=1, source_target_pairs={{1,3},{3,5},{5,7},{7,6},{10,12},{12,14},{14,15},{15,13},{16,17},{1... | collective-permute-start | bytes 1572872 | tf_op jit(solution)/shard_map/ppermute | solution.py:369
  31.8 3.7 %collective-permute-done.4.refs_1_ = bf16[128,2048]{1,0:T(8,128)(2,1)S(1)} collective-permute-done((bf16[128,2048]{1,0:T(8,128)(2,1)S(1)}, bf16[128,2048]{1,0:T(8,128)(2,1)S(1)}, u32[]{:S(2)}, u32[]{:S(2)}) %collective-permute-start.4) | collective-permute-done | bytes 524320 | tf_op jit(solution)/shard_map/ppermute | solution.py:369
  35.5 1.9 %collective-permute-start.7 = (bf16[128,2048]{1,0:T(8,128)(2,1)S(1)}, bf16[128,2048]{1,0:T(8,128)(2,1)S(1)}, u32[]{:S(2)}, u32[]{:S(2)}) collective-permute-start(bf16[128,2048]{1,0:T(8,128)(2,1)S(1)} %collective-permute-done.4.refs_1_), channel_id=1, source_target_pairs={{3,5},{5,7},{6,20},{7,6},{10,12},{12,14},{14,15},{15,13},{16,17},{... | collective-permute-start | bytes 1572872 | tf_op jit(solution)/shard_map/ppermute | solution.py:369
  37.4 3.6 %collective-permute-done.8.refs_1_ = bf16[128,2048]{1,0:T(8,128)(2,1)S(1)} collective-permute-done((bf16[128,2048]{1,0:T(8,128)(2,1)S(1)}, bf16[128,2048]{1,0:T(8,128)(2,1)S(1)}, u32[]{:S(2)}, u32[]{:S(2)}) %collective-permute-start.8) | collective-permute-done | bytes 524320 | tf_op jit(solution)/shard_map/ppermute | solution.py:369
  41.1 1.9 %collective-permute-start.11 = (bf16[128,2048]{1,0:T(8,128)(2,1)S(1)}, bf16[128,2048]{1,0:T(8,128)(2,1)S(1)}, u32[]{:S(2)}, u32[]{:S(2)}) collective-permute-start(bf16[128,2048]{1,0:T(8,128)(2,1)S(1)} %collective-permute-done.8.refs_1_), channel_id=1, source_target_pairs={{3,5},{5,7},{6,4},{7,6},{12,14},{13,19},{14,15},{15,13},{16,25},{1... | collective-permute-start | bytes 1572872 | tf_op jit(solution)/shard_map/ppermute | solution.py:369
  43.0 3.7 %collective-permute-done.7.kv_ref = bf16[128,2048]{1,0:T(8,128)(2,1)S(1)} collective-permute-done((bf16[128,2048]{1,0:T(8,128)(2,1)S(1)}, bf16[128,2048]{1,0:T(8,128)(2,1)S(1)}, u32[]{:S(2)}, u32[]{:S(2)}) %collective-permute-start.7) | collective-permute-done | bytes 524320 | tf_op jit(solution)/shard_map/ppermute | solution.py:369
  46.7 0.1 mate_part.1
  46.9 0.1 collective-permute-start.10
  46.9 5.4 %collective-permute-done.11.refs_0_ = bf16[128,2048]{1,0:T(8,128)(2,1)S(1)} collective-permute-done((bf16[128,2048]{1,0:T(8,128)(2,1)S(1)}, bf16[128,2048]{1,0:T(8,128)(2,1)S(1)}, u32[]{:S(2)}, u32[]{:S(2)}) %collective-permute-start.11) | collective-permute-done | bytes 524320 | tf_op jit(solution)/shard_map/ppermute | solution.py:369
  52.3 1.6 %merge.1 = bf16[128,4096]{1,0:T(8,128)(2,1)} custom-call(s32[30]{0:T(128)S(4)} %get-tuple-element.55.info_ref, bf16[128,4352]{1,0:T(8,128)(2,1)S(1)} %collective-permute-done.10.refs_0_, f32[2,8,128,512]{3,2,1,0:T(8,128)S(1)} %get-tuple-element.102.refs_1_, f32[2,8,1,512]{3,2,1,0:T(1,128)S(1)} %get-tuple-element.103.refs_2_, ...), custom_call_target="tpu_custom_call" | custom-call | flops 1000 | bytes 1024 | tf_op jit(solution)/shard_map/merge/pallas_call | solution.py:297
  (14 shorter events, 0.2 us)
Async XLA Ops:
  1.1 6.4 %collective-permute-start.1 = (bf16[128,2048]{1,0:T(8,128)(2,1)S(1)}, bf16[128,2048]{1,0:T(8,128)(2,1)S(1)}, u32[]{:S(2)}, u32[]{:S(2)}) collective-permute-start(bf16[128,2048]{1,0:T(8,128)(2,1)S(1)} %get-tuple-element.83.kv_ref), channel_id=1, source_target_pairs={{0,8},{1,9},{2,10},{3,11},{4,12},{5,13},{6,14},{7,15},{8,0},{9,1},... | collective-permute-start | bytes 1572872 | tf_op jit(solution)/shard_map/ppermute | solution.py:374
  1.2 15.2 %collective-permute-start = (bf16[128,4096]{1,0:T(8,128)(2,1)}, bf16[128,4096]{1,0:T(8,128)(2,1)S(1)}, u32[]{:S(2)}, u32[]{:S(2)}) collective-permute-start(bf16[128,4096]{1,0:T(8,128)(2,1)} %q_ref.1), channel_id=1, source_target_pairs={{0,8},{1,9},{2,10},{3,11},{4,12},{5,13},{6,14},{7,15},{8,0},{9,1},... | collective-permute-start | bytes 3145736 | tf_op jit(solution)/shard_map/ppermute | solution.py:378
  1.7 11.2 %collective-permute-start.3 = (bf16[128,2048]{1,0:T(8,128)(2,1)S(1)}, bf16[128,2048]{1,0:T(8,128)(2,1)}, u32[]{:S(2)}, u32[]{:S(2)}) collective-permute-start(bf16[128,2048]{1,0:T(8,128)(2,1)S(1)} %get-tuple-element.83.kv_ref), channel_id=1, source_target_pairs={{0,1},{1,3},{2,0},{3,5},{5,7},{8,10},{9,8},{10,12},{11,25},{12,14}... | collective-permute-start | bytes 1572872 | tf_op jit(solution)/shard_map/ppermute | solution.py:369
  7.5 14.7 %collective-permute-start.2 = (bf16[128,2048]{1,0:T(8,128)(2,1)S(1)}, bf16[128,2048]{1,0:T(8,128)(2,1)S(1)}, u32[]{:S(2)}, u32[]{:S(2)}) collective-permute-start(bf16[128,2048]{1,0:T(8,128)(2,1)S(1)} %collective-permute-done.1.refs_0_), channel_id=1, source_target_pairs={{0,1},{1,3},{2,16},{3,5},{4,18},{5,7},{6,20},{7,22},{8,10},{9,8},{... | collective-permute-start | bytes 1572872 | tf_op jit(solution)/shard_map/ppermute | solution.py:369
  10.0 14.2 %collective-permute-start.6 = (bf16[128,2048]{1,0:T(8,128)(2,1)S(1)}, bf16[128,2048]{1,0:T(8,128)(2,1)S(1)}, u32[]{:S(2)}, u32[]{:S(2)}) collective-permute-start(bf16[128,2048]{1,0:T(8,128)(2,1)S(1)} %get-tuple-element.83.kv_ref), channel_id=1, source_target_pairs={{26,27},{27,28},{9,16}} | collective-permute-start | bytes 1572872 | tf_op jit(solution)/shard_map/ppermute | solution.py:379
  12.9 17.0 %collective-permute-start.5 = (bf16[128,2048]{1,0:T(8,128)(2,1)}, bf16[128,2048]{1,0:T(8,128)(2,1)S(1)}, u32[]{:S(2)}, u32[]{:S(2)}) collective-permute-start(bf16[128,2048]{1,0:T(8,128)(2,1)} %collective-permute-done.3.refs_1_), channel_id=1, source_target_pairs={{0,1},{1,3},{3,5},{5,7},{7,6},{8,10},{10,12},{12,14},{14,15},{15,2... | collective-permute-start | bytes 1572872 | tf_op jit(solution)/shard_map/ppermute | solution.py:369
  22.2 13.2 %collective-permute-start.4 = (bf16[128,2048]{1,0:T(8,128)(2,1)S(1)}, bf16[128,2048]{1,0:T(8,128)(2,1)S(1)}, u32[]{:S(2)}, u32[]{:S(2)}) collective-permute-start(bf16[128,2048]{1,0:T(8,128)(2,1)S(1)} %collective-permute-done.2.refs_1_), channel_id=1, source_target_pairs={{1,3},{3,5},{5,7},{7,6},{8,10},{10,12},{12,14},{14,15},{16,17},{17... | collective-permute-start | bytes 1572872 | tf_op jit(solution)/shard_map/ppermute | solution.py:369
  24.2 13.2 %collective-permute-start.9 = (bf16[128,2048]{1,0:T(8,128)(2,1)S(1)}, bf16[128,2048]{1,0:T(8,128)(2,1)S(1)}, u32[]{:S(2)}, u32[]{:S(2)}) collective-permute-start(bf16[128,2048]{1,0:T(8,128)(2,1)S(1)} %get-tuple-element.83.kv_ref), channel_id=1, source_target_pairs={{8,16},{9,17},{10,18},{11,19},{12,20},{13,21},{14,22},{15,23}} | collective-permute-start | bytes 1572872 | tf_op jit(solution)/shard_map/ppermute | solution.py:386
  29.9 11.2 %collective-permute-start.8 = (bf16[128,2048]{1,0:T(8,128)(2,1)S(1)}, bf16[128,2048]{1,0:T(8,128)(2,1)S(1)}, u32[]{:S(2)}, u32[]{:S(2)}) collective-permute-start(bf16[128,2048]{1,0:T(8,128)(2,1)S(1)} %collective-permute-done.5.refs_1_), channel_id=1, source_target_pairs={{1,3},{3,5},{5,7},{7,6},{10,12},{12,14},{14,15},{15,13},{16,17},{1... | collective-permute-start | bytes 1572872 | tf_op jit(solution)/shard_map/ppermute | solution.py:369
  35.5 11.2 %collective-permute-start.7 = (bf16[128,2048]{1,0:T(8,128)(2,1)S(1)}, bf16[128,2048]{1,0:T(8,128)(2,1)S(1)}, u32[]{:S(2)}, u32[]{:S(2)}) collective-permute-start(bf16[128,2048]{1,0:T(8,128)(2,1)S(1)} %collective-permute-done.4.refs_1_), channel_id=1, source_target_pairs={{3,5},{5,7},{6,20},{7,6},{10,12},{12,14},{14,15},{15,13},{16,17},{... | collective-permute-start | bytes 1572872 | tf_op jit(solution)/shard_map/ppermute | solution.py:369
  41.1 11.2 %collective-permute-start.11 = (bf16[128,2048]{1,0:T(8,128)(2,1)S(1)}, bf16[128,2048]{1,0:T(8,128)(2,1)S(1)}, u32[]{:S(2)}, u32[]{:S(2)}) collective-permute-start(bf16[128,2048]{1,0:T(8,128)(2,1)S(1)} %collective-permute-done.8.refs_1_), channel_id=1, source_target_pairs={{3,5},{5,7},{6,4},{7,6},{12,14},{13,19},{14,15},{15,13},{16,25},{1... | collective-permute-start | bytes 1572872 | tf_op jit(solution)/shard_map/ppermute | solution.py:369
  46.9 5.5 %collective-permute-start.10 = (bf16[128,4352]{1,0:T(8,128)(2,1)S(1)}, bf16[128,4352]{1,0:T(8,128)(2,1)S(1)}, u32[]{:S(2)}, u32[]{:S(2)}) collective-permute-start(bf16[128,4352]{1,0:T(8,128)(2,1)S(1)} %get-tuple-element.97), channel_id=1, source_target_pairs={{0,8},{1,9},{2,10},{3,11},{4,12},{5,13},{6,14},{7,15},{8,0},{9,1},... | collective-permute-start | bytes 3342344 | tf_op jit(solution)/shard_map/ppermute | solution.py:395

commit v4 on v3

--- a/solution.py
+++ b/solution.py
@@ -17,7 +17,7 @@
 RING = (0, 2, 4, 6, 7, 5, 3, 1)
 OWN, MATE, NONE = 0, 1, 2
 VMEM_LIMIT = 40 * 1024 * 1024
-SLOTS = 10
+SLOTS = 12
 STARTS = 2 + 2 * SLOTS
 FLOPS = 1000
 LAST_FLOPS = 50_000_000_000
@@ -35,10 +35,15 @@
             o = (o + 2) % groups
         return o * m + j
 
-    straight = [(n - m + 2, n - m + 3), (n - m + 3, n - m + 4), (n - 3 * m + 1, n - 2 * m)]
+    last = n - m
+    straight = [
+        (last + 2, last + 3, last + 2),
+        (last + 3, last + 4, last - m + 5),
+        (last - 2 * m + 1, last - m, last - 2 * m),
+    ]
 
     def uses(q, b):
-        return 0 < q - b <= HOPS and not (b < first_blocks <= q) and (b, q) not in straight
+        return 0 < q - b <= HOPS and not (b < first_blocks <= q) and (b, q) not in [x[:2] for x in straight]
 
     def user(d, b):
         return d if uses(d, b) else d ^ m if uses(d ^ m, b) else None
@@ -81,7 +86,8 @@
         row += [d ^ m, OWN if user(d, d ^ m) == d else NONE]
         o = d // m
         row += [d - m, OWN] if o % 2 == 0 and o > 0 else [0, NONE]
-        row += [x for b, q in straight if q == d for x in (b, OWN)] or [0, NONE]
+        for b, q, _ in straight:
+            row += [b, OWN] if q == d else [0, NONE]
         rows.append(row)
     return rows
 
@@ -91,7 +97,7 @@
     return lax.axis_index(outer) * lax.axis_size(inner) + lax.axis_index(inner)
 
 
-def attend_block(sizes, q_of, kv_ref, bias, state, u, fresh):
+def attend_block(sizes, q_of, kv_ref, bias, state, u, fresh, finish=None):
     kv_heads, group_size, _ = sizes
     acc_ref, max_ref, sum_ref = state
     tile = 2 if group_size % 2 == 0 else 1
@@ -115,6 +121,8 @@
             max_ref[u, g, :, columns] = top
             sum_ref[u, g, :, columns] = total if fresh else sum_ref[u, g, :, columns] * fade + total
             acc_ref[u, g, :, columns] = mixed if fresh else acc_ref[u, g, :, columns] * fade + mixed
+        if finish is not None:
+            finish(g)
 
 
 def head_of(ref):
@@ -252,19 +260,27 @@
             part_ref[k * heads : (k + 1) * heads, place : place + HD] = piece
 
 
-def merge_kernel(sizes, mated, info_ref, *refs):
+def touch_kernel(info_ref, kv_ref, *refs):
+    pass
+
+
+def last_kernel(sizes, n_docs, slot, mated, info_ref, q_ref, *refs):
     kv_heads, group_size, rows = sizes
     heads = kv_heads * group_size
+    width = group_size * HD
     part_ref, refs = (refs[0], refs[1:]) if mated else (None, refs)
-    acc_ref, max_ref, sum_ref, out_ref = refs
+    kv_ref, acc_ref, max_ref, sum_ref, out_ref, out_here, sems = refs
     if mated:
         tops, sums = (
             sum(part_ref[k * heads : (k + 1) * heads, c * HD : (c + 1) * HD].astype(jnp.float32) for k in range(3))
             for c in (heads, heads + 1)
         )
-        met = info_ref[1] != info_ref[0]
-        tops, sums = jnp.where(met, tops, NEG), jnp.where(met, sums, 0.0)
-    for g in range(kv_heads):
+
+    def store(g):
+        columns = pl.ds(g * width, width)
+        return pltpu.make_async_copy(out_here.at[:, columns], out_ref.at[:, columns], sems.at[g])
+
+    def finish(g):
         for j in range(group_size):
             h, mine = g * group_size + j, slice(j * HD, (j + 1) * HD)
             numer, top, total = acc_ref[OWN, g, :, mine], max_ref[OWN, g, :, mine], sum_ref[OWN, g, :, mine]
@@ -272,11 +288,27 @@
                 both = jnp.maximum(top, tops[h : h + 1])
                 weight, other = jnp.exp2(top - both), jnp.exp2(tops[h : h + 1] - both) * sums[h : h + 1]
                 share = 1.0 / (total * weight + other)
-                theirs = jnp.where(met, part_ref[:, h * HD : (h + 1) * HD].astype(jnp.float32), 0.0)
+                theirs = part_ref[:, h * HD : (h + 1) * HD].astype(jnp.float32)
                 out = numer * (weight * share) + theirs * (other * share)
             else:
                 out = numer * (1.0 / total)
-            out_ref[:, h * HD : (h + 1) * HD] = out.astype(jnp.bfloat16).T
+            out_here[:, h * HD : (h + 1) * HD] = out.astype(jnp.bfloat16).T
+        store(g).start()
+
+    use = info_ref[3 + 2 * slot]
+
+    @pl.when(use != NONE)
+    def _():
+        bias = mask_bias(info_ref, n_docs, info_ref[0] * rows, info_ref[2 + 2 * slot] * rows, rows)
+        attend_block(sizes, head_of(q_ref), kv_ref, bias, (acc_ref, max_ref, sum_ref), OWN, False, finish)
+
+    @pl.when(use == NONE)
+    def _():
+        for g in range(kv_heads):
+            finish(g)
+
+    for g in range(kv_heads):
+        store(g).wait()
 
 
 def calls(sizes, n_docs, info, mated):
@@ -312,24 +344,37 @@
     def own(q, kv):
         call(functools.partial(own_kernel, sizes, n_docs), [q, kv], [], "own_block")
 
-    def add(slot, q, qm, kv, flops=FLOPS):
+    def add(slot, q, qm, kv):
         qs = [q] if qm is None else [q, qm]
         kernel = functools.partial(add_kernel, sizes, n_docs, slot, qm is not None)
-        call(kernel, qs + [kv], [], "add_block", flops=flops)
+        call(kernel, qs + [kv], [], "add_block")
 
     def part(slot, q, qm, kv):
         out = jax.ShapeDtypeStruct((rows, (kv_heads * group_size + 2) * HD), jnp.bfloat16)
         return call(functools.partial(part_kernel, sizes, n_docs, slot), [q, qm, kv], [out], "mate_part")[0]
 
-    def merge(parts):
-        out = jax.ShapeDtypeStruct((rows, kv_heads * group_size * HD), jnp.bfloat16)
-        return call(functools.partial(merge_kernel, sizes, mated), parts, [out], "merge", keeps=False)[0]
+    def touch(kv):
+        call(touch_kernel, [kv], [], "last_block_here", flops=LAST_FLOPS)
+
+    def last(slot, q, parts, kv):
+        return pl.pallas_call(
+            functools.partial(last_kernel, sizes, n_docs, slot, mated),
+            out_shape=jax.ShapeDtypeStruct((rows, kv_heads * group_size * HD), jnp.bfloat16),
+            in_specs=[smem] + [vmem] * (2 + len(parts) + len(held)),
+            out_specs=pl.BlockSpec(memory_space=pltpu.HBM),
+            scratch_shapes=[
+                pltpu.VMEM((rows, kv_heads * group_size * HD), jnp.bfloat16),
+                pltpu.SemaphoreType.DMA((kv_heads,)),
+            ],
+            compiler_params=pltpu.CompilerParams(vmem_limit_bytes=VMEM_LIMIT),
+            name="last_block",
+        )(info, q, *parts, kv, *held)
 
     def after(block):
         block, held[-1] = lax.optimization_barrier((block, held[-1]))
         return block
 
-    return own, add, part, merge, after
+    return own, add, part, touch, last, after
 
 
 def pack(keys, values, lengths, pack_order, table):
@@ -363,7 +408,7 @@
     route, user, straight = make_plan(groups, FIRST // rows)
     table = jnp.array(block_table(route, user, straight, groups), jnp.int32)
     kv, info = pack(keys, values, lengths, pack_order, table)
-    own, add, part, merge, after = calls(sizes, lengths.shape[0], info, True)
+    own, add, part, touch, last, after = calls(sizes, lengths.shape[0], info, True)
 
     def send(block, op, step):
         return lax.ppermute(block, AXES, sorted((e, d) for d, (e, _) in route[op, step].items()))
@@ -376,25 +421,29 @@
     own(q, kv)
     w1 = send(after(kvm), "mate", 1)
     qm = lax.ppermute(queries, AXES, mates)
-    kv1 = lax.ppermute(kv, AXES, straight)
+    beside = [[(e, q)] for _, q, e in straight]
+    near = [lax.ppermute(kv, AXES, beside[0])]
     u2 = send(after(u1), "own", 2)
     add(7, q, None, kvm)
     add(0, q, qm, u1)
     w2 = send(after(w1), "mate", 2)
     add(1, q, qm, w1)
-    add(9, q, None, kv1)
+    add(9, q, None, near[0])
+    near += [lax.ppermute(after(w1), AXES, beside[1]), lax.ppermute(u1, AXES, beside[2])]
     kv8 = lax.ppermute(after(kv), AXES, eight_back)
     u3 = send(after(u2), "own", 3)
     add(2, q, qm, u2)
     w3 = send(after(w2), "mate", 3)
     add(3, q, qm, w2)
-    add(8, q, None, kv8)
     u4 = send(after(u3), "own", 4)
     add(4, q, qm, u3)
+    add(10, q, None, near[1])
+    add(11, q, None, near[2])
     mine = part(5, q, qm, w3)
     theirs = lax.ppermute(mine, AXES, mates)
-    add(6, q, None, u4, LAST_FLOPS)
-    return merge([theirs])
+    add(8, q, None, kv8)
+    touch(u4)
+    return last(6, q, [theirs], u4)
 
 
 def chain_shards(queries, keys, values, lengths, pack_order):
@@ -402,13 +451,14 @@
     sizes = (kv_heads, queries.shape[1] // keys.shape[1], rows)
     n = lax.axis_size(AXES)
     kv, info = pack(keys, values, lengths, pack_order, None)
-    own, add, part, merge, after = calls(sizes, lengths.shape[0], info, False)
+    own, add, part, touch, last, after = calls(sizes, lengths.shape[0], info, False)
     q = queries
     own(q, kv)
     for hop in range(HOPS):
         kv = lax.ppermute(kv, AXES, [(d, d + 1) for d in range(n - 1)])
-        add(hop, q, None, kv)
-    return merge([])
+        if hop < HOPS - 1:
+            add(hop, q, None, kv)
+    return last(HOPS - 1, q, [], kv)
 
 
 def solution(mesh):

time: 54.9 us -> 51.4 us (0.936)
  the two profiles are of different devices: /device:TPU:22 before, /device:TPU:14 now
where the time goes in v4:
time: 51.4 us; the launch traced here: 51 us
  starting transfers between devices  28.5 us (55%)
  waiting for transfers between devices  13.3 us (26%)
  Pallas kernels  8.79 us (17%)
    ppermute x7, starting transfers between devices, send(): lax.ppermute(block, AXES, sorted(((e, d) for d, (e, _) in route[op, step]...  24.4 us
    ppermute x1, waiting for transfers between devices, ring_shards(): kv8 = lax.ppermute(after(kv), AXES, eight_back)  8.75 us
    pallas_call x13, Pallas kernels, call(): pl.pallas_call(kernel, out_shape=out, in_specs=[smem] + [vmem] * (len(arr...  5.12 us
    ppermute x7, waiting for transfers between devices, send(): lax.ppermute(block, AXES, sorted(((e, d) for d, (e, _) in route[op, step]...  4.54 us
    pallas_call x1, Pallas kernels, last(): pl.pallas_call(functools.partial(last_kernel, sizes, n_docs, slot, mated)...  1.31 us
    ppermute x1, starting transfers between devices, ring_shards(): kv8 = lax.ppermute(after(kv), AXES, eight_back)  1.29 us
    pallas_call x1, Pallas kernels, fetched(): pl.pallas_call(fetch_kernel, out_shape=pltpu.VMEM(queries.shape, queries....  1.24 us
    pallas_call x1, Pallas kernels, pack(): pl.pallas_call(functools.partial(pack_kernel, rows, n_docs, table is not...  1.12 us
  transfers between devices with their start and end apart: 14, of which 6 were waited for; matrix products, arithmetic and copies ran while one was open for 0% of the time, Pallas kernels for 12%

profile of v4, /device:TPU:14, one launch (start us, length us, event | category | flops | bytes accessed | tf_op | source)
XLA Modules:
  0.0 51.0 jit_solution(10026690594209856421)
XLA Ops:
  0.0 1.1 %pack_keys_values.1 = (bf16[128,2048]{1,0:T(8,128)(2,1)S(1)}, s32[34]{0:T(128)S(4)}) custom-call(s32[8]{0:T(128)} %refs_0_.1, s32[8]{0:T(128)} %refs_1_.1, s32[32,25]{1,0:T(8,128)} %constant.2.clone.refs_2_, bf16[128,1024]{1,0:T(8,128)(2,1)} %refs_3_.1, bf16[128,1024]{1,0:T(8,128)(2,1)} %refs_4_.1), custom_call_target="tpu_custom_call" | custom-call | tf_op jit(solution)/shard_map/pack_keys_values/pallas_call | solution.py:385
  1.7 3.5 %collective-permute-start.3 = (bf16[128,2048]{1,0:T(8,128)(2,1)S(1)}, bf16[128,2048]{1,0:T(8,128)(2,1)}, u32[]{:S(2)}, u32[]{:S(2)}) collective-permute-start(bf16[128,2048]{1,0:T(8,128)(2,1)S(1)} %get-tuple-element.111.kv_ref), channel_id=1, source_target_pairs={{0,1},{1,3},{2,0},{3,5},{5,7},{8,10},{9,8},{10,12},{11,25},{12,14}... | collective-permute-start | bytes 1572872 | tf_op jit(solution)/shard_map/ppermute | solution.py:414
  5.2 1.2 %fetch_queries.1.q_ref = bf16[128,4096]{1,0:T(8,128)(2,1)S(1)} custom-call(bf16[128,4096]{1,0:T(8,128)(2,1)} %q_ref.1), custom_call_target="tpu_custom_call" | custom-call | tf_op jit(solution)/shard_map/fetch_queries/pallas_call | solution.py:195
  6.4 1.1 %own_block.1 = (f32[2,8,128,512]{3,2,1,0:T(8,128)S(1)}, f32[2,8,1,512]{3,2,1,0:T(1,128)S(1)}, f32[2,8,1,512]{3,2,1,0:T(1,128)S(1)}) custom-call(s32[34]{0:T(128)S(4)} %get-tuple-element.63.info_ref, bf16[128,4096]{1,0:T(8,128)(2,1)S(1)} %fetch_queries.1.q_ref, bf16[128,2048]{1,0:T(8,128)(2,1)S(1)} %get-tuple-element.111.kv_ref), custom_call_target="tpu_custom_call" | custom-call | flops 1000 | bytes 1024 | tf_op jit(solution)/shard_map/own_block/pallas_call | solution.py:329
  7.6 3.5 %collective-permute-start.2 = (bf16[128,2048]{1,0:T(8,128)(2,1)S(1)}, bf16[128,2048]{1,0:T(8,128)(2,1)S(1)}, u32[]{:S(2)}, u32[]{:S(2)}) collective-permute-start(bf16[128,2048]{1,0:T(8,128)(2,1)S(1)} %collective-permute-done.1.refs_0_), channel_id=1, source_target_pairs={{0,1},{1,3},{2,16},{3,5},{4,18},{5,7},{6,20},{7,22},{8,10},{9,8},{... | collective-permute-start | bytes 1572872 | tf_op jit(solution)/shard_map/ppermute | solution.py:414
  11.0 0.7 %collective-permute-start.6 = (bf16[128,2048]{1,0:T(8,128)(2,1)S(1)}, bf16[128,2048]{1,0:T(8,128)(2,1)S(1)}, u32[]{:S(2)}, u32[]{:S(2)}) collective-permute-start(bf16[128,2048]{1,0:T(8,128)(2,1)S(1)} %get-tuple-element.111.kv_ref), channel_id=1, source_target_pairs={{26,27}} | collective-permute-start | bytes 1572872 | tf_op jit(solution)/shard_map/ppermute | solution.py:425
  11.7 1.1 %collective-permute-done.3.refs_1_ = bf16[128,2048]{1,0:T(8,128)(2,1)} collective-permute-done((bf16[128,2048]{1,0:T(8,128)(2,1)S(1)}, bf16[128,2048]{1,0:T(8,128)(2,1)}, u32[]{:S(2)}, u32[]{:S(2)}) %collective-permute-start.3) | collective-permute-done | bytes 524320 | tf_op jit(solution)/shard_map/ppermute | solution.py:414
  12.9 3.5 %collective-permute-start.5 = (bf16[128,2048]{1,0:T(8,128)(2,1)}, bf16[128,2048]{1,0:T(8,128)(2,1)S(1)}, u32[]{:S(2)}, u32[]{:S(2)}) collective-permute-start(bf16[128,2048]{1,0:T(8,128)(2,1)} %collective-permute-done.3.refs_1_), channel_id=1, source_target_pairs={{0,1},{1,3},{3,5},{5,7},{7,6},{8,10},{10,12},{12,14},{14,15},{15,2... | collective-permute-start | bytes 1572872 | tf_op jit(solution)/shard_map/ppermute | solution.py:414
  16.4 1.1 %add_block.11 = (f32[2,8,128,512]{3,2,1,0:T(8,128)S(1)}, f32[2,8,1,512]{3,2,1,0:T(1,128)S(1)}, f32[2,8,1,512]{3,2,1,0:T(1,128)S(1)}) custom-call(s32[34]{0:T(128)S(4)} %get-tuple-element.63.info_ref, bf16[128,4096]{1,0:T(8,128)(2,1)S(1)} %fetch_queries.1.q_ref, ...), custom_call_target="tpu_custom_call", output_to_operand_aliasing={{0}: (4, {}), {1}: (5, {}), {2}: (6, {})} | custom-call | flops 1000 | bytes 1024 | tf_op jit(solution)/shard_map/add_block/pallas_call | solution.py:329
  17.4 1.2 %collective-permute-done.2.refs_1_ = bf16[128,2048]{1,0:T(8,128)(2,1)S(1)} collective-permute-done((bf16[128,2048]{1,0:T(8,128)(2,1)S(1)}, bf16[128,2048]{1,0:T(8,128)(2,1)S(1)}, u32[]{:S(2)}, u32[]{:S(2)}) %collective-permute-start.2) | collective-permute-done | bytes 524320 | tf_op jit(solution)/shard_map/ppermute | solution.py:414
  18.6 3.6 %collective-permute-start.4 = (bf16[128,2048]{1,0:T(8,128)(2,1)S(1)}, bf16[128,2048]{1,0:T(8,128)(2,1)S(1)}, u32[]{:S(2)}, u32[]{:S(2)}) collective-permute-start(bf16[128,2048]{1,0:T(8,128)(2,1)S(1)} %collective-permute-done.2.refs_1_), channel_id=1, source_target_pairs={{1,3},{3,5},{5,7},{7,6},{8,10},{10,12},{12,14},{14,15},{16,17},{17... | collective-permute-start | bytes 1572872 | tf_op jit(solution)/shard_map/ppermute | solution.py:414
  22.2 1.3 %add_block.12 = (f32[2,8,128,512]{3,2,1,0:T(8,128)S(1)}, f32[2,8,1,512]{3,2,1,0:T(1,128)S(1)}, f32[2,8,1,512]{3,2,1,0:T(1,128)S(1)}) custom-call(s32[34]{0:T(128)S(4)} %get-tuple-element.63.info_ref, bf16[128,4096]{1,0:T(8,128)(2,1)S(1)} %fetch_queries.1.q_ref, ...), custom_call_target="tpu_custom_call", output_to_operand_aliasing={{0}: (4, {}), {1}: (5, {}), {2}: (6, {})} | custom-call | flops 1000 | bytes 1024 | tf_op jit(solution)/shard_map/add_block/pallas_call | solution.py:329
  23.5 0.7 %collective-permute-done.5.refs_1_ = bf16[128,2048]{1,0:T(8,128)(2,1)S(1)} collective-permute-done((bf16[128,2048]{1,0:T(8,128)(2,1)}, bf16[128,2048]{1,0:T(8,128)(2,1)S(1)}, u32[]{:S(2)}, u32[]{:S(2)}) %collective-permute-start.5) | collective-permute-done | bytes 524320 | tf_op jit(solution)/shard_map/ppermute | solution.py:414
  24.2 3.5 %collective-permute-start.10 = (bf16[128,2048]{1,0:T(8,128)(2,1)S(1)}, bf16[128,2048]{1,0:T(8,128)(2,1)S(1)}, u32[]{:S(2)}, u32[]{:S(2)}) collective-permute-start(bf16[128,2048]{1,0:T(8,128)(2,1)S(1)} %collective-permute-done.5.refs_1_), channel_id=1, source_target_pairs={{1,3},{3,5},{5,7},{7,6},{10,12},{12,14},{14,15},{15,13},{16,17},{1... | collective-permute-start | bytes 1572872 | tf_op jit(solution)/shard_map/ppermute | solution.py:414
  27.7 0.7 %collective-permute-start.8 = (bf16[128,2048]{1,0:T(8,128)(2,1)}, bf16[128,2048]{1,0:T(8,128)(2,1)S(1)}, u32[]{:S(2)}, u32[]{:S(2)}) collective-permute-start(bf16[128,2048]{1,0:T(8,128)(2,1)} %collective-permute-done.3.refs_1_), channel_id=1, source_target_pairs={{8,16}} | collective-permute-start | bytes 1572872 | tf_op jit(solution)/shard_map/ppermute | solution.py:432
  28.4 0.7 %collective-permute-start.9 = (bf16[128,2048]{1,0:T(8,128)(2,1)S(1)}, bf16[128,2048]{1,0:T(8,128)(2,1)S(1)}, u32[]{:S(2)}, u32[]{:S(2)}) collective-permute-start(bf16[128,2048]{1,0:T(8,128)(2,1)S(1)} %collective-permute-done.2.refs_1_), channel_id=1, source_target_pairs={{21,28}} | collective-permute-start | bytes 1572872 | tf_op jit(solution)/shard_map/ppermute | solution.py:432
  29.1 0.7 %collective-permute-done.4.refs_1_ = bf16[128,2048]{1,0:T(8,128)(2,1)S(1)} collective-permute-done((bf16[128,2048]{1,0:T(8,128)(2,1)S(1)}, bf16[128,2048]{1,0:T(8,128)(2,1)S(1)}, u32[]{:S(2)}, u32[]{:S(2)}) %collective-permute-start.4) | collective-permute-done | bytes 524320 | tf_op jit(solution)/shard_map/ppermute | solution.py:414
  29.9 3.5 %collective-permute-start.7 = (bf16[128,2048]{1,0:T(8,128)(2,1)S(1)}, bf16[128,2048]{1,0:T(8,128)(2,1)S(1)}, u32[]{:S(2)}, u32[]{:S(2)}) collective-permute-start(bf16[128,2048]{1,0:T(8,128)(2,1)S(1)} %collective-permute-done.4.refs_1_), channel_id=1, source_target_pairs={{3,5},{5,7},{6,20},{7,6},{10,12},{12,14},{14,15},{15,13},{16,17},{... | collective-permute-start | bytes 1572872 | tf_op jit(solution)/shard_map/ppermute | solution.py:414
  33.4 1.3 %collective-permute-start.13 = (bf16[128,2048]{1,0:T(8,128)(2,1)S(1)}, bf16[128,2048]{1,0:T(8,128)(2,1)S(1)}, u32[]{:S(2)}, u32[]{:S(2)}) collective-permute-start(bf16[128,2048]{1,0:T(8,128)(2,1)S(1)} %get-tuple-element.111.kv_ref), channel_id=1, source_target_pairs={{8,16},{9,17},{10,18},{11,19},{12,20},{13,21},{14,22},{15,23}} | collective-permute-start | bytes 1572872 | tf_op jit(solution)/shard_map/ppermute | solution.py:433
  34.7 0.8 %collective-permute-done.10.refs_1_ = bf16[128,2048]{1,0:T(8,128)(2,1)S(1)} collective-permute-done((bf16[128,2048]{1,0:T(8,128)(2,1)S(1)}, bf16[128,2048]{1,0:T(8,128)(2,1)S(1)}, u32[]{:S(2)}, u32[]{:S(2)}) %collective-permute-start.10) | collective-permute-done | bytes 524320 | tf_op jit(solution)/shard_map/ppermute | solution.py:414
  35.5 3.5 %collective-permute-start.12 = (bf16[128,2048]{1,0:T(8,128)(2,1)S(1)}, bf16[128,2048]{1,0:T(8,128)(2,1)S(1)}, u32[]{:S(2)}, u32[]{:S(2)}) collective-permute-start(bf16[128,2048]{1,0:T(8,128)(2,1)S(1)} %collective-permute-done.10.refs_1_), channel_id=1, source_target_pairs={{3,5},{5,7},{6,4},{7,6},{12,14},{13,19},{14,15},{15,13},{16,25},{1... | collective-permute-start | bytes 1572872 | tf_op jit(solution)/shard_map/ppermute | solution.py:414
  39.0 1.3 %add_block.16 = (f32[2,8,128,512]{3,2,1,0:T(8,128)S(1)}, f32[2,8,1,512]{3,2,1,0:T(1,128)S(1)}, f32[2,8,1,512]{3,2,1,0:T(1,128)S(1)}) custom-call(s32[34]{0:T(128)S(4)} %get-tuple-element.63.info_ref, bf16[128,4096]{1,0:T(8,128)(2,1)S(1)} %fetch_queries.1.q_ref, ...), custom_call_target="tpu_custom_call", output_to_operand_aliasing={{0}: (4, {}), {1}: (5, {}), {2}: (6, {})} | custom-call | flops 1000 | bytes 1024 | tf_op jit(solution)/shard_map/add_block/pallas_call | solution.py:329
  40.7 8.8 %collective-permute-done.13.refs_0_ = bf16[128,2048]{1,0:T(8,128)(2,1)S(1)} collective-permute-done((bf16[128,2048]{1,0:T(8,128)(2,1)S(1)}, bf16[128,2048]{1,0:T(8,128)(2,1)S(1)}, u32[]{:S(2)}, u32[]{:S(2)}) %collective-permute-start.13) | collective-permute-done | bytes 524320 | tf_op jit(solution)/shard_map/ppermute | solution.py:433
  49.5 1.3 %last_block.1 = bf16[128,4096]{1,0:T(8,128)(2,1)} custom-call(s32[34]{0:T(128)S(4)} %get-tuple-element.63.info_ref, bf16[128,4096]{1,0:T(8,128)(2,1)S(1)} %fetch_queries.1.q_ref, bf16[128,4352]{1,0:T(8,128)(2,1)S(1)} %collective-permute-done.11.refs_0_, bf16[128,2048]{1,0:T(8,128)(2,1)S(1)} %collective-permute-done.12.kv_ref.refs_1_, ...), custom_call_target="tpu_custom_call" | custom-call | tf_op jit(solution)/shard_map/last_block/pallas_call | solution.py:360
  (20 shorter events, 1.1 us)
Async XLA Ops:
  1.1 6.4 %collective-permute-start.1 = (bf16[128,2048]{1,0:T(8,128)(2,1)S(1)}, bf16[128,2048]{1,0:T(8,128)(2,1)S(1)}, u32[]{:S(2)}, u32[]{:S(2)}) collective-permute-start(bf16[128,2048]{1,0:T(8,128)(2,1)S(1)} %get-tuple-element.111.kv_ref), channel_id=1, source_target_pairs={{0,8},{1,9},{2,10},{3,11},{4,12},{5,13},{6,14},{7,15},{8,0},{9,1},... | collective-permute-start | bytes 1572872 | tf_op jit(solution)/shard_map/ppermute | solution.py:419
  1.2 15.2 %collective-permute-start = (bf16[128,4096]{1,0:T(8,128)(2,1)}, bf16[128,4096]{1,0:T(8,128)(2,1)S(1)}, u32[]{:S(2)}, u32[]{:S(2)}) collective-permute-start(bf16[128,4096]{1,0:T(8,128)(2,1)} %q_ref.1), channel_id=1, source_target_pairs={{0,8},{1,9},{2,10},{3,11},{4,12},{5,13},{6,14},{7,15},{8,0},{9,1},... | collective-permute-start | bytes 3145736 | tf_op jit(solution)/shard_map/ppermute | solution.py:423
  1.7 11.2 %collective-permute-start.3 = (bf16[128,2048]{1,0:T(8,128)(2,1)S(1)}, bf16[128,2048]{1,0:T(8,128)(2,1)}, u32[]{:S(2)}, u32[]{:S(2)}) collective-permute-start(bf16[128,2048]{1,0:T(8,128)(2,1)S(1)} %get-tuple-element.111.kv_ref), channel_id=1, source_target_pairs={{0,1},{1,3},{2,0},{3,5},{5,7},{8,10},{9,8},{10,12},{11,25},{12,14}... | collective-permute-start | bytes 1572872 | tf_op jit(solution)/shard_map/ppermute | solution.py:414
  7.6 11.1 %collective-permute-start.2 = (bf16[128,2048]{1,0:T(8,128)(2,1)S(1)}, bf16[128,2048]{1,0:T(8,128)(2,1)S(1)}, u32[]{:S(2)}, u32[]{:S(2)}) collective-permute-start(bf16[128,2048]{1,0:T(8,128)(2,1)S(1)} %collective-permute-done.1.refs_0_), channel_id=1, source_target_pairs={{0,1},{1,3},{2,16},{3,5},{4,18},{5,7},{6,20},{7,22},{8,10},{9,8},{... | collective-permute-start | bytes 1572872 | tf_op jit(solution)/shard_map/ppermute | solution.py:414
  11.0 12.4 %collective-permute-start.6 = (bf16[128,2048]{1,0:T(8,128)(2,1)S(1)}, bf16[128,2048]{1,0:T(8,128)(2,1)S(1)}, u32[]{:S(2)}, u32[]{:S(2)}) collective-permute-start(bf16[128,2048]{1,0:T(8,128)(2,1)S(1)} %get-tuple-element.111.kv_ref), channel_id=1, source_target_pairs={{26,27}} | collective-permute-start | bytes 1572872 | tf_op jit(solution)/shard_map/ppermute | solution.py:425
  12.9 11.4 %collective-permute-start.5 = (bf16[128,2048]{1,0:T(8,128)(2,1)}, bf16[128,2048]{1,0:T(8,128)(2,1)S(1)}, u32[]{:S(2)}, u32[]{:S(2)}) collective-permute-start(bf16[128,2048]{1,0:T(8,128)(2,1)} %collective-permute-done.3.refs_1_), channel_id=1, source_target_pairs={{0,1},{1,3},{3,5},{5,7},{7,6},{8,10},{10,12},{12,14},{14,15},{15,2... | collective-permute-start | bytes 1572872 | tf_op jit(solution)/shard_map/ppermute | solution.py:414
  18.6 11.2 %collective-permute-start.4 = (bf16[128,2048]{1,0:T(8,128)(2,1)S(1)}, bf16[128,2048]{1,0:T(8,128)(2,1)S(1)}, u32[]{:S(2)}, u32[]{:S(2)}) collective-permute-start(bf16[128,2048]{1,0:T(8,128)(2,1)S(1)} %collective-permute-done.2.refs_1_), channel_id=1, source_target_pairs={{1,3},{3,5},{5,7},{7,6},{8,10},{10,12},{12,14},{14,15},{16,17},{17... | collective-permute-start | bytes 1572872 | tf_op jit(solution)/shard_map/ppermute | solution.py:414
  24.2 11.2 %collective-permute-start.10 = (bf16[128,2048]{1,0:T(8,128)(2,1)S(1)}, bf16[128,2048]{1,0:T(8,128)(2,1)S(1)}, u32[]{:S(2)}, u32[]{:S(2)}) collective-permute-start(bf16[128,2048]{1,0:T(8,128)(2,1)S(1)} %collective-permute-done.5.refs_1_), channel_id=1, source_target_pairs={{1,3},{3,5},{5,7},{7,6},{10,12},{12,14},{14,15},{15,13},{16,17},{1... | collective-permute-start | bytes 1572872 | tf_op jit(solution)/shard_map/ppermute | solution.py:414
  27.7 12.5 %collective-permute-start.8 = (bf16[128,2048]{1,0:T(8,128)(2,1)}, bf16[128,2048]{1,0:T(8,128)(2,1)S(1)}, u32[]{:S(2)}, u32[]{:S(2)}) collective-permute-start(bf16[128,2048]{1,0:T(8,128)(2,1)} %collective-permute-done.3.refs_1_), channel_id=1, source_target_pairs={{8,16}} | collective-permute-start | bytes 1572872 | tf_op jit(solution)/shard_map/ppermute | solution.py:432
  28.4 11.8 %collective-permute-start.9 = (bf16[128,2048]{1,0:T(8,128)(2,1)S(1)}, bf16[128,2048]{1,0:T(8,128)(2,1)S(1)}, u32[]{:S(2)}, u32[]{:S(2)}) collective-permute-start(bf16[128,2048]{1,0:T(8,128)(2,1)S(1)} %collective-permute-done.2.refs_1_), channel_id=1, source_target_pairs={{21,28}} | collective-permute-start | bytes 1572872 | tf_op jit(solution)/shard_map/ppermute | solution.py:432
  29.9 10.6 %collective-permute-start.7 = (bf16[128,2048]{1,0:T(8,128)(2,1)S(1)}, bf16[128,2048]{1,0:T(8,128)(2,1)S(1)}, u32[]{:S(2)}, u32[]{:S(2)}) collective-permute-start(bf16[128,2048]{1,0:T(8,128)(2,1)S(1)} %collective-permute-done.4.refs_1_), channel_id=1, source_target_pairs={{3,5},{5,7},{6,20},{7,6},{10,12},{12,14},{14,15},{15,13},{16,17},{... | collective-permute-start | bytes 1572872 | tf_op jit(solution)/shard_map/ppermute | solution.py:414
  33.4 16.1 %collective-permute-start.13 = (bf16[128,2048]{1,0:T(8,128)(2,1)S(1)}, bf16[128,2048]{1,0:T(8,128)(2,1)S(1)}, u32[]{:S(2)}, u32[]{:S(2)}) collective-permute-start(bf16[128,2048]{1,0:T(8,128)(2,1)S(1)} %get-tuple-element.111.kv_ref), channel_id=1, source_target_pairs={{8,16},{9,17},{10,18},{11,19},{12,20},{13,21},{14,22},{15,23}} | collective-permute-start | bytes 1572872 | tf_op jit(solution)/shard_map/ppermute | solution.py:433
  35.5 14.0 %collective-permute-start.12 = (bf16[128,2048]{1,0:T(8,128)(2,1)S(1)}, bf16[128,2048]{1,0:T(8,128)(2,1)S(1)}, u32[]{:S(2)}, u32[]{:S(2)}) collective-permute-start(bf16[128,2048]{1,0:T(8,128)(2,1)S(1)} %collective-permute-done.10.refs_1_), channel_id=1, source_target_pairs={{3,5},{5,7},{6,4},{7,6},{12,14},{13,19},{14,15},{15,13},{16,25},{1... | collective-permute-start | bytes 1572872 | tf_op jit(solution)/shard_map/ppermute | solution.py:414
  40.7 8.8 %collective-permute-start.11 = (bf16[128,4352]{1,0:T(8,128)(2,1)S(1)}, bf16[128,4352]{1,0:T(8,128)(2,1)S(1)}, u32[]{:S(2)}, u32[]{:S(2)}) collective-permute-start(bf16[128,4352]{1,0:T(8,128)(2,1)S(1)} %get-tuple-element.109), channel_id=1, source_target_pairs={{0,8},{1,9},{2,10},{3,11},{4,12},{5,13},{6,14},{7,15},{8,0},{9,1},... | collective-permute-start | bytes 3342344 | tf_op jit(solution)/shard_map/ppermute | solution.py:443

commit v5 on v4

--- a/solution.py
+++ b/solution.py
@@ -85,9 +85,11 @@
             row += [b, NONE if u is None else OWN if u == d else MATE]
         row += [d ^ m, OWN if user(d, d ^ m) == d else NONE]
         o = d // m
-        row += [d - m, OWN] if o % 2 == 0 and o > 0 else [0, NONE]
-        for b, q, _ in straight:
-            row += [b, OWN] if q == d else [0, NONE]
+        back = [d - m, OWN] if o % 2 == 0 and o > 0 else [0, NONE]
+        early = d % m in (3, 4)
+        row += [0, NONE] if early else back
+        for b, q, e in straight:
+            row += [b, OWN] if q == d else back if early and b == e else [0, NONE]
         rows.append(row)
     return rows
 
@@ -103,6 +105,7 @@
     tile = 2 if group_size % 2 == 0 else 1
     bias = jnp.concatenate([bias] * tile, axis=1)
     for g in range(kv_heads):
+        row = slice(g, g + 1)
         keys = kv_ref[:, g * HD : (g + 1) * HD]
         values = kv_ref[:, (kv_heads + g) * HD : (kv_heads + g + 1) * HD]
         for j in range(0, group_size, tile):
@@ -112,17 +115,17 @@
             s = s * SCALE + bias
             top = jnp.max(s, axis=0, keepdims=True)
             if not fresh:
-                old = max_ref[u, g, :, columns]
+                old = max_ref[u, row, columns]
                 top = jnp.maximum(old, top)
                 fade = jnp.exp2(old - top)
             p = jnp.exp2(s - top)
             total = jnp.sum(p, axis=0, keepdims=True)
             mixed = jnp.dot(values, p.astype(jnp.bfloat16), preferred_element_type=jnp.float32)
-            max_ref[u, g, :, columns] = top
-            sum_ref[u, g, :, columns] = total if fresh else sum_ref[u, g, :, columns] * fade + total
+            max_ref[u, row, columns] = top
+            sum_ref[u, row, columns] = total if fresh else sum_ref[u, row, columns] * fade + total
             acc_ref[u, g, :, columns] = mixed if fresh else acc_ref[u, g, :, columns] * fade + mixed
-        if finish is not None:
-            finish(g)
+        if finish is not None and (g + 1) % (kv_heads // 2) == 0:
+            finish(slice(g + 1 - kv_heads // 2, g + 1))
 
 
 def head_of(ref):
@@ -245,19 +248,13 @@
     add_block(sizes, n_docs, slot, info_ref, q_ref, qm_ref, kv_ref, state)
     acc_ref, max_ref, sum_ref = state
     width = group_size * HD
-    heads = kv_heads * group_size
-    tops, sums = [], []
+    totals = sum_ref[MATE]
+    shares = 1.0 / jnp.where(totals > 0, totals, 1.0)
     for g in range(kv_heads):
-        top, total = max_ref[MATE, g], sum_ref[MATE, g]
-        share = 1.0 / jnp.where(total > 0, total, 1.0)
-        part_ref[:, g * width : (g + 1) * width] = (acc_ref[MATE, g] * share).astype(jnp.bfloat16)
-        for j in range(group_size):
-            tops.append(top[:, j * HD : (j + 1) * HD])
-            sums.append(total[:, j * HD : (j + 1) * HD])
-    for column, stats in enumerate((tops, sums)):
-        place = (heads + column) * HD
-        for k, piece in enumerate(split3(jnp.concatenate(stats, axis=0))):
-            part_ref[k * heads : (k + 1) * heads, place : place + HD] = piece
+        part_ref[:, g * width : (g + 1) * width] = (acc_ref[MATE, g] * shares[g : g + 1]).astype(jnp.bfloat16)
+    stats = jnp.concatenate([max_ref[MATE], totals], axis=0)
+    for k, piece in enumerate(split3(stats)):
+        part_ref[2 * k * kv_heads : 2 * (k + 1) * kv_heads, kv_heads * width :] = piece
 
 
 def touch_kernel(info_ref, kv_ref, *refs):
@@ -266,34 +263,38 @@
 
 def last_kernel(sizes, n_docs, slot, mated, info_ref, q_ref, *refs):
     kv_heads, group_size, rows = sizes
-    heads = kv_heads * group_size
     width = group_size * HD
     part_ref, refs = (refs[0], refs[1:]) if mated else (None, refs)
     kv_ref, acc_ref, max_ref, sum_ref, out_ref, out_here, sems = refs
     if mated:
-        tops, sums = (
-            sum(part_ref[k * heads : (k + 1) * heads, c * HD : (c + 1) * HD].astype(jnp.float32) for k in range(3))
-            for c in (heads, heads + 1)
+        stats = sum(
+            part_ref[2 * k * kv_heads : 2 * (k + 1) * kv_heads, kv_heads * width :].astype(jnp.float32) for k in range(3)
         )
+        tops, sums = stats[:kv_heads], stats[kv_heads:]
 
     def store(g):
         columns = pl.ds(g * width, width)
         return pltpu.make_async_copy(out_here.at[:, columns], out_ref.at[:, columns], sems.at[g])
 
-    def finish(g):
-        for j in range(group_size):
-            h, mine = g * group_size + j, slice(j * HD, (j + 1) * HD)
-            numer, top, total = acc_ref[OWN, g, :, mine], max_ref[OWN, g, :, mine], sum_ref[OWN, g, :, mine]
+    def finish(some):
+        top, total = max_ref[OWN, some], sum_ref[OWN, some]
+        if mated:
+            both = jnp.maximum(top, tops[some])
+            weight, other = jnp.exp2(top - both), jnp.exp2(tops[some] - both) * sums[some]
+            share = 1.0 / (total * weight + other)
+            mine, others = weight * share, other * share
+        else:
+            mine = 1.0 / total
+        for k, g in enumerate(range(some.start, some.stop)):
+            out = acc_ref[OWN, g] * mine[k : k + 1]
             if mated:
-                both = jnp.maximum(top, tops[h : h + 1])
-                weight, other = jnp.exp2(top - both), jnp.exp2(tops[h : h + 1] - both) * sums[h : h + 1]
-                share = 1.0 / (total * weight + other)
-                theirs = part_ref[:, h * HD : (h + 1) * HD].astype(jnp.float32)
-                out = numer * (weight * share) + theirs * (other * share)
-            else:
-                out = numer * (1.0 / total)
-            out_here[:, h * HD : (h + 1) * HD] = out.astype(jnp.bfloat16).T
-        store(g).start()
+                theirs = part_ref[:, g * width : (g + 1) * width].astype(jnp.float32)
+                out = out + theirs * others[k : k + 1]
+            out = out.astype(jnp.bfloat16)
+            for j in range(group_size):
+                h = g * group_size + j
+                out_here[:, h * HD : (h + 1) * HD] = out[:, j * HD : (j + 1) * HD].T
+            store(g).start()
 
     use = info_ref[3 + 2 * slot]
 
@@ -304,8 +305,7 @@
 
     @pl.when(use == NONE)
     def _():
-        for g in range(kv_heads):
-            finish(g)
+        finish(slice(0, kv_heads))
 
     for g in range(kv_heads):
         store(g).wait()
@@ -317,8 +317,8 @@
     sets = 2 if mated else 1
     state = [
         pltpu.VMEM((sets, kv_heads, HD, tall), jnp.float32),
-        pltpu.VMEM((sets, kv_heads, 1, tall), jnp.float32),
-        pltpu.VMEM((sets, kv_heads, 1, tall), jnp.float32),
+        pltpu.VMEM((sets, kv_heads, tall), jnp.float32),
+        pltpu.VMEM((sets, kv_heads, tall), jnp.float32),
     ]
     smem, vmem = pl.BlockSpec(memory_space=pltpu.SMEM), pl.BlockSpec(memory_space=pltpu.VMEM)
     held = []
@@ -350,7 +350,7 @@
         call(kernel, qs + [kv], [], "add_block")
 
     def part(slot, q, qm, kv):
-        out = jax.ShapeDtypeStruct((rows, (kv_heads * group_size + 2) * HD), jnp.bfloat16)
+        out = jax.ShapeDtypeStruct((rows, (kv_heads + 1) * group_size * HD), jnp.bfloat16)
         return call(functools.partial(part_kernel, sizes, n_docs, slot), [q, qm, kv], [out], "mate_part")[0]
 
     def touch(kv):
@@ -415,6 +415,7 @@
 
     mates = [(d, d ^ m) for d in range(groups * m)]
     eight_back = [(d - m, d) for o in range(2, groups, 2) for d in range(o * m, (o + 1) * m)]
+    busy = [(e, d) for e, d in eight_back if d % m in (3, 4)]
     u1 = send(kv, "own", 1)
     kvm = lax.ppermute(kv, AXES, mates)
     q = fetched(queries)
@@ -422,7 +423,7 @@
     w1 = send(after(kvm), "mate", 1)
     qm = lax.ppermute(queries, AXES, mates)
     beside = [[(e, q)] for _, q, e in straight]
-    near = [lax.ppermute(kv, AXES, beside[0])]
+    near = [lax.ppermute(kv, AXES, beside[0] + busy)]
     u2 = send(after(u1), "own", 2)
     add(7, q, None, kvm)
     add(0, q, qm, u1)
@@ -430,7 +431,7 @@
     add(1, q, qm, w1)
     add(9, q, None, near[0])
     near += [lax.ppermute(after(w1), AXES, beside[1]), lax.ppermute(u1, AXES, beside[2])]
-    kv8 = lax.ppermute(after(kv), AXES, eight_back)
+    kv8 = lax.ppermute(after(kv), AXES, [x for x in eight_back if x not in busy])
     u3 = send(after(u2), "own", 3)
     add(2, q, qm, u2)
     w3 = send(after(w2), "mate", 3)

time: 51.4 us -> 50.6 us (0.984)
  the two profiles are of different devices: /device:TPU:14 before, /device:TPU:22 now
where the time goes in v5:
time: 50.6 us; the launch traced here: 50.2 us
  starting transfers between devices  25.8 us (51%)
  Pallas kernels  13.6 us (27%)
  waiting for transfers between devices  10.3 us (20%)
    ppermute x7, starting transfers between devices, send(): lax.ppermute(block, AXES, sorted(((e, d) for d, (e, _) in route[op, step]...  21.2 us
    pallas_call x13, Pallas kernels, call(): pl.pallas_call(kernel, out_shape=out, in_specs=[smem] + [vmem] * (len(arr...  8.89 us
    ppermute x7, waiting for transfers between devices, send(): lax.ppermute(block, AXES, sorted(((e, d) for d, (e, _) in route[op, step]...  8.81 us
    pallas_call x1, Pallas kernels, last(): pl.pallas_call(functools.partial(last_kernel, sizes, n_docs, slot, mated)...  2.35 us
    ppermute x1, waiting for transfers between devices, ring_shards(): lax.ppermute(after(kv), AXES, [x for x in eight_back if x not in busy])  1.51 us
    ppermute x1, starting transfers between devices, ring_shards(): lax.ppermute(after(w1), AXES, beside[1])  1.32 us
    ppermute x1, starting transfers between devices, ring_shards(): lax.ppermute(after(kv), AXES, [x for x in eight_back if x not in busy])  1.29 us
    pallas_call x1, Pallas kernels, fetched(): pl.pallas_call(fetch_kernel, out_shape=pltpu.VMEM(queries.shape, queries....  1.24 us
  transfers between devices with their start and end apart: 14, of which 5 were waited for; matrix products, arithmetic and copies ran while one was open for 0% of the time, Pallas kernels for 20%

profile of v5, /device:TPU:22, one launch (start us, length us, event | category | flops | bytes accessed | tf_op | source)
XLA Modules:
  0.0 50.2 jit_solution(4767026864908799311)
XLA Ops:
  0.0 1.1 %pack_keys_values.1 = (bf16[128,2048]{1,0:T(8,128)(2,1)S(1)}, s32[34]{0:T(128)S(4)}) custom-call(s32[8]{0:T(128)} %refs_0_.1, s32[8]{0:T(128)} %refs_1_.1, s32[32,25]{1,0:T(8,128)} %constant.2.clone.refs_2_, bf16[128,1024]{1,0:T(8,128)(2,1)} %refs_3_.1, bf16[128,1024]{1,0:T(8,128)(2,1)} %refs_4_.1), custom_call_target="tpu_custom_call" | custom-call | tf_op jit(solution)/shard_map/pack_keys_values/pallas_call | solution.py:385
  1.7 3.5 %collective-permute-start.3 = (bf16[128,2048]{1,0:T(8,128)(2,1)S(1)}, bf16[128,2048]{1,0:T(8,128)(2,1)}, u32[]{:S(2)}, u32[]{:S(2)}) collective-permute-start(bf16[128,2048]{1,0:T(8,128)(2,1)S(1)} %get-tuple-element.111.kv_ref), channel_id=1, source_target_pairs={{0,1},{1,3},{2,0},{3,5},{5,7},{8,10},{9,8},{10,12},{11,25},{12,14}... | collective-permute-start | bytes 1572872 | tf_op jit(solution)/shard_map/ppermute | solution.py:414
  5.2 1.2 %fetch_queries.1.q_ref = bf16[128,4096]{1,0:T(8,128)(2,1)S(1)} custom-call(bf16[128,4096]{1,0:T(8,128)(2,1)} %q_ref.1), custom_call_target="tpu_custom_call" | custom-call | tf_op jit(solution)/shard_map/fetch_queries/pallas_call | solution.py:198
  6.4 1.1 %own_block.1 = (f32[2,8,128,512]{3,2,1,0:T(8,128)S(1)}, f32[2,8,512]{2,1,0:T(8,128)S(1)}, f32[2,8,512]{2,1,0:T(8,128)S(1)}) custom-call(s32[34]{0:T(128)S(4)} %get-tuple-element.63.info_ref, bf16[128,4096]{1,0:T(8,128)(2,1)S(1)} %fetch_queries.1.q_ref, bf16[128,2048]{1,0:T(8,128)(2,1)S(1)} %get-tuple-element.111.kv_ref), custom_call_target="tpu_custom_call" | custom-call | flops 1000 | bytes 1024 | tf_op jit(solution)/shard_map/own_block/pallas_call | solution.py:329
  7.6 2.4 %collective-permute-start.2 = (bf16[128,2048]{1,0:T(8,128)(2,1)S(1)}, bf16[128,2048]{1,0:T(8,128)(2,1)S(1)}, u32[]{:S(2)}, u32[]{:S(2)}) collective-permute-start(bf16[128,2048]{1,0:T(8,128)(2,1)S(1)} %collective-permute-done.1.refs_0_), channel_id=1, source_target_pairs={{0,1},{1,3},{2,16},{3,5},{4,18},{5,7},{6,20},{7,22},{8,10},{9,8},{... | collective-permute-start | bytes 1572872 | tf_op jit(solution)/shard_map/ppermute | solution.py:414
  10.0 0.7 %collective-permute-start.6 = (bf16[128,2048]{1,0:T(8,128)(2,1)S(1)}, bf16[128,2048]{1,0:T(8,128)(2,1)S(1)}, u32[]{:S(2)}, u32[]{:S(2)}) collective-permute-start(bf16[128,2048]{1,0:T(8,128)(2,1)S(1)} %get-tuple-element.111.kv_ref), channel_id=1, source_target_pairs={{26,27},{11,19},{12,20}} | collective-permute-start | bytes 1572872 | tf_op jit(solution)/shard_map/ppermute | solution.py:426
  10.7 2.2 %collective-permute-done.3.refs_1_ = bf16[128,2048]{1,0:T(8,128)(2,1)} collective-permute-done((bf16[128,2048]{1,0:T(8,128)(2,1)S(1)}, bf16[128,2048]{1,0:T(8,128)(2,1)}, u32[]{:S(2)}, u32[]{:S(2)}) %collective-permute-start.3) | collective-permute-done | bytes 524320 | tf_op jit(solution)/shard_map/ppermute | solution.py:414
  12.9 3.5 %collective-permute-start.5 = (bf16[128,2048]{1,0:T(8,128)(2,1)}, bf16[128,2048]{1,0:T(8,128)(2,1)S(1)}, u32[]{:S(2)}, u32[]{:S(2)}) collective-permute-start(bf16[128,2048]{1,0:T(8,128)(2,1)} %collective-permute-done.3.refs_1_), channel_id=1, source_target_pairs={{0,1},{1,3},{3,5},{5,7},{7,6},{8,10},{10,12},{12,14},{14,15},{15,2... | collective-permute-start | bytes 1572872 | tf_op jit(solution)/shard_map/ppermute | solution.py:414
  16.4 2.3 %add_block.11 = (f32[2,8,128,512]{3,2,1,0:T(8,128)S(1)}, f32[2,8,512]{2,1,0:T(8,128)S(1)}, f32[2,8,512]{2,1,0:T(8,128)S(1)}) custom-call(s32[34]{0:T(128)S(4)} %get-tuple-element.63.info_ref, bf16[128,4096]{1,0:T(8,128)(2,1)S(1)} %fetch_queries.1.q_ref, ...), custom_call_target="tpu_custom_call", output_to_operand_aliasing={{0}: (4, {}), {1}: (5, {}), {2}: (6, {})} | custom-call | flops 1000 | bytes 1024 | tf_op jit(solution)/shard_map/add_block/pallas_call | solution.py:329
  18.7 3.1 %collective-permute-start.4 = (bf16[128,2048]{1,0:T(8,128)(2,1)S(1)}, bf16[128,2048]{1,0:T(8,128)(2,1)S(1)}, u32[]{:S(2)}, u32[]{:S(2)}) collective-permute-start(bf16[128,2048]{1,0:T(8,128)(2,1)S(1)} %collective-permute-done.2.refs_1_), channel_id=1, source_target_pairs={{1,3},{3,5},{5,7},{7,6},{8,10},{10,12},{12,14},{14,15},{16,17},{17... | collective-permute-start | bytes 1572872 | tf_op jit(solution)/shard_map/ppermute | solution.py:414
  21.9 1.3 %add_block.12 = (f32[2,8,128,512]{3,2,1,0:T(8,128)S(1)}, f32[2,8,512]{2,1,0:T(8,128)S(1)}, f32[2,8,512]{2,1,0:T(8,128)S(1)}) custom-call(s32[34]{0:T(128)S(4)} %get-tuple-element.63.info_ref, bf16[128,4096]{1,0:T(8,128)(2,1)S(1)} %fetch_queries.1.q_ref, ...), custom_call_target="tpu_custom_call", output_to_operand_aliasing={{0}: (4, {}), {1}: (5, {}), {2}: (6, {})} | custom-call | flops 1000 | bytes 1024 | tf_op jit(solution)/shard_map/add_block/pallas_call | solution.py:329
  23.2 1.1 %collective-permute-done.5.refs_1_ = bf16[128,2048]{1,0:T(8,128)(2,1)S(1)} collective-permute-done((bf16[128,2048]{1,0:T(8,128)(2,1)}, bf16[128,2048]{1,0:T(8,128)(2,1)S(1)}, u32[]{:S(2)}, u32[]{:S(2)}) %collective-permute-start.5) | collective-permute-done | bytes 524320 | tf_op jit(solution)/shard_map/ppermute | solution.py:414
  24.2 3.4 %collective-permute-start.10 = (bf16[128,2048]{1,0:T(8,128)(2,1)S(1)}, bf16[128,2048]{1,0:T(8,128)(2,1)S(1)}, u32[]{:S(2)}, u32[]{:S(2)}) collective-permute-start(bf16[128,2048]{1,0:T(8,128)(2,1)S(1)} %collective-permute-done.5.refs_1_), channel_id=1, source_target_pairs={{1,3},{3,5},{5,7},{7,6},{10,12},{12,14},{14,15},{15,13},{16,17},{1... | collective-permute-start | bytes 1572872 | tf_op jit(solution)/shard_map/ppermute | solution.py:414
  28.3 1.3 %collective-permute-start.9 = (bf16[128,2048]{1,0:T(8,128)(2,1)S(1)}, bf16[128,2048]{1,0:T(8,128)(2,1)S(1)}, u32[]{:S(2)}, u32[]{:S(2)}) collective-permute-start(bf16[128,2048]{1,0:T(8,128)(2,1)S(1)} %collective-permute-done.2.refs_1_), channel_id=1, source_target_pairs={{21,28}} | collective-permute-start | bytes 1572872 | tf_op jit(solution)/shard_map/ppermute | solution.py:433
  29.7 1.3 %add_block.14 = (f32[2,8,128,512]{3,2,1,0:T(8,128)S(1)}, f32[2,8,512]{2,1,0:T(8,128)S(1)}, f32[2,8,512]{2,1,0:T(8,128)S(1)}) custom-call(s32[34]{0:T(128)S(4)} %get-tuple-element.63.info_ref, bf16[128,4096]{1,0:T(8,128)(2,1)S(1)} %fetch_queries.1.q_ref, ...), custom_call_target="tpu_custom_call", output_to_operand_aliasing={{0}: (4, {}), {1}: (5, {}), {2}: (6, {})} | custom-call | flops 1000 | bytes 1024 | tf_op jit(solution)/shard_map/add_block/pallas_call | solution.py:329
  31.0 2.3 %collective-permute-start.7 = (bf16[128,2048]{1,0:T(8,128)(2,1)S(1)}, bf16[128,2048]{1,0:T(8,128)(2,1)S(1)}, u32[]{:S(2)}, u32[]{:S(2)}) collective-permute-start(bf16[128,2048]{1,0:T(8,128)(2,1)S(1)} %collective-permute-done.4.refs_1_), channel_id=1, source_target_pairs={{3,5},{5,7},{6,20},{7,6},{10,12},{12,14},{14,15},{15,13},{16,17},{... | collective-permute-start | bytes 1572872 | tf_op jit(solution)/shard_map/ppermute | solution.py:414
  33.2 1.3 %collective-permute-start.13 = (bf16[128,2048]{1,0:T(8,128)(2,1)S(1)}, bf16[128,2048]{1,0:T(8,128)(2,1)S(1)}, u32[]{:S(2)}, u32[]{:S(2)}) collective-permute-start(bf16[128,2048]{1,0:T(8,128)(2,1)S(1)} %get-tuple-element.111.kv_ref), channel_id=1, source_target_pairs={{8,16},{9,17},{10,18},{13,21},{14,22},{15,23}} | collective-permute-start | bytes 1572872 | tf_op jit(solution)/shard_map/ppermute | solution.py:434
  34.5 1.3 %add_block.15 = (f32[2,8,128,512]{3,2,1,0:T(8,128)S(1)}, f32[2,8,512]{2,1,0:T(8,128)S(1)}, f32[2,8,512]{2,1,0:T(8,128)S(1)}) custom-call(s32[34]{0:T(128)S(4)} %get-tuple-element.63.info_ref, bf16[128,4096]{1,0:T(8,128)(2,1)S(1)} %fetch_queries.1.q_ref, ...), custom_call_target="tpu_custom_call", output_to_operand_aliasing={{0}: (4, {}), {1}: (5, {}), {2}: (6, {})} | custom-call | flops 1000 | bytes 1024 | tf_op jit(solution)/shard_map/add_block/pallas_call | solution.py:329
  35.8 3.0 %collective-permute-start.12 = (bf16[128,2048]{1,0:T(8,128)(2,1)S(1)}, bf16[128,2048]{1,0:T(8,128)(2,1)S(1)}, u32[]{:S(2)}, u32[]{:S(2)}) collective-permute-start(bf16[128,2048]{1,0:T(8,128)(2,1)S(1)} %collective-permute-done.10.refs_1_), channel_id=1, source_target_pairs={{3,5},{5,7},{6,4},{7,6},{12,14},{13,19},{14,15},{15,13},{16,25},{1... | collective-permute-start | bytes 1572872 | tf_op jit(solution)/shard_map/ppermute | solution.py:414
  38.9 1.3 %add_block.16 = (f32[2,8,128,512]{3,2,1,0:T(8,128)S(1)}, f32[2,8,512]{2,1,0:T(8,128)S(1)}, f32[2,8,512]{2,1,0:T(8,128)S(1)}) custom-call(s32[34]{0:T(128)S(4)} %get-tuple-element.63.info_ref, bf16[128,4096]{1,0:T(8,128)(2,1)S(1)} %fetch_queries.1.q_ref, ...), custom_call_target="tpu_custom_call", output_to_operand_aliasing={{0}: (4, {}), {1}: (5, {}), {2}: (6, {})} | custom-call | flops 1000 | bytes 1024 | tf_op jit(solution)/shard_map/add_block/pallas_call | solution.py:329
  40.4 1.6 %collective-permute-done.7.kv_ref = bf16[128,2048]{1,0:T(8,128)(2,1)S(1)} collective-permute-done((bf16[128,2048]{1,0:T(8,128)(2,1)S(1)}, bf16[128,2048]{1,0:T(8,128)(2,1)S(1)}, u32[]{:S(2)}, u32[]{:S(2)}) %collective-permute-start.7) | collective-permute-done | bytes 524320 | tf_op jit(solution)/shard_map/ppermute | solution.py:414
  42.2 1.5 %collective-permute-done.13.refs_0_ = bf16[128,2048]{1,0:T(8,128)(2,1)S(1)} collective-permute-done((bf16[128,2048]{1,0:T(8,128)(2,1)S(1)}, bf16[128,2048]{1,0:T(8,128)(2,1)S(1)}, u32[]{:S(2)}, u32[]{:S(2)}) %collective-permute-start.13) | collective-permute-done | bytes 524320 | tf_op jit(solution)/shard_map/ppermute | solution.py:434
  43.7 3.9 %collective-permute-done.12.kv_ref.refs_1_ = bf16[128,2048]{1,0:T(8,128)(2,1)S(1)} collective-permute-done((bf16[128,2048]{1,0:T(8,128)(2,1)S(1)}, bf16[128,2048]{1,0:T(8,128)(2,1)S(1)}, u32[]{:S(2)}, u32[]{:S(2)}) %collective-permute-start.12) | collective-permute-done | bytes 524320 | tf_op jit(solution)/shard_map/ppermute | solution.py:414
  47.6 2.4 %last_block.1 = bf16[128,4096]{1,0:T(8,128)(2,1)} custom-call(s32[34]{0:T(128)S(4)} %get-tuple-element.63.info_ref, bf16[128,4096]{1,0:T(8,128)(2,1)S(1)} %fetch_queries.1.q_ref, bf16[128,4608]{1,0:T(8,128)(2,1)S(1)} %collective-permute-done.11.refs_0_, bf16[128,2048]{1,0:T(8,128)(2,1)S(1)} %collective-permute-done.12.kv_ref.refs_1_, ...), custom_call_target="tpu_custom_call" | custom-call | tf_op jit(solution)/shard_map/last_block/pallas_call | solution.py:360
  (20 shorter events, 1.7 us)
Async XLA Ops:
  1.1 6.4 %collective-permute-start.1 = (bf16[128,2048]{1,0:T(8,128)(2,1)S(1)}, bf16[128,2048]{1,0:T(8,128)(2,1)S(1)}, u32[]{:S(2)}, u32[]{:S(2)}) collective-permute-start(bf16[128,2048]{1,0:T(8,128)(2,1)S(1)} %get-tuple-element.111.kv_ref), channel_id=1, source_target_pairs={{0,8},{1,9},{2,10},{3,11},{4,12},{5,13},{6,14},{7,15},{8,0},{9,1},... | collective-permute-start | bytes 1572872 | tf_op jit(solution)/shard_map/ppermute | solution.py:420
  1.2 15.2 %collective-permute-start = (bf16[128,4096]{1,0:T(8,128)(2,1)}, bf16[128,4096]{1,0:T(8,128)(2,1)S(1)}, u32[]{:S(2)}, u32[]{:S(2)}) collective-permute-start(bf16[128,4096]{1,0:T(8,128)(2,1)} %q_ref.1), channel_id=1, source_target_pairs={{0,8},{1,9},{2,10},{3,11},{4,12},{5,13},{6,14},{7,15},{8,0},{9,1},... | collective-permute-start | bytes 3145736 | tf_op jit(solution)/shard_map/ppermute | solution.py:424
  1.7 11.2 %collective-permute-start.3 = (bf16[128,2048]{1,0:T(8,128)(2,1)S(1)}, bf16[128,2048]{1,0:T(8,128)(2,1)}, u32[]{:S(2)}, u32[]{:S(2)}) collective-permute-start(bf16[128,2048]{1,0:T(8,128)(2,1)S(1)} %get-tuple-element.111.kv_ref), channel_id=1, source_target_pairs={{0,1},{1,3},{2,0},{3,5},{5,7},{8,10},{9,8},{10,12},{11,25},{12,14}... | collective-permute-start | bytes 1572872 | tf_op jit(solution)/shard_map/ppermute | solution.py:414
  7.6 11.2 %collective-permute-start.2 = (bf16[128,2048]{1,0:T(8,128)(2,1)S(1)}, bf16[128,2048]{1,0:T(8,128)(2,1)S(1)}, u32[]{:S(2)}, u32[]{:S(2)}) collective-permute-start(bf16[128,2048]{1,0:T(8,128)(2,1)S(1)} %collective-permute-done.1.refs_0_), channel_id=1, source_target_pairs={{0,1},{1,3},{2,16},{3,5},{4,18},{5,7},{6,20},{7,22},{8,10},{9,8},{... | collective-permute-start | bytes 1572872 | tf_op jit(solution)/shard_map/ppermute | solution.py:414
  10.0 13.2 %collective-permute-start.6 = (bf16[128,2048]{1,0:T(8,128)(2,1)S(1)}, bf16[128,2048]{1,0:T(8,128)(2,1)S(1)}, u32[]{:S(2)}, u32[]{:S(2)}) collective-permute-start(bf16[128,2048]{1,0:T(8,128)(2,1)S(1)} %get-tuple-element.111.kv_ref), channel_id=1, source_target_pairs={{26,27},{11,19},{12,20}} | collective-permute-start | bytes 1572872 | tf_op jit(solution)/shard_map/ppermute | solution.py:426
  12.9 11.4 %collective-permute-start.5 = (bf16[128,2048]{1,0:T(8,128)(2,1)}, bf16[128,2048]{1,0:T(8,128)(2,1)S(1)}, u32[]{:S(2)}, u32[]{:S(2)}) collective-permute-start(bf16[128,2048]{1,0:T(8,128)(2,1)} %collective-permute-done.3.refs_1_), channel_id=1, source_target_pairs={{0,1},{1,3},{3,5},{5,7},{7,6},{8,10},{10,12},{12,14},{14,15},{15,2... | collective-permute-start | bytes 1572872 | tf_op jit(solution)/shard_map/ppermute | solution.py:414
  18.7 12.2 %collective-permute-start.4 = (bf16[128,2048]{1,0:T(8,128)(2,1)S(1)}, bf16[128,2048]{1,0:T(8,128)(2,1)S(1)}, u32[]{:S(2)}, u32[]{:S(2)}) collective-permute-start(bf16[128,2048]{1,0:T(8,128)(2,1)S(1)} %collective-permute-done.2.refs_1_), channel_id=1, source_target_pairs={{1,3},{3,5},{5,7},{7,6},{8,10},{10,12},{12,14},{14,15},{16,17},{17... | collective-permute-start | bytes 1572872 | tf_op jit(solution)/shard_map/ppermute | solution.py:414
  24.2 11.6 %collective-permute-start.10 = (bf16[128,2048]{1,0:T(8,128)(2,1)S(1)}, bf16[128,2048]{1,0:T(8,128)(2,1)S(1)}, u32[]{:S(2)}, u32[]{:S(2)}) collective-permute-start(bf16[128,2048]{1,0:T(8,128)(2,1)S(1)} %collective-permute-done.5.refs_1_), channel_id=1, source_target_pairs={{1,3},{3,5},{5,7},{7,6},{10,12},{12,14},{14,15},{15,13},{16,17},{1... | collective-permute-start | bytes 1572872 | tf_op jit(solution)/shard_map/ppermute | solution.py:414
  27.6 12.5 %collective-permute-start.8 = (bf16[128,2048]{1,0:T(8,128)(2,1)}, bf16[128,2048]{1,0:T(8,128)(2,1)S(1)}, u32[]{:S(2)}, u32[]{:S(2)}) collective-permute-start(bf16[128,2048]{1,0:T(8,128)(2,1)} %collective-permute-done.3.refs_1_), channel_id=1, source_target_pairs={{8,16}} | collective-permute-start | bytes 1572872 | tf_op jit(solution)/shard_map/ppermute | solution.py:433
  28.3 11.8 %collective-permute-start.9 = (bf16[128,2048]{1,0:T(8,128)(2,1)S(1)}, bf16[128,2048]{1,0:T(8,128)(2,1)S(1)}, u32[]{:S(2)}, u32[]{:S(2)}) collective-permute-start(bf16[128,2048]{1,0:T(8,128)(2,1)S(1)} %collective-permute-done.2.refs_1_), channel_id=1, source_target_pairs={{21,28}} | collective-permute-start | bytes 1572872 | tf_op jit(solution)/shard_map/ppermute | solution.py:433
  31.0 11.1 %collective-permute-start.7 = (bf16[128,2048]{1,0:T(8,128)(2,1)S(1)}, bf16[128,2048]{1,0:T(8,128)(2,1)S(1)}, u32[]{:S(2)}, u32[]{:S(2)}) collective-permute-start(bf16[128,2048]{1,0:T(8,128)(2,1)S(1)} %collective-permute-done.4.refs_1_), channel_id=1, source_target_pairs={{3,5},{5,7},{6,20},{7,6},{10,12},{12,14},{14,15},{15,13},{16,17},{... | collective-permute-start | bytes 1572872 | tf_op jit(solution)/shard_map/ppermute | solution.py:414
  33.2 10.5 %collective-permute-start.13 = (bf16[128,2048]{1,0:T(8,128)(2,1)S(1)}, bf16[128,2048]{1,0:T(8,128)(2,1)S(1)}, u32[]{:S(2)}, u32[]{:S(2)}) collective-permute-start(bf16[128,2048]{1,0:T(8,128)(2,1)S(1)} %get-tuple-element.111.kv_ref), channel_id=1, source_target_pairs={{8,16},{9,17},{10,18},{13,21},{14,22},{15,23}} | collective-permute-start | bytes 1572872 | tf_op jit(solution)/shard_map/ppermute | solution.py:434
  35.8 11.8 %collective-permute-start.12 = (bf16[128,2048]{1,0:T(8,128)(2,1)S(1)}, bf16[128,2048]{1,0:T(8,128)(2,1)S(1)}, u32[]{:S(2)}, u32[]{:S(2)}) collective-permute-start(bf16[128,2048]{1,0:T(8,128)(2,1)S(1)} %collective-permute-done.10.refs_1_), channel_id=1, source_target_pairs={{3,5},{5,7},{6,4},{7,6},{12,14},{13,19},{14,15},{15,13},{16,25},{1... | collective-permute-start | bytes 1572872 | tf_op jit(solution)/shard_map/ppermute | solution.py:414
  42.2 5.5 %collective-permute-start.11 = (bf16[128,4608]{1,0:T(8,128)(2,1)S(1)}, bf16[128,4608]{1,0:T(8,128)(2,1)S(1)}, u32[]{:S(2)}, u32[]{:S(2)}) collective-permute-start(bf16[128,4608]{1,0:T(8,128)(2,1)S(1)} %get-tuple-element.109), channel_id=1, source_target_pairs={{0,8},{1,9},{2,10},{3,11},{4,12},{5,13},{6,14},{7,15},{8,0},{9,1},... | collective-permute-start | bytes 3538952 | tf_op jit(solution)/shard_map/ppermute | solution.py:444

commit v6 on v5

--- a/solution.py
+++ b/solution.py
@@ -210,9 +210,6 @@
     base = info_ref[0] * rows
     bias = mask_bias(info_ref, n_docs, base, base, rows)
     attend_block(sizes, head_of(q_ref), kv_ref, bias, state, OWN, True)
-    if state[0].shape[0] > 1:
-        for ref, value in zip(state, (0.0, NEG, 0.0)):
-            ref[MATE] = jnp.full(ref.shape[1:], value, jnp.float32)
 
 
 def add_block(sizes, n_docs, slot, info_ref, q_ref, qm_ref, kv_ref, state):
@@ -231,8 +228,11 @@
         attend_block(sizes, q_of, kv_ref, bias, state, use, False)
 
 
-def add_kernel(sizes, n_docs, slot, mated, info_ref, q_ref, *refs):
+def add_kernel(sizes, n_docs, slot, mated, clear, info_ref, q_ref, *refs):
     qm_ref, refs = (refs[0], refs[1:]) if mated else (None, refs)
+    if clear:
+        for ref, value in zip(refs[4:], (0.0, NEG, 0.0)):
+            ref[MATE] = jnp.full(ref.shape[1:], value, jnp.float32)
     add_block(sizes, n_docs, slot, info_ref, q_ref, qm_ref, refs[0], refs[4:])
 
 
@@ -344,9 +344,9 @@
     def own(q, kv):
         call(functools.partial(own_kernel, sizes, n_docs), [q, kv], [], "own_block")
 
-    def add(slot, q, qm, kv):
+    def add(slot, q, qm, kv, clear=False):
         qs = [q] if qm is None else [q, qm]
-        kernel = functools.partial(add_kernel, sizes, n_docs, slot, qm is not None)
+        kernel = functools.partial(add_kernel, sizes, n_docs, slot, qm is not None, clear)
         call(kernel, qs + [kv], [], "add_block")
 
     def part(slot, q, qm, kv):
@@ -425,7 +425,7 @@
     beside = [[(e, q)] for _, q, e in straight]
     near = [lax.ppermute(kv, AXES, beside[0] + busy)]
     u2 = send(after(u1), "own", 2)
-    add(7, q, None, kvm)
+    add(7, q, None, kvm, clear=True)
     add(0, q, qm, u1)
     w2 = send(after(w1), "mate", 2)
     add(1, q, qm, w1)
@@ -438,11 +438,11 @@
     add(3, q, qm, w2)
     u4 = send(after(u3), "own", 4)
     add(4, q, qm, u3)
-    add(10, q, None, near[1])
     add(11, q, None, near[2])
     mine = part(5, q, qm, w3)
     theirs = lax.ppermute(mine, AXES, mates)
     add(8, q, None, kv8)
+    add(10, q, None, near[1])
     touch(u4)
     return last(6, q, [theirs], u4)
 

time: 50.6 us -> 50.4 us (level)
  the two profiles are of different devices: /device:TPU:22 before, /device:TPU:16 now
where the time goes in v6:
time: 50.4 us; the launch traced here: 49.9 us
  starting transfers between devices  32.2 us (64%)
  waiting for transfers between devices  9.9 us (20%)
  Pallas kernels  7.39 us (15%)
    ppermute x1, starting transfers between devices, ring_shards(): theirs = lax.ppermute(mine, AXES, mates)  19.1 us
    ppermute x7, waiting for transfers between devices, send(): lax.ppermute(block, AXES, sorted(((e, d) for d, (e, _) in route[op, step]...  9.88 us
    ppermute x7, starting transfers between devices, send(): lax.ppermute(block, AXES, sorted(((e, d) for d, (e, _) in route[op, step]...  9.73 us
    pallas_call x13, Pallas kernels, call(): pl.pallas_call(kernel, out_shape=out, in_specs=[smem] + [vmem] * (len(arr...  2.69 us
    pallas_call x1, Pallas kernels, last(): pl.pallas_call(functools.partial(last_kernel, sizes, n_docs, slot, mated)...  2.35 us
    pallas_call x1, Pallas kernels, fetched(): pl.pallas_call(fetch_kernel, out_shape=pltpu.VMEM(queries.shape, queries....  1.23 us
    pallas_call x1, Pallas kernels, pack(): pl.pallas_call(functools.partial(pack_kernel, rows, n_docs, table is not...  1.12 us
  transfers between devices with their start and end apart: 14, of which 2 were waited for; matrix products, arithmetic and copies ran while one was open for 0% of the time, Pallas kernels for 8%

profile of v6, /device:TPU:16, one launch (start us, length us, event | category | flops | bytes accessed | tf_op | source)
XLA Modules:
  0.0 49.9 jit_solution(6876042541345733282)
XLA Ops:
  0.0 1.1 %pack_keys_values.1 = (bf16[128,2048]{1,0:T(8,128)(2,1)S(1)}, s32[34]{0:T(128)S(4)}) custom-call(s32[8]{0:T(128)} %refs_0_.1, s32[8]{0:T(128)} %refs_1_.1, s32[32,25]{1,0:T(8,128)} %constant.2.clone.refs_2_, bf16[128,1024]{1,0:T(8,128)(2,1)} %refs_3_.1, bf16[128,1024]{1,0:T(8,128)(2,1)} %refs_4_.1), custom_call_target="tpu_custom_call" | custom-call | tf_op jit(solution)/shard_map/pack_keys_values/pallas_call | solution.py:385
  1.1 0.1 collective-permute-start.1
  1.2 0.5 collective-permute-start
  1.7 1.5 %collective-permute-start.3 = (bf16[128,2048]{1,0:T(8,128)(2,1)S(1)}, bf16[128,2048]{1,0:T(8,128)(2,1)}, u32[]{:S(2)}, u32[]{:S(2)}) collective-permute-start(bf16[128,2048]{1,0:T(8,128)(2,1)S(1)} %get-tuple-element.108.kv_ref), channel_id=1, source_target_pairs={{0,1},{1,3},{2,0},{3,5},{5,7},{8,10},{9,8},{10,12},{11,25},{12,14}... | collective-permute-start | bytes 1572872 | tf_op jit(solution)/shard_map/ppermute | solution.py:414
  3.2 1.2 %fetch_queries.1.q_ref = bf16[128,4096]{1,0:T(8,128)(2,1)S(1)} custom-call(bf16[128,4096]{1,0:T(8,128)(2,1)} %q_ref.1), custom_call_target="tpu_custom_call" | custom-call | tf_op jit(solution)/shard_map/fetch_queries/pallas_call | solution.py:198
  4.4 1.1 %own_block.1 = (f32[2,8,128,512]{3,2,1,0:T(8,128)S(1)}, f32[2,8,512]{2,1,0:T(8,128)S(1)}, f32[2,8,512]{2,1,0:T(8,128)S(1)}) custom-call(s32[34]{0:T(128)S(4)} %get-tuple-element.63.info_ref, bf16[128,4096]{1,0:T(8,128)(2,1)S(1)} %fetch_queries.1.q_ref, bf16[128,2048]{1,0:T(8,128)(2,1)S(1)} %get-tuple-element.108.kv_ref), custom_call_target="tpu_custom_call" | custom-call | flops 1000 | bytes 1024 | tf_op jit(solution)/shard_map/own_block/pallas_call | solution.py:329
  5.5 0.0 collective-permute-done.1.refs_0_
  5.5 4.2 %collective-permute-start.2 = (bf16[128,2048]{1,0:T(8,128)(2,1)S(1)}, bf16[128,2048]{1,0:T(8,128)(2,1)S(1)}, u32[]{:S(2)}, u32[]{:S(2)}) collective-permute-start(bf16[128,2048]{1,0:T(8,128)(2,1)S(1)} %collective-permute-done.1.refs_0_), channel_id=1, source_target_pairs={{0,1},{1,3},{2,16},{3,5},{4,18},{5,7},{6,20},{7,22},{8,10},{9,8},{... | collective-permute-start | bytes 1572872 | tf_op jit(solution)/shard_map/ppermute | solution.py:414
  9.7 0.7 %collective-permute-start.6 = (bf16[128,2048]{1,0:T(8,128)(2,1)S(1)}, bf16[128,2048]{1,0:T(8,128)(2,1)S(1)}, u32[]{:S(2)}, u32[]{:S(2)}) collective-permute-start(bf16[128,2048]{1,0:T(8,128)(2,1)S(1)} %get-tuple-element.108.kv_ref), channel_id=1, source_target_pairs={{26,27},{11,19},{12,20}} | collective-permute-start | bytes 1572872 | tf_op jit(solution)/shard_map/ppermute | solution.py:426
  10.5 0.7 %collective-permute-start.5 = (bf16[128,2048]{1,0:T(8,128)(2,1)}, bf16[128,2048]{1,0:T(8,128)(2,1)S(1)}, u32[]{:S(2)}, u32[]{:S(2)}) collective-permute-start(bf16[128,2048]{1,0:T(8,128)(2,1)} %collective-permute-done.3.refs_1_), channel_id=1, source_target_pairs={{0,1},{1,3},{3,5},{5,7},{7,6},{8,10},{10,12},{12,14},{14,15},{15,2... | collective-permute-start | bytes 1572872 | tf_op jit(solution)/shard_map/ppermute | solution.py:414
  11.2 0.1 add_block.10
  11.3 1.0 %add_block.11 = (f32[2,8,128,512]{3,2,1,0:T(8,128)S(1)}, f32[2,8,512]{2,1,0:T(8,128)S(1)}, f32[2,8,512]{2,1,0:T(8,128)S(1)}) custom-call(s32[34]{0:T(128)S(4)} %get-tuple-element.63.info_ref, bf16[128,4096]{1,0:T(8,128)(2,1)S(1)} %fetch_queries.1.q_ref, ...), custom_call_target="tpu_custom_call", output_to_operand_aliasing={{0}: (4, {}), {1}: (5, {}), {2}: (6, {})} | custom-call | flops 1000 | bytes 1024 | tf_op jit(solution)/shard_map/add_block/pallas_call | solution.py:329
  12.4 4.0 %collective-permute-done.2.refs_1_ = bf16[128,2048]{1,0:T(8,128)(2,1)S(1)} collective-permute-done((bf16[128,2048]{1,0:T(8,128)(2,1)S(1)}, bf16[128,2048]{1,0:T(8,128)(2,1)S(1)}, u32[]{:S(2)}, u32[]{:S(2)}) %collective-permute-start.2) | collective-permute-done | bytes 524320 | tf_op jit(solution)/shard_map/ppermute | solution.py:414
  16.4 0.7 %collective-permute-start.4 = (bf16[128,2048]{1,0:T(8,128)(2,1)S(1)}, bf16[128,2048]{1,0:T(8,128)(2,1)S(1)}, u32[]{:S(2)}, u32[]{:S(2)}) collective-permute-start(bf16[128,2048]{1,0:T(8,128)(2,1)S(1)} %collective-permute-done.2.refs_1_), channel_id=1, source_target_pairs={{1,3},{3,5},{5,7},{7,6},{8,10},{10,12},{12,14},{14,15},{16,17},{17... | collective-permute-start | bytes 1572872 | tf_op jit(solution)/shard_map/ppermute | solution.py:414
  17.1 0.7 %collective-permute-start.9 = (bf16[128,2048]{1,0:T(8,128)(2,1)S(1)}, bf16[128,2048]{1,0:T(8,128)(2,1)S(1)}, u32[]{:S(2)}, u32[]{:S(2)}) collective-permute-start(bf16[128,2048]{1,0:T(8,128)(2,1)S(1)} %collective-permute-done.5.refs_1_), channel_id=1, source_target_pairs={{1,3},{3,5},{5,7},{7,6},{10,12},{12,14},{14,15},{15,13},{16,17},{1... | collective-permute-start | bytes 1572872 | tf_op jit(solution)/shard_map/ppermute | solution.py:414
  17.8 0.7 %collective-permute-start.8 = (bf16[128,2048]{1,0:T(8,128)(2,1)}, bf16[128,2048]{1,0:T(8,128)(2,1)S(1)}, u32[]{:S(2)}, u32[]{:S(2)}) collective-permute-start(bf16[128,2048]{1,0:T(8,128)(2,1)} %collective-permute-done.3.refs_1_), channel_id=1, source_target_pairs={{8,16}} | collective-permute-start | bytes 1572872 | tf_op jit(solution)/shard_map/ppermute | solution.py:433
  18.6 0.7 %collective-permute-start.7 = (bf16[128,2048]{1,0:T(8,128)(2,1)S(1)}, bf16[128,2048]{1,0:T(8,128)(2,1)S(1)}, u32[]{:S(2)}, u32[]{:S(2)}) collective-permute-start(bf16[128,2048]{1,0:T(8,128)(2,1)S(1)} %collective-permute-done.4.refs_1_), channel_id=1, source_target_pairs={{3,5},{5,7},{6,20},{7,6},{10,12},{12,14},{14,15},{15,13},{16,17},{... | collective-permute-start | bytes 1572872 | tf_op jit(solution)/shard_map/ppermute | solution.py:414
  19.3 0.7 %collective-permute-start.13 = (bf16[128,2048]{1,0:T(8,128)(2,1)S(1)}, bf16[128,2048]{1,0:T(8,128)(2,1)S(1)}, u32[]{:S(2)}, u32[]{:S(2)}) collective-permute-start(bf16[128,2048]{1,0:T(8,128)(2,1)S(1)} %get-tuple-element.108.kv_ref), channel_id=1, source_target_pairs={{8,16},{9,17},{10,18},{13,21},{14,22},{15,23}} | collective-permute-start | bytes 1572872 | tf_op jit(solution)/shard_map/ppermute | solution.py:434
  20.0 0.7 %collective-permute-start.12 = (bf16[128,2048]{1,0:T(8,128)(2,1)S(1)}, bf16[128,2048]{1,0:T(8,128)(2,1)S(1)}, u32[]{:S(2)}, u32[]{:S(2)}) collective-permute-start(bf16[128,2048]{1,0:T(8,128)(2,1)S(1)} %collective-permute-done.2.refs_1_), channel_id=1, source_target_pairs={{21,28}} | collective-permute-start | bytes 1572872 | tf_op jit(solution)/shard_map/ppermute | solution.py:433
  20.7 1.3 %collective-permute-start.11 = (bf16[128,2048]{1,0:T(8,128)(2,1)S(1)}, bf16[128,2048]{1,0:T(8,128)(2,1)S(1)}, u32[]{:S(2)}, u32[]{:S(2)}) collective-permute-start(bf16[128,2048]{1,0:T(8,128)(2,1)S(1)} %collective-permute-done.9.refs_1_), channel_id=1, source_target_pairs={{3,5},{5,7},{6,4},{7,6},{12,14},{13,19},{14,15},{15,13},{16,25},{1... | collective-permute-start | bytes 1572872 | tf_op jit(solution)/shard_map/ppermute | solution.py:414
  22.1 0.3 mate_part.1
  22.4 19.1 %collective-permute-start.10 = (bf16[128,4608]{1,0:T(8,128)(2,1)S(1)}, bf16[128,4608]{1,0:T(8,128)(2,1)S(1)}, u32[]{:S(2)}, u32[]{:S(2)}) collective-permute-start(bf16[128,4608]{1,0:T(8,128)(2,1)S(1)} %get-tuple-element.105), channel_id=1, source_target_pairs={{0,8},{1,9},{2,10},{3,11},{4,12},{5,13},{6,14},{7,15},{8,0},{9,1},... | collective-permute-start | bytes 3538952 | tf_op jit(solution)/shard_map/ppermute | solution.py:443
  41.5 5.8 %collective-permute-done.11.kv_ref.refs_1_ = bf16[128,2048]{1,0:T(8,128)(2,1)S(1)} collective-permute-done((bf16[128,2048]{1,0:T(8,128)(2,1)S(1)}, bf16[128,2048]{1,0:T(8,128)(2,1)S(1)}, u32[]{:S(2)}, u32[]{:S(2)}) %collective-permute-start.11) | collective-permute-done | bytes 524320 | tf_op jit(solution)/shard_map/ppermute | solution.py:414
  47.4 2.4 %last_block.1 = bf16[128,4096]{1,0:T(8,128)(2,1)} custom-call(s32[34]{0:T(128)S(4)} %get-tuple-element.63.info_ref, bf16[128,4096]{1,0:T(8,128)(2,1)S(1)} %fetch_queries.1.q_ref, bf16[128,4608]{1,0:T(8,128)(2,1)S(1)} %collective-permute-done.10.refs_0_, bf16[128,2048]{1,0:T(8,128)(2,1)S(1)} %collective-permute-done.11.kv_ref.refs_1_, ...), custom_call_target="tpu_custom_call" | custom-call | tf_op jit(solution)/shard_map/last_block/pallas_call | solution.py:360
  (20 shorter events, 0.1 us)
Async XLA Ops:
  1.1 4.4 %collective-permute-start.1 = (bf16[128,2048]{1,0:T(8,128)(2,1)S(1)}, bf16[128,2048]{1,0:T(8,128)(2,1)S(1)}, u32[]{:S(2)}, u32[]{:S(2)}) collective-permute-start(bf16[128,2048]{1,0:T(8,128)(2,1)S(1)} %get-tuple-element.108.kv_ref), channel_id=1, source_target_pairs={{0,8},{1,9},{2,10},{3,11},{4,12},{5,13},{6,14},{7,15},{8,0},{9,1},... | collective-permute-start | bytes 1572872 | tf_op jit(solution)/shard_map/ppermute | solution.py:420
  1.2 10.1 %collective-permute-start = (bf16[128,4096]{1,0:T(8,128)(2,1)}, bf16[128,4096]{1,0:T(8,128)(2,1)S(1)}, u32[]{:S(2)}, u32[]{:S(2)}) collective-permute-start(bf16[128,4096]{1,0:T(8,128)(2,1)} %q_ref.1), channel_id=1, source_target_pairs={{0,8},{1,9},{2,10},{3,11},{4,12},{5,13},{6,14},{7,15},{8,0},{9,1},... | collective-permute-start | bytes 3145736 | tf_op jit(solution)/shard_map/ppermute | solution.py:424
  1.7 8.7 %collective-permute-start.3 = (bf16[128,2048]{1,0:T(8,128)(2,1)S(1)}, bf16[128,2048]{1,0:T(8,128)(2,1)}, u32[]{:S(2)}, u32[]{:S(2)}) collective-permute-start(bf16[128,2048]{1,0:T(8,128)(2,1)S(1)} %get-tuple-element.108.kv_ref), channel_id=1, source_target_pairs={{0,1},{1,3},{2,0},{3,5},{5,7},{8,10},{9,8},{10,12},{11,25},{12,14}... | collective-permute-start | bytes 1572872 | tf_op jit(solution)/shard_map/ppermute | solution.py:414
  5.5 10.9 %collective-permute-start.2 = (bf16[128,2048]{1,0:T(8,128)(2,1)S(1)}, bf16[128,2048]{1,0:T(8,128)(2,1)S(1)}, u32[]{:S(2)}, u32[]{:S(2)}) collective-permute-start(bf16[128,2048]{1,0:T(8,128)(2,1)S(1)} %collective-permute-done.1.refs_0_), channel_id=1, source_target_pairs={{0,1},{1,3},{2,16},{3,5},{4,18},{5,7},{6,20},{7,22},{8,10},{9,8},{... | collective-permute-start | bytes 1572872 | tf_op jit(solution)/shard_map/ppermute | solution.py:414
  9.7 7.4 %collective-permute-start.6 = (bf16[128,2048]{1,0:T(8,128)(2,1)S(1)}, bf16[128,2048]{1,0:T(8,128)(2,1)S(1)}, u32[]{:S(2)}, u32[]{:S(2)}) collective-permute-start(bf16[128,2048]{1,0:T(8,128)(2,1)S(1)} %get-tuple-element.108.kv_ref), channel_id=1, source_target_pairs={{26,27},{11,19},{12,20}} | collective-permute-start | bytes 1572872 | tf_op jit(solution)/shard_map/ppermute | solution.py:426
  10.5 6.7 %collective-permute-start.5 = (bf16[128,2048]{1,0:T(8,128)(2,1)}, bf16[128,2048]{1,0:T(8,128)(2,1)S(1)}, u32[]{:S(2)}, u32[]{:S(2)}) collective-permute-start(bf16[128,2048]{1,0:T(8,128)(2,1)} %collective-permute-done.3.refs_1_), channel_id=1, source_target_pairs={{0,1},{1,3},{3,5},{5,7},{7,6},{8,10},{10,12},{12,14},{14,15},{15,2... | collective-permute-start | bytes 1572872 | tf_op jit(solution)/shard_map/ppermute | solution.py:414
  16.4 2.2 %collective-permute-start.4 = (bf16[128,2048]{1,0:T(8,128)(2,1)S(1)}, bf16[128,2048]{1,0:T(8,128)(2,1)S(1)}, u32[]{:S(2)}, u32[]{:S(2)}) collective-permute-start(bf16[128,2048]{1,0:T(8,128)(2,1)S(1)} %collective-permute-done.2.refs_1_), channel_id=1, source_target_pairs={{1,3},{3,5},{5,7},{7,6},{8,10},{10,12},{12,14},{14,15},{16,17},{17... | collective-permute-start | bytes 1572872 | tf_op jit(solution)/shard_map/ppermute | solution.py:414
  17.1 3.6 %collective-permute-start.9 = (bf16[128,2048]{1,0:T(8,128)(2,1)S(1)}, bf16[128,2048]{1,0:T(8,128)(2,1)S(1)}, u32[]{:S(2)}, u32[]{:S(2)}) collective-permute-start(bf16[128,2048]{1,0:T(8,128)(2,1)S(1)} %collective-permute-done.5.refs_1_), channel_id=1, source_target_pairs={{1,3},{3,5},{5,7},{7,6},{10,12},{12,14},{14,15},{15,13},{16,17},{1... | collective-permute-start | bytes 1572872 | tf_op jit(solution)/shard_map/ppermute | solution.py:414
  17.8 4.2 %collective-permute-start.8 = (bf16[128,2048]{1,0:T(8,128)(2,1)}, bf16[128,2048]{1,0:T(8,128)(2,1)S(1)}, u32[]{:S(2)}, u32[]{:S(2)}) collective-permute-start(bf16[128,2048]{1,0:T(8,128)(2,1)} %collective-permute-done.3.refs_1_), channel_id=1, source_target_pairs={{8,16}} | collective-permute-start | bytes 1572872 | tf_op jit(solution)/shard_map/ppermute | solution.py:433
  18.6 3.5 %collective-permute-start.7 = (bf16[128,2048]{1,0:T(8,128)(2,1)S(1)}, bf16[128,2048]{1,0:T(8,128)(2,1)S(1)}, u32[]{:S(2)}, u32[]{:S(2)}) collective-permute-start(bf16[128,2048]{1,0:T(8,128)(2,1)S(1)} %collective-permute-done.4.refs_1_), channel_id=1, source_target_pairs={{3,5},{5,7},{6,20},{7,6},{10,12},{12,14},{14,15},{15,13},{16,17},{... | collective-permute-start | bytes 1572872 | tf_op jit(solution)/shard_map/ppermute | solution.py:414
  19.3 22.2 %collective-permute-start.13 = (bf16[128,2048]{1,0:T(8,128)(2,1)S(1)}, bf16[128,2048]{1,0:T(8,128)(2,1)S(1)}, u32[]{:S(2)}, u32[]{:S(2)}) collective-permute-start(bf16[128,2048]{1,0:T(8,128)(2,1)S(1)} %get-tuple-element.108.kv_ref), channel_id=1, source_target_pairs={{8,16},{9,17},{10,18},{13,21},{14,22},{15,23}} | collective-permute-start | bytes 1572872 | tf_op jit(solution)/shard_map/ppermute | solution.py:434
  20.0 21.5 %collective-permute-start.12 = (bf16[128,2048]{1,0:T(8,128)(2,1)S(1)}, bf16[128,2048]{1,0:T(8,128)(2,1)S(1)}, u32[]{:S(2)}, u32[]{:S(2)}) collective-permute-start(bf16[128,2048]{1,0:T(8,128)(2,1)S(1)} %collective-permute-done.2.refs_1_), channel_id=1, source_target_pairs={{21,28}} | collective-permute-start | bytes 1572872 | tf_op jit(solution)/shard_map/ppermute | solution.py:433
  20.7 26.7 %collective-permute-start.11 = (bf16[128,2048]{1,0:T(8,128)(2,1)S(1)}, bf16[128,2048]{1,0:T(8,128)(2,1)S(1)}, u32[]{:S(2)}, u32[]{:S(2)}) collective-permute-start(bf16[128,2048]{1,0:T(8,128)(2,1)S(1)} %collective-permute-done.9.refs_1_), channel_id=1, source_target_pairs={{3,5},{5,7},{6,4},{7,6},{12,14},{13,19},{14,15},{15,13},{16,25},{1... | collective-permute-start | bytes 1572872 | tf_op jit(solution)/shard_map/ppermute | solution.py:414
  22.4 25.0 %collective-permute-start.10 = (bf16[128,4608]{1,0:T(8,128)(2,1)S(1)}, bf16[128,4608]{1,0:T(8,128)(2,1)S(1)}, u32[]{:S(2)}, u32[]{:S(2)}) collective-permute-start(bf16[128,4608]{1,0:T(8,128)(2,1)S(1)} %get-tuple-element.105), channel_id=1, source_target_pairs={{0,8},{1,9},{2,10},{3,11},{4,12},{5,13},{6,14},{7,15},{8,0},{9,1},... | collective-permute-start | bytes 3538952 | tf_op jit(solution)/shard_map/ppermute | solution.py:443

commit v7 on v5

--- a/solution.py
+++ b/solution.py
@@ -427,10 +427,11 @@
     u2 = send(after(u1), "own", 2)
     add(7, q, None, kvm)
     add(0, q, qm, u1)
+    near2 = lax.ppermute(after(u1), AXES, beside[2])
     w2 = send(after(w1), "mate", 2)
     add(1, q, qm, w1)
     add(9, q, None, near[0])
-    near += [lax.ppermute(after(w1), AXES, beside[1]), lax.ppermute(u1, AXES, beside[2])]
+    near += [lax.ppermute(after(w1), AXES, beside[1])]
     kv8 = lax.ppermute(after(kv), AXES, [x for x in eight_back if x not in busy])
     u3 = send(after(u2), "own", 3)
     add(2, q, qm, u2)
@@ -438,11 +439,11 @@
     add(3, q, qm, w2)
     u4 = send(after(u3), "own", 4)
     add(4, q, qm, u3)
-    add(10, q, None, near[1])
-    add(11, q, None, near[2])
+    add(11, q, None, near2)
     mine = part(5, q, qm, w3)
     theirs = lax.ppermute(mine, AXES, mates)
     add(8, q, None, kv8)
+    add(10, q, None, near[1])
     touch(u4)
     return last(6, q, [theirs], u4)
 

time: 50.6 us -> 50.9 us (level)
  waiting for transfers between devices: 10.3 us -> 11.2 us
    ppermute x1, waiting for transfers between devices: 1.51 us -> 2.44 us  [ring_shards(): lax.ppermute(after(kv), AXES, [x for x in eight_back if x not in busy])]
  transfers between devices with their start and end apart: 14 -> 14, of which waited for: 5 -> 6; matrix products, arithmetic and copies ran while one was open for 0% -> 0% of each run, Pallas kernels for 20% -> 22%
where the time goes in v7:
time: 50.9 us; the launch traced here: 50.8 us
  starting transfers between devices  25.8 us (51%)
  Pallas kernels  13.4 us (26%)
  waiting for transfers between devices  11.2 us (22%)
    ppermute x7, starting transfers between devices, send(): lax.ppermute(block, AXES, sorted(((e, d) for d, (e, _) in route[op, step]...  21.2 us
    ppermute x7, waiting for transfers between devices, send(): lax.ppermute(block, AXES, sorted(((e, d) for d, (e, _) in route[op, step]...  8.71 us
    pallas_call x13, Pallas kernels, call(): pl.pallas_call(kernel, out_shape=out, in_specs=[smem] + [vmem] * (len(arr...  8.69 us
    ppermute x1, waiting for transfers between devices, ring_shards(): lax.ppermute(after(kv), AXES, [x for x in eight_back if x not in busy])  2.44 us
    pallas_call x1, Pallas kernels, last(): pl.pallas_call(functools.partial(last_kernel, sizes, n_docs, slot, mated)...  2.35 us
    ppermute x1, starting transfers between devices, ring_shards(): near += [lax.ppermute(after(w1), AXES, beside[1])]  1.32 us
    ppermute x1, starting transfers between devices, ring_shards(): lax.ppermute(after(kv), AXES, [x for x in eight_back if x not in busy])  1.29 us
    pallas_call x1, Pallas kernels, fetched(): pl.pallas_call(fetch_kernel, out_shape=pltpu.VMEM(queries.shape, queries....  1.24 us
  transfers between devices with their start and end apart: 14, of which 6 were waited for; matrix products, arithmetic and copies ran while one was open for 0% of the time, Pallas kernels for 22%

profile of v7, /device:TPU:22, one launch (start us, length us, event | category | flops | bytes accessed | tf_op | source)
XLA Modules:
  0.0 50.8 jit_solution(1737860316040932088)
XLA Ops:
  0.0 1.1 %pack_keys_values.1 = (bf16[128,2048]{1,0:T(8,128)(2,1)S(1)}, s32[34]{0:T(128)S(4)}) custom-call(s32[8]{0:T(128)} %refs_0_.1, s32[8]{0:T(128)} %refs_1_.1, s32[32,25]{1,0:T(8,128)} %constant.2.clone.refs_2_, bf16[128,1024]{1,0:T(8,128)(2,1)} %refs_3_.1, bf16[128,1024]{1,0:T(8,128)(2,1)} %refs_4_.1), custom_call_target="tpu_custom_call" | custom-call | tf_op jit(solution)/shard_map/pack_keys_values/pallas_call | solution.py:385
  1.7 3.5 %collective-permute-start.3 = (bf16[128,2048]{1,0:T(8,128)(2,1)S(1)}, bf16[128,2048]{1,0:T(8,128)(2,1)}, u32[]{:S(2)}, u32[]{:S(2)}) collective-permute-start(bf16[128,2048]{1,0:T(8,128)(2,1)S(1)} %get-tuple-element.112.kv_ref), channel_id=1, source_target_pairs={{0,1},{1,3},{2,0},{3,5},{5,7},{8,10},{9,8},{10,12},{11,25},{12,14}... | collective-permute-start | bytes 1572872 | tf_op jit(solution)/shard_map/ppermute | solution.py:414
  5.2 1.2 %fetch_queries.1.q_ref = bf16[128,4096]{1,0:T(8,128)(2,1)S(1)} custom-call(bf16[128,4096]{1,0:T(8,128)(2,1)} %q_ref.1), custom_call_target="tpu_custom_call" | custom-call | tf_op jit(solution)/shard_map/fetch_queries/pallas_call | solution.py:198
  6.4 1.1 %own_block.1 = (f32[2,8,128,512]{3,2,1,0:T(8,128)S(1)}, f32[2,8,512]{2,1,0:T(8,128)S(1)}, f32[2,8,512]{2,1,0:T(8,128)S(1)}) custom-call(s32[34]{0:T(128)S(4)} %get-tuple-element.65.info_ref, bf16[128,4096]{1,0:T(8,128)(2,1)S(1)} %fetch_queries.1.q_ref, bf16[128,2048]{1,0:T(8,128)(2,1)S(1)} %get-tuple-element.112.kv_ref), custom_call_target="tpu_custom_call" | custom-call | flops 1000 | bytes 1024 | tf_op jit(solution)/shard_map/own_block/pallas_call | solution.py:329
  7.6 2.4 %collective-permute-start.2 = (bf16[128,2048]{1,0:T(8,128)(2,1)S(1)}, bf16[128,2048]{1,0:T(8,128)(2,1)S(1)}, u32[]{:S(2)}, u32[]{:S(2)}) collective-permute-start(bf16[128,2048]{1,0:T(8,128)(2,1)S(1)} %collective-permute-done.1.refs_0_), channel_id=1, source_target_pairs={{0,1},{1,3},{2,16},{3,5},{4,18},{5,7},{6,20},{7,22},{8,10},{9,8},{... | collective-permute-start | bytes 1572872 | tf_op jit(solution)/shard_map/ppermute | solution.py:414
  10.0 0.7 %collective-permute-start.6 = (bf16[128,2048]{1,0:T(8,128)(2,1)S(1)}, bf16[128,2048]{1,0:T(8,128)(2,1)S(1)}, u32[]{:S(2)}, u32[]{:S(2)}) collective-permute-start(bf16[128,2048]{1,0:T(8,128)(2,1)S(1)} %get-tuple-element.112.kv_ref), channel_id=1, source_target_pairs={{26,27},{11,19},{12,20}} | collective-permute-start | bytes 1572872 | tf_op jit(solution)/shard_map/ppermute | solution.py:426
  10.7 2.2 %collective-permute-done.3.refs_1_ = bf16[128,2048]{1,0:T(8,128)(2,1)} collective-permute-done((bf16[128,2048]{1,0:T(8,128)(2,1)S(1)}, bf16[128,2048]{1,0:T(8,128)(2,1)}, u32[]{:S(2)}, u32[]{:S(2)}) %collective-permute-start.3) | collective-permute-done | bytes 524320 | tf_op jit(solution)/shard_map/ppermute | solution.py:414
  12.9 3.5 %collective-permute-start.5 = (bf16[128,2048]{1,0:T(8,128)(2,1)}, bf16[128,2048]{1,0:T(8,128)(2,1)S(1)}, u32[]{:S(2)}, u32[]{:S(2)}) collective-permute-start(bf16[128,2048]{1,0:T(8,128)(2,1)} %collective-permute-done.3.refs_1_), channel_id=1, source_target_pairs={{0,1},{1,3},{3,5},{5,7},{7,6},{8,10},{10,12},{12,14},{14,15},{15,2... | collective-permute-start | bytes 1572872 | tf_op jit(solution)/shard_map/ppermute | solution.py:414
  16.4 2.3 %add_block.11 = (f32[2,8,128,512]{3,2,1,0:T(8,128)S(1)}, f32[2,8,512]{2,1,0:T(8,128)S(1)}, f32[2,8,512]{2,1,0:T(8,128)S(1)}) custom-call(s32[34]{0:T(128)S(4)} %get-tuple-element.65.info_ref, bf16[128,4096]{1,0:T(8,128)(2,1)S(1)} %fetch_queries.1.q_ref, ...), custom_call_target="tpu_custom_call", output_to_operand_aliasing={{0}: (4, {}), {1}: (5, {}), {2}: (6, {})} | custom-call | flops 1000 | bytes 1024 | tf_op jit(solution)/shard_map/add_block/pallas_call | solution.py:329
  18.7 3.1 %collective-permute-start.4 = (bf16[128,2048]{1,0:T(8,128)(2,1)S(1)}, bf16[128,2048]{1,0:T(8,128)(2,1)S(1)}, u32[]{:S(2)}, u32[]{:S(2)}) collective-permute-start(bf16[128,2048]{1,0:T(8,128)(2,1)S(1)} %collective-permute-done.2.refs_1_), channel_id=1, source_target_pairs={{1,3},{3,5},{5,7},{7,6},{8,10},{10,12},{12,14},{14,15},{16,17},{17... | collective-permute-start | bytes 1572872 | tf_op jit(solution)/shard_map/ppermute | solution.py:414
  21.9 1.3 %add_block.12 = (f32[2,8,128,512]{3,2,1,0:T(8,128)S(1)}, f32[2,8,512]{2,1,0:T(8,128)S(1)}, f32[2,8,512]{2,1,0:T(8,128)S(1)}) custom-call(s32[34]{0:T(128)S(4)} %get-tuple-element.65.info_ref, bf16[128,4096]{1,0:T(8,128)(2,1)S(1)} %fetch_queries.1.q_ref, ...), custom_call_target="tpu_custom_call", output_to_operand_aliasing={{0}: (4, {}), {1}: (5, {}), {2}: (6, {})} | custom-call | flops 1000 | bytes 1024 | tf_op jit(solution)/shard_map/add_block/pallas_call | solution.py:329
  23.2 1.1 %collective-permute-done.5.refs_1_ = bf16[128,2048]{1,0:T(8,128)(2,1)S(1)} collective-permute-done((bf16[128,2048]{1,0:T(8,128)(2,1)}, bf16[128,2048]{1,0:T(8,128)(2,1)S(1)}, u32[]{:S(2)}, u32[]{:S(2)}) %collective-permute-start.5) | collective-permute-done | bytes 524320 | tf_op jit(solution)/shard_map/ppermute | solution.py:414
  24.2 3.4 %collective-permute-start.9 = (bf16[128,2048]{1,0:T(8,128)(2,1)S(1)}, bf16[128,2048]{1,0:T(8,128)(2,1)S(1)}, u32[]{:S(2)}, u32[]{:S(2)}) collective-permute-start(bf16[128,2048]{1,0:T(8,128)(2,1)S(1)} %collective-permute-done.5.refs_1_), channel_id=1, source_target_pairs={{1,3},{3,5},{5,7},{7,6},{10,12},{12,14},{14,15},{15,13},{16,17},{1... | collective-permute-start | bytes 1572872 | tf_op jit(solution)/shard_map/ppermute | solution.py:414
  27.6 0.7 %collective-permute-start.8 = (bf16[128,2048]{1,0:T(8,128)(2,1)}, bf16[128,2048]{1,0:T(8,128)(2,1)S(1)}, u32[]{:S(2)}, u32[]{:S(2)}) collective-permute-start(bf16[128,2048]{1,0:T(8,128)(2,1)} %collective-permute-done.3.refs_1_), channel_id=1, source_target_pairs={{8,16}} | collective-permute-start | bytes 1572872 | tf_op jit(solution)/shard_map/ppermute | solution.py:430
  28.3 1.3 %add_block.14 = (f32[2,8,128,512]{3,2,1,0:T(8,128)S(1)}, f32[2,8,512]{2,1,0:T(8,128)S(1)}, f32[2,8,512]{2,1,0:T(8,128)S(1)}) custom-call(s32[34]{0:T(128)S(4)} %get-tuple-element.65.info_ref, bf16[128,4096]{1,0:T(8,128)(2,1)S(1)} %fetch_queries.1.q_ref, ...), custom_call_target="tpu_custom_call", output_to_operand_aliasing={{0}: (4, {}), {1}: (5, {}), {2}: (6, {})} | custom-call | flops 1000 | bytes 1024 | tf_op jit(solution)/shard_map/add_block/pallas_call | solution.py:329
  29.9 3.4 %collective-permute-start.7 = (bf16[128,2048]{1,0:T(8,128)(2,1)S(1)}, bf16[128,2048]{1,0:T(8,128)(2,1)S(1)}, u32[]{:S(2)}, u32[]{:S(2)}) collective-permute-start(bf16[128,2048]{1,0:T(8,128)(2,1)S(1)} %collective-permute-done.4.refs_1_), channel_id=1, source_target_pairs={{3,5},{5,7},{6,20},{7,6},{10,12},{12,14},{14,15},{15,13},{16,17},{... | collective-permute-start | bytes 1572872 | tf_op jit(solution)/shard_map/ppermute | solution.py:414
  33.2 1.3 %collective-permute-start.13 = (bf16[128,2048]{1,0:T(8,128)(2,1)S(1)}, bf16[128,2048]{1,0:T(8,128)(2,1)S(1)}, u32[]{:S(2)}, u32[]{:S(2)}) collective-permute-start(bf16[128,2048]{1,0:T(8,128)(2,1)S(1)} %get-tuple-element.112.kv_ref), channel_id=1, source_target_pairs={{8,16},{9,17},{10,18},{13,21},{14,22},{15,23}} | collective-permute-start | bytes 1572872 | tf_op jit(solution)/shard_map/ppermute | solution.py:435
  34.5 1.3 %collective-permute-start.12 = (bf16[128,2048]{1,0:T(8,128)(2,1)S(1)}, bf16[128,2048]{1,0:T(8,128)(2,1)S(1)}, u32[]{:S(2)}, u32[]{:S(2)}) collective-permute-start(bf16[128,2048]{1,0:T(8,128)(2,1)S(1)} %collective-permute-done.2.refs_1_), channel_id=1, source_target_pairs={{21,28}} | collective-permute-start | bytes 1572872 | tf_op jit(solution)/shard_map/ppermute | solution.py:434
  35.9 1.3 %add_block.15 = (f32[2,8,128,512]{3,2,1,0:T(8,128)S(1)}, f32[2,8,512]{2,1,0:T(8,128)S(1)}, f32[2,8,512]{2,1,0:T(8,128)S(1)}) custom-call(s32[34]{0:T(128)S(4)} %get-tuple-element.65.info_ref, bf16[128,4096]{1,0:T(8,128)(2,1)S(1)} %fetch_queries.1.q_ref, ...), custom_call_target="tpu_custom_call", output_to_operand_aliasing={{0}: (4, {}), {1}: (5, {}), {2}: (6, {})} | custom-call | flops 1000 | bytes 1024 | tf_op jit(solution)/shard_map/add_block/pallas_call | solution.py:329
  37.2 1.9 %collective-permute-start.11 = (bf16[128,2048]{1,0:T(8,128)(2,1)S(1)}, bf16[128,2048]{1,0:T(8,128)(2,1)S(1)}, u32[]{:S(2)}, u32[]{:S(2)}) collective-permute-start(bf16[128,2048]{1,0:T(8,128)(2,1)S(1)} %collective-permute-done.9.refs_1_), channel_id=1, source_target_pairs={{3,5},{5,7},{6,4},{7,6},{12,14},{13,19},{14,15},{15,13},{16,25},{1... | collective-permute-start | bytes 1572872 | tf_op jit(solution)/shard_map/ppermute | solution.py:414
  39.1 1.3 %add_block.16 = (f32[2,8,128,512]{3,2,1,0:T(8,128)S(1)}, f32[2,8,512]{2,1,0:T(8,128)S(1)}, f32[2,8,512]{2,1,0:T(8,128)S(1)}) custom-call(s32[34]{0:T(128)S(4)} %get-tuple-element.65.info_ref, bf16[128,4096]{1,0:T(8,128)(2,1)S(1)} %fetch_queries.1.q_ref, ...), custom_call_target="tpu_custom_call", output_to_operand_aliasing={{0}: (4, {}), {1}: (5, {}), {2}: (6, {})} | custom-call | flops 1000 | bytes 1024 | tf_op jit(solution)/shard_map/add_block/pallas_call | solution.py:329
  41.3 2.4 %collective-permute-done.13.refs_0_ = bf16[128,2048]{1,0:T(8,128)(2,1)S(1)} collective-permute-done((bf16[128,2048]{1,0:T(8,128)(2,1)S(1)}, bf16[128,2048]{1,0:T(8,128)(2,1)S(1)}, u32[]{:S(2)}, u32[]{:S(2)}) %collective-permute-start.13) | collective-permute-done | bytes 524320 | tf_op jit(solution)/shard_map/ppermute | solution.py:435
  43.8 4.5 %collective-permute-done.11.kv_ref.refs_1_ = bf16[128,2048]{1,0:T(8,128)(2,1)S(1)} collective-permute-done((bf16[128,2048]{1,0:T(8,128)(2,1)S(1)}, bf16[128,2048]{1,0:T(8,128)(2,1)S(1)}, u32[]{:S(2)}, u32[]{:S(2)}) %collective-permute-start.11) | collective-permute-done | bytes 524320 | tf_op jit(solution)/shard_map/ppermute | solution.py:414
  48.2 2.4 %last_block.1 = bf16[128,4096]{1,0:T(8,128)(2,1)} custom-call(s32[34]{0:T(128)S(4)} %get-tuple-element.65.info_ref, bf16[128,4096]{1,0:T(8,128)(2,1)S(1)} %fetch_queries.1.q_ref, bf16[128,4608]{1,0:T(8,128)(2,1)S(1)} %collective-permute-done.10.refs_0_, bf16[128,2048]{1,0:T(8,128)(2,1)S(1)} %collective-permute-done.11.kv_ref.refs_1_, ...), custom_call_target="tpu_custom_call" | custom-call | tf_op jit(solution)/shard_map/last_block/pallas_call | solution.py:360
  (20 shorter events, 1.8 us)
Async XLA Ops:
  0.0 16.4 %collective-permute-start = (bf16[128,4096]{1,0:T(8,128)(2,1)}, bf16[128,4096]{1,0:T(8,128)(2,1)S(1)}, u32[]{:S(2)}, u32[]{:S(2)}) collective-permute-start(bf16[128,4096]{1,0:T(8,128)(2,1)} %q_ref.1), channel_id=1, source_target_pairs={{0,8},{1,9},{2,10},{3,11},{4,12},{5,13},{6,14},{7,15},{8,0},{9,1},... | collective-permute-start | bytes 3145736 | tf_op jit(solution)/shard_map/ppermute | solution.py:424
  1.1 6.4 %collective-permute-start.1 = (bf16[128,2048]{1,0:T(8,128)(2,1)S(1)}, bf16[128,2048]{1,0:T(8,128)(2,1)S(1)}, u32[]{:S(2)}, u32[]{:S(2)}) collective-permute-start(bf16[128,2048]{1,0:T(8,128)(2,1)S(1)} %get-tuple-element.112.kv_ref), channel_id=1, source_target_pairs={{0,8},{1,9},{2,10},{3,11},{4,12},{5,13},{6,14},{7,15},{8,0},{9,1},... | collective-permute-start | bytes 1572872 | tf_op jit(solution)/shard_map/ppermute | solution.py:420
  1.7 11.2 %collective-permute-start.3 = (bf16[128,2048]{1,0:T(8,128)(2,1)S(1)}, bf16[128,2048]{1,0:T(8,128)(2,1)}, u32[]{:S(2)}, u32[]{:S(2)}) collective-permute-start(bf16[128,2048]{1,0:T(8,128)(2,1)S(1)} %get-tuple-element.112.kv_ref), channel_id=1, source_target_pairs={{0,1},{1,3},{2,0},{3,5},{5,7},{8,10},{9,8},{10,12},{11,25},{12,14}... | collective-permute-start | bytes 1572872 | tf_op jit(solution)/shard_map/ppermute | solution.py:414
  7.6 11.2 %collective-permute-start.2 = (bf16[128,2048]{1,0:T(8,128)(2,1)S(1)}, bf16[128,2048]{1,0:T(8,128)(2,1)S(1)}, u32[]{:S(2)}, u32[]{:S(2)}) collective-permute-start(bf16[128,2048]{1,0:T(8,128)(2,1)S(1)} %collective-permute-done.1.refs_0_), channel_id=1, source_target_pairs={{0,1},{1,3},{2,16},{3,5},{4,18},{5,7},{6,20},{7,22},{8,10},{9,8},{... | collective-permute-start | bytes 1572872 | tf_op jit(solution)/shard_map/ppermute | solution.py:414
  10.0 13.2 %collective-permute-start.6 = (bf16[128,2048]{1,0:T(8,128)(2,1)S(1)}, bf16[128,2048]{1,0:T(8,128)(2,1)S(1)}, u32[]{:S(2)}, u32[]{:S(2)}) collective-permute-start(bf16[128,2048]{1,0:T(8,128)(2,1)S(1)} %get-tuple-element.112.kv_ref), channel_id=1, source_target_pairs={{26,27},{11,19},{12,20}} | collective-permute-start | bytes 1572872 | tf_op jit(solution)/shard_map/ppermute | solution.py:426
  12.9 11.4 %collective-permute-start.5 = (bf16[128,2048]{1,0:T(8,128)(2,1)}, bf16[128,2048]{1,0:T(8,128)(2,1)S(1)}, u32[]{:S(2)}, u32[]{:S(2)}) collective-permute-start(bf16[128,2048]{1,0:T(8,128)(2,1)} %collective-permute-done.3.refs_1_), channel_id=1, source_target_pairs={{0,1},{1,3},{3,5},{5,7},{7,6},{8,10},{10,12},{12,14},{14,15},{15,2... | collective-permute-start | bytes 1572872 | tf_op jit(solution)/shard_map/ppermute | solution.py:414
  18.7 11.1 %collective-permute-start.4 = (bf16[128,2048]{1,0:T(8,128)(2,1)S(1)}, bf16[128,2048]{1,0:T(8,128)(2,1)S(1)}, u32[]{:S(2)}, u32[]{:S(2)}) collective-permute-start(bf16[128,2048]{1,0:T(8,128)(2,1)S(1)} %collective-permute-done.2.refs_1_), channel_id=1, source_target_pairs={{1,3},{3,5},{5,7},{7,6},{8,10},{10,12},{12,14},{14,15},{16,17},{17... | collective-permute-start | bytes 1572872 | tf_op jit(solution)/shard_map/ppermute | solution.py:414
  24.2 12.9 %collective-permute-start.9 = (bf16[128,2048]{1,0:T(8,128)(2,1)S(1)}, bf16[128,2048]{1,0:T(8,128)(2,1)S(1)}, u32[]{:S(2)}, u32[]{:S(2)}) collective-permute-start(bf16[128,2048]{1,0:T(8,128)(2,1)S(1)} %collective-permute-done.5.refs_1_), channel_id=1, source_target_pairs={{1,3},{3,5},{5,7},{7,6},{10,12},{12,14},{14,15},{15,13},{16,17},{1... | collective-permute-start | bytes 1572872 | tf_op jit(solution)/shard_map/ppermute | solution.py:414
  27.6 12.8 %collective-permute-start.8 = (bf16[128,2048]{1,0:T(8,128)(2,1)}, bf16[128,2048]{1,0:T(8,128)(2,1)S(1)}, u32[]{:S(2)}, u32[]{:S(2)}) collective-permute-start(bf16[128,2048]{1,0:T(8,128)(2,1)} %collective-permute-done.3.refs_1_), channel_id=1, source_target_pairs={{8,16}} | collective-permute-start | bytes 1572872 | tf_op jit(solution)/shard_map/ppermute | solution.py:430
  29.9 11.2 %collective-permute-start.7 = (bf16[128,2048]{1,0:T(8,128)(2,1)S(1)}, bf16[128,2048]{1,0:T(8,128)(2,1)S(1)}, u32[]{:S(2)}, u32[]{:S(2)}) collective-permute-start(bf16[128,2048]{1,0:T(8,128)(2,1)S(1)} %collective-permute-done.4.refs_1_), channel_id=1, source_target_pairs={{3,5},{5,7},{6,20},{7,6},{10,12},{12,14},{14,15},{15,13},{16,17},{... | collective-permute-start | bytes 1572872 | tf_op jit(solution)/shard_map/ppermute | solution.py:414
  33.2 10.5 %collective-permute-start.13 = (bf16[128,2048]{1,0:T(8,128)(2,1)S(1)}, bf16[128,2048]{1,0:T(8,128)(2,1)S(1)}, u32[]{:S(2)}, u32[]{:S(2)}) collective-permute-start(bf16[128,2048]{1,0:T(8,128)(2,1)S(1)} %get-tuple-element.112.kv_ref), channel_id=1, source_target_pairs={{8,16},{9,17},{10,18},{13,21},{14,22},{15,23}} | collective-permute-start | bytes 1572872 | tf_op jit(solution)/shard_map/ppermute | solution.py:435
  34.5 9.2 %collective-permute-start.12 = (bf16[128,2048]{1,0:T(8,128)(2,1)S(1)}, bf16[128,2048]{1,0:T(8,128)(2,1)S(1)}, u32[]{:S(2)}, u32[]{:S(2)}) collective-permute-start(bf16[128,2048]{1,0:T(8,128)(2,1)S(1)} %collective-permute-done.2.refs_1_), channel_id=1, source_target_pairs={{21,28}} | collective-permute-start | bytes 1572872 | tf_op jit(solution)/shard_map/ppermute | solution.py:434
  37.2 11.1 %collective-permute-start.11 = (bf16[128,2048]{1,0:T(8,128)(2,1)S(1)}, bf16[128,2048]{1,0:T(8,128)(2,1)S(1)}, u32[]{:S(2)}, u32[]{:S(2)}) collective-permute-start(bf16[128,2048]{1,0:T(8,128)(2,1)S(1)} %collective-permute-done.9.refs_1_), channel_id=1, source_target_pairs={{3,5},{5,7},{6,4},{7,6},{12,14},{13,19},{14,15},{15,13},{16,25},{1... | collective-permute-start | bytes 1572872 | tf_op jit(solution)/shard_map/ppermute | solution.py:414
  41.2 7.0 %collective-permute-start.10 = (bf16[128,4608]{1,0:T(8,128)(2,1)S(1)}, bf16[128,4608]{1,0:T(8,128)(2,1)S(1)}, u32[]{:S(2)}, u32[]{:S(2)}) collective-permute-start(bf16[128,4608]{1,0:T(8,128)(2,1)S(1)} %get-tuple-element.109), channel_id=1, source_target_pairs={{0,8},{1,9},{2,10},{3,11},{4,12},{5,13},{6,14},{7,15},{8,0},{9,1},... | collective-permute-start | bytes 3538952 | tf_op jit(solution)/shard_map/ppermute | solution.py:444

commit v8 on v6

--- a/solution.py
+++ b/solution.py
@@ -427,10 +427,11 @@
     u2 = send(after(u1), "own", 2)
     add(7, q, None, kvm, clear=True)
     add(0, q, qm, u1)
+    near2 = lax.ppermute(after(u1), AXES, beside[2])
     w2 = send(after(w1), "mate", 2)
     add(1, q, qm, w1)
     add(9, q, None, near[0])
-    near += [lax.ppermute(after(w1), AXES, beside[1]), lax.ppermute(u1, AXES, beside[2])]
+    near += [lax.ppermute(after(w1), AXES, beside[1])]
     kv8 = lax.ppermute(after(kv), AXES, [x for x in eight_back if x not in busy])
     u3 = send(after(u2), "own", 3)
     add(2, q, qm, u2)
@@ -438,7 +439,7 @@
     add(3, q, qm, w2)
     u4 = send(after(u3), "own", 4)
     add(4, q, qm, u3)
-    add(11, q, None, near[2])
+    add(11, q, None, near2)
     mine = part(5, q, qm, w3)
     theirs = lax.ppermute(mine, AXES, mates)
     add(8, q, None, kv8)

time: 50.4 us -> 50.9 us (level)
  the two profiles are of different devices: /device:TPU:16 before, /device:TPU:22 now
where the time goes in v8:
time: 50.9 us; the launch traced here: 50.8 us
  starting transfers between devices  25.7 us (50%)
  waiting for transfers between devices  13.7 us (27%)
  Pallas kernels  11 us (22%)
    ppermute x7, starting transfers between devices, send(): lax.ppermute(block, AXES, sorted(((e, d) for d, (e, _) in route[op, step]...  21 us
    ppermute x7, waiting for transfers between devices, send(): lax.ppermute(block, AXES, sorted(((e, d) for d, (e, _) in route[op, step]...  11.3 us
    pallas_call x13, Pallas kernels, call(): pl.pallas_call(kernel, out_shape=out, in_specs=[smem] + [vmem] * (len(arr...  6.28 us
    ppermute x1, waiting for transfers between devices, ring_shards(): lax.ppermute(after(kv), AXES, [x for x in eight_back if x not in busy])  2.39 us
    pallas_call x1, Pallas kernels, last(): pl.pallas_call(functools.partial(last_kernel, sizes, n_docs, slot, mated)...  2.35 us
    ppermute x1, starting transfers between devices, ring_shards(): near += [lax.ppermute(after(w1), AXES, beside[1])]  1.32 us
    ppermute x1, starting transfers between devices, ring_shards(): lax.ppermute(after(kv), AXES, [x for x in eight_back if x not in busy])  1.29 us
    pallas_call x1, Pallas kernels, fetched(): pl.pallas_call(fetch_kernel, out_shape=pltpu.VMEM(queries.shape, queries....  1.24 us
  transfers between devices with their start and end apart: 14, of which 6 were waited for; matrix products, arithmetic and copies ran while one was open for 0% of the time, Pallas kernels for 17%

profile of v8, /device:TPU:22, one launch (start us, length us, event | category | flops | bytes accessed | tf_op | source)
XLA Modules:
  0.0 50.8 jit_solution(3408323207293892093)
XLA Ops:
  0.0 1.1 %pack_keys_values.1 = (bf16[128,2048]{1,0:T(8,128)(2,1)S(1)}, s32[34]{0:T(128)S(4)}) custom-call(s32[8]{0:T(128)} %refs_0_.1, s32[8]{0:T(128)} %refs_1_.1, s32[32,25]{1,0:T(8,128)} %constant.2.clone.refs_2_, bf16[128,1024]{1,0:T(8,128)(2,1)} %refs_3_.1, bf16[128,1024]{1,0:T(8,128)(2,1)} %refs_4_.1), custom_call_target="tpu_custom_call" | custom-call | tf_op jit(solution)/shard_map/pack_keys_values/pallas_call | solution.py:385
  1.7 3.5 %collective-permute-start.3 = (bf16[128,2048]{1,0:T(8,128)(2,1)S(1)}, bf16[128,2048]{1,0:T(8,128)(2,1)}, u32[]{:S(2)}, u32[]{:S(2)}) collective-permute-start(bf16[128,2048]{1,0:T(8,128)(2,1)S(1)} %get-tuple-element.112.kv_ref), channel_id=1, source_target_pairs={{0,1},{1,3},{2,0},{3,5},{5,7},{8,10},{9,8},{10,12},{11,25},{12,14}... | collective-permute-start | bytes 1572872 | tf_op jit(solution)/shard_map/ppermute | solution.py:414
  5.2 1.2 %fetch_queries.1.q_ref = bf16[128,4096]{1,0:T(8,128)(2,1)S(1)} custom-call(bf16[128,4096]{1,0:T(8,128)(2,1)} %q_ref.1), custom_call_target="tpu_custom_call" | custom-call | tf_op jit(solution)/shard_map/fetch_queries/pallas_call | solution.py:198
  6.4 1.1 %own_block.1 = (f32[2,8,128,512]{3,2,1,0:T(8,128)S(1)}, f32[2,8,512]{2,1,0:T(8,128)S(1)}, f32[2,8,512]{2,1,0:T(8,128)S(1)}) custom-call(s32[34]{0:T(128)S(4)} %get-tuple-element.65.info_ref, bf16[128,4096]{1,0:T(8,128)(2,1)S(1)} %fetch_queries.1.q_ref, bf16[128,2048]{1,0:T(8,128)(2,1)S(1)} %get-tuple-element.112.kv_ref), custom_call_target="tpu_custom_call" | custom-call | flops 1000 | bytes 1024 | tf_op jit(solution)/shard_map/own_block/pallas_call | solution.py:329
  7.5 2.4 %collective-permute-start.2 = (bf16[128,2048]{1,0:T(8,128)(2,1)S(1)}, bf16[128,2048]{1,0:T(8,128)(2,1)S(1)}, u32[]{:S(2)}, u32[]{:S(2)}) collective-permute-start(bf16[128,2048]{1,0:T(8,128)(2,1)S(1)} %collective-permute-done.1.refs_0_), channel_id=1, source_target_pairs={{0,1},{1,3},{2,16},{3,5},{4,18},{5,7},{6,20},{7,22},{8,10},{9,8},{... | collective-permute-start | bytes 1572872 | tf_op jit(solution)/shard_map/ppermute | solution.py:414
  10.0 0.7 %collective-permute-start.6 = (bf16[128,2048]{1,0:T(8,128)(2,1)S(1)}, bf16[128,2048]{1,0:T(8,128)(2,1)S(1)}, u32[]{:S(2)}, u32[]{:S(2)}) collective-permute-start(bf16[128,2048]{1,0:T(8,128)(2,1)S(1)} %get-tuple-element.112.kv_ref), channel_id=1, source_target_pairs={{26,27},{11,19},{12,20}} | collective-permute-start | bytes 1572872 | tf_op jit(solution)/shard_map/ppermute | solution.py:426
  10.7 2.2 %collective-permute-done.3.refs_1_ = bf16[128,2048]{1,0:T(8,128)(2,1)} collective-permute-done((bf16[128,2048]{1,0:T(8,128)(2,1)S(1)}, bf16[128,2048]{1,0:T(8,128)(2,1)}, u32[]{:S(2)}, u32[]{:S(2)}) %collective-permute-start.3) | collective-permute-done | bytes 524320 | tf_op jit(solution)/shard_map/ppermute | solution.py:414
  12.9 3.5 %collective-permute-start.5 = (bf16[128,2048]{1,0:T(8,128)(2,1)}, bf16[128,2048]{1,0:T(8,128)(2,1)S(1)}, u32[]{:S(2)}, u32[]{:S(2)}) collective-permute-start(bf16[128,2048]{1,0:T(8,128)(2,1)} %collective-permute-done.3.refs_1_), channel_id=1, source_target_pairs={{0,1},{1,3},{3,5},{5,7},{7,6},{8,10},{10,12},{12,14},{14,15},{15,2... | collective-permute-start | bytes 1572872 | tf_op jit(solution)/shard_map/ppermute | solution.py:414
  16.5 2.3 %add_block.11 = (f32[2,8,128,512]{3,2,1,0:T(8,128)S(1)}, f32[2,8,512]{2,1,0:T(8,128)S(1)}, f32[2,8,512]{2,1,0:T(8,128)S(1)}) custom-call(s32[34]{0:T(128)S(4)} %get-tuple-element.65.info_ref, bf16[128,4096]{1,0:T(8,128)(2,1)S(1)} %fetch_queries.1.q_ref, ...), custom_call_target="tpu_custom_call", output_to_operand_aliasing={{0}: (4, {}), {1}: (5, {}), {2}: (6, {})} | custom-call | flops 1000 | bytes 1024 | tf_op jit(solution)/shard_map/add_block/pallas_call | solution.py:329
  18.8 3.0 %collective-permute-start.4 = (bf16[128,2048]{1,0:T(8,128)(2,1)S(1)}, bf16[128,2048]{1,0:T(8,128)(2,1)S(1)}, u32[]{:S(2)}, u32[]{:S(2)}) collective-permute-start(bf16[128,2048]{1,0:T(8,128)(2,1)S(1)} %collective-permute-done.2.refs_1_), channel_id=1, source_target_pairs={{1,3},{3,5},{5,7},{7,6},{8,10},{10,12},{12,14},{14,15},{16,17},{17... | collective-permute-start | bytes 1572872 | tf_op jit(solution)/shard_map/ppermute | solution.py:414
  21.9 1.3 %add_block.12 = (f32[2,8,128,512]{3,2,1,0:T(8,128)S(1)}, f32[2,8,512]{2,1,0:T(8,128)S(1)}, f32[2,8,512]{2,1,0:T(8,128)S(1)}) custom-call(s32[34]{0:T(128)S(4)} %get-tuple-element.65.info_ref, bf16[128,4096]{1,0:T(8,128)(2,1)S(1)} %fetch_queries.1.q_ref, ...), custom_call_target="tpu_custom_call", output_to_operand_aliasing={{0}: (4, {}), {1}: (5, {}), {2}: (6, {})} | custom-call | flops 1000 | bytes 1024 | tf_op jit(solution)/shard_map/add_block/pallas_call | solution.py:329
  23.2 1.1 %collective-permute-done.5.refs_1_ = bf16[128,2048]{1,0:T(8,128)(2,1)S(1)} collective-permute-done((bf16[128,2048]{1,0:T(8,128)(2,1)}, bf16[128,2048]{1,0:T(8,128)(2,1)S(1)}, u32[]{:S(2)}, u32[]{:S(2)}) %collective-permute-start.5) | collective-permute-done | bytes 524320 | tf_op jit(solution)/shard_map/ppermute | solution.py:414
  24.2 3.4 %collective-permute-start.9 = (bf16[128,2048]{1,0:T(8,128)(2,1)S(1)}, bf16[128,2048]{1,0:T(8,128)(2,1)S(1)}, u32[]{:S(2)}, u32[]{:S(2)}) collective-permute-start(bf16[128,2048]{1,0:T(8,128)(2,1)S(1)} %collective-permute-done.5.refs_1_), channel_id=1, source_target_pairs={{1,3},{3,5},{5,7},{7,6},{10,12},{12,14},{14,15},{15,13},{16,17},{1... | collective-permute-start | bytes 1572872 | tf_op jit(solution)/shard_map/ppermute | solution.py:414
  27.6 0.7 %collective-permute-start.8 = (bf16[128,2048]{1,0:T(8,128)(2,1)}, bf16[128,2048]{1,0:T(8,128)(2,1)S(1)}, u32[]{:S(2)}, u32[]{:S(2)}) collective-permute-start(bf16[128,2048]{1,0:T(8,128)(2,1)} %collective-permute-done.3.refs_1_), channel_id=1, source_target_pairs={{8,16}} | collective-permute-start | bytes 1572872 | tf_op jit(solution)/shard_map/ppermute | solution.py:430
  28.3 1.6 %collective-permute-done.4.refs_1_ = bf16[128,2048]{1,0:T(8,128)(2,1)S(1)} collective-permute-done((bf16[128,2048]{1,0:T(8,128)(2,1)S(1)}, bf16[128,2048]{1,0:T(8,128)(2,1)S(1)}, u32[]{:S(2)}, u32[]{:S(2)}) %collective-permute-start.4) | collective-permute-done | bytes 524320 | tf_op jit(solution)/shard_map/ppermute | solution.py:414
  29.9 3.3 %collective-permute-start.7 = (bf16[128,2048]{1,0:T(8,128)(2,1)S(1)}, bf16[128,2048]{1,0:T(8,128)(2,1)S(1)}, u32[]{:S(2)}, u32[]{:S(2)}) collective-permute-start(bf16[128,2048]{1,0:T(8,128)(2,1)S(1)} %collective-permute-done.4.refs_1_), channel_id=1, source_target_pairs={{3,5},{5,7},{6,20},{7,6},{10,12},{12,14},{14,15},{15,13},{16,17},{... | collective-permute-start | bytes 1572872 | tf_op jit(solution)/shard_map/ppermute | solution.py:414
  33.2 1.3 %collective-permute-start.13 = (bf16[128,2048]{1,0:T(8,128)(2,1)S(1)}, bf16[128,2048]{1,0:T(8,128)(2,1)S(1)}, u32[]{:S(2)}, u32[]{:S(2)}) collective-permute-start(bf16[128,2048]{1,0:T(8,128)(2,1)S(1)} %get-tuple-element.112.kv_ref), channel_id=1, source_target_pairs={{8,16},{9,17},{10,18},{13,21},{14,22},{15,23}} | collective-permute-start | bytes 1572872 | tf_op jit(solution)/shard_map/ppermute | solution.py:435
  34.5 1.3 %collective-permute-start.12 = (bf16[128,2048]{1,0:T(8,128)(2,1)S(1)}, bf16[128,2048]{1,0:T(8,128)(2,1)S(1)}, u32[]{:S(2)}, u32[]{:S(2)}) collective-permute-start(bf16[128,2048]{1,0:T(8,128)(2,1)S(1)} %collective-permute-done.2.refs_1_), channel_id=1, source_target_pairs={{21,28}} | collective-permute-start | bytes 1572872 | tf_op jit(solution)/shard_map/ppermute | solution.py:434
  35.9 1.3 %add_block.15 = (f32[2,8,128,512]{3,2,1,0:T(8,128)S(1)}, f32[2,8,512]{2,1,0:T(8,128)S(1)}, f32[2,8,512]{2,1,0:T(8,128)S(1)}) custom-call(s32[34]{0:T(128)S(4)} %get-tuple-element.65.info_ref, bf16[128,4096]{1,0:T(8,128)(2,1)S(1)} %fetch_queries.1.q_ref, ...), custom_call_target="tpu_custom_call", output_to_operand_aliasing={{0}: (4, {}), {1}: (5, {}), {2}: (6, {})} | custom-call | flops 1000 | bytes 1024 | tf_op jit(solution)/shard_map/add_block/pallas_call | solution.py:329
  37.2 1.9 %collective-permute-start.11 = (bf16[128,2048]{1,0:T(8,128)(2,1)S(1)}, bf16[128,2048]{1,0:T(8,128)(2,1)S(1)}, u32[]{:S(2)}, u32[]{:S(2)}) collective-permute-start(bf16[128,2048]{1,0:T(8,128)(2,1)S(1)} %collective-permute-done.9.refs_1_), channel_id=1, source_target_pairs={{3,5},{5,7},{6,4},{7,6},{12,14},{13,19},{14,15},{15,13},{16,25},{1... | collective-permute-start | bytes 1572872 | tf_op jit(solution)/shard_map/ppermute | solution.py:414
  39.1 2.0 %collective-permute-done.7.kv_ref = bf16[128,2048]{1,0:T(8,128)(2,1)S(1)} collective-permute-done((bf16[128,2048]{1,0:T(8,128)(2,1)S(1)}, bf16[128,2048]{1,0:T(8,128)(2,1)S(1)}, u32[]{:S(2)}, u32[]{:S(2)}) %collective-permute-start.7) | collective-permute-done | bytes 524320 | tf_op jit(solution)/shard_map/ppermute | solution.py:414
  41.4 2.4 %collective-permute-done.13.refs_0_ = bf16[128,2048]{1,0:T(8,128)(2,1)S(1)} collective-permute-done((bf16[128,2048]{1,0:T(8,128)(2,1)S(1)}, bf16[128,2048]{1,0:T(8,128)(2,1)S(1)}, u32[]{:S(2)}, u32[]{:S(2)}) %collective-permute-start.13) | collective-permute-done | bytes 524320 | tf_op jit(solution)/shard_map/ppermute | solution.py:435
  43.8 4.5 %collective-permute-done.11.kv_ref.refs_1_ = bf16[128,2048]{1,0:T(8,128)(2,1)S(1)} collective-permute-done((bf16[128,2048]{1,0:T(8,128)(2,1)S(1)}, bf16[128,2048]{1,0:T(8,128)(2,1)S(1)}, u32[]{:S(2)}, u32[]{:S(2)}) %collective-permute-start.11) | collective-permute-done | bytes 524320 | tf_op jit(solution)/shard_map/ppermute | solution.py:414
  48.2 2.4 %last_block.1 = bf16[128,4096]{1,0:T(8,128)(2,1)} custom-call(s32[34]{0:T(128)S(4)} %get-tuple-element.65.info_ref, bf16[128,4096]{1,0:T(8,128)(2,1)S(1)} %fetch_queries.1.q_ref, bf16[128,4608]{1,0:T(8,128)(2,1)S(1)} %collective-permute-done.10.refs_0_, bf16[128,2048]{1,0:T(8,128)(2,1)S(1)} %collective-permute-done.11.kv_ref.refs_1_, ...), custom_call_target="tpu_custom_call" | custom-call | tf_op jit(solution)/shard_map/last_block/pallas_call | solution.py:360
  (20 shorter events, 1.0 us)
Async XLA Ops:
  0.0 16.5 %collective-permute-start = (bf16[128,4096]{1,0:T(8,128)(2,1)}, bf16[128,4096]{1,0:T(8,128)(2,1)S(1)}, u32[]{:S(2)}, u32[]{:S(2)}) collective-permute-start(bf16[128,4096]{1,0:T(8,128)(2,1)} %q_ref.1), channel_id=1, source_target_pairs={{0,8},{1,9},{2,10},{3,11},{4,12},{5,13},{6,14},{7,15},{8,0},{9,1},... | collective-permute-start | bytes 3145736 | tf_op jit(solution)/shard_map/ppermute | solution.py:424
  1.1 6.4 %collective-permute-start.1 = (bf16[128,2048]{1,0:T(8,128)(2,1)S(1)}, bf16[128,2048]{1,0:T(8,128)(2,1)S(1)}, u32[]{:S(2)}, u32[]{:S(2)}) collective-permute-start(bf16[128,2048]{1,0:T(8,128)(2,1)S(1)} %get-tuple-element.112.kv_ref), channel_id=1, source_target_pairs={{0,8},{1,9},{2,10},{3,11},{4,12},{5,13},{6,14},{7,15},{8,0},{9,1},... | collective-permute-start | bytes 1572872 | tf_op jit(solution)/shard_map/ppermute | solution.py:420
  1.7 11.2 %collective-permute-start.3 = (bf16[128,2048]{1,0:T(8,128)(2,1)S(1)}, bf16[128,2048]{1,0:T(8,128)(2,1)}, u32[]{:S(2)}, u32[]{:S(2)}) collective-permute-start(bf16[128,2048]{1,0:T(8,128)(2,1)S(1)} %get-tuple-element.112.kv_ref), channel_id=1, source_target_pairs={{0,1},{1,3},{2,0},{3,5},{5,7},{8,10},{9,8},{10,12},{11,25},{12,14}... | collective-permute-start | bytes 1572872 | tf_op jit(solution)/shard_map/ppermute | solution.py:414
  7.5 11.3 %collective-permute-start.2 = (bf16[128,2048]{1,0:T(8,128)(2,1)S(1)}, bf16[128,2048]{1,0:T(8,128)(2,1)S(1)}, u32[]{:S(2)}, u32[]{:S(2)}) collective-permute-start(bf16[128,2048]{1,0:T(8,128)(2,1)S(1)} %collective-permute-done.1.refs_0_), channel_id=1, source_target_pairs={{0,1},{1,3},{2,16},{3,5},{4,18},{5,7},{6,20},{7,22},{8,10},{9,8},{... | collective-permute-start | bytes 1572872 | tf_op jit(solution)/shard_map/ppermute | solution.py:414
  10.0 13.2 %collective-permute-start.6 = (bf16[128,2048]{1,0:T(8,128)(2,1)S(1)}, bf16[128,2048]{1,0:T(8,128)(2,1)S(1)}, u32[]{:S(2)}, u32[]{:S(2)}) collective-permute-start(bf16[128,2048]{1,0:T(8,128)(2,1)S(1)} %get-tuple-element.112.kv_ref), channel_id=1, source_target_pairs={{26,27},{11,19},{12,20}} | collective-permute-start | bytes 1572872 | tf_op jit(solution)/shard_map/ppermute | solution.py:426
  12.9 11.4 %collective-permute-start.5 = (bf16[128,2048]{1,0:T(8,128)(2,1)}, bf16[128,2048]{1,0:T(8,128)(2,1)S(1)}, u32[]{:S(2)}, u32[]{:S(2)}) collective-permute-start(bf16[128,2048]{1,0:T(8,128)(2,1)} %collective-permute-done.3.refs_1_), channel_id=1, source_target_pairs={{0,1},{1,3},{3,5},{5,7},{7,6},{8,10},{10,12},{12,14},{14,15},{15,2... | collective-permute-start | bytes 1572872 | tf_op jit(solution)/shard_map/ppermute | solution.py:414
  18.8 11.1 %collective-permute-start.4 = (bf16[128,2048]{1,0:T(8,128)(2,1)S(1)}, bf16[128,2048]{1,0:T(8,128)(2,1)S(1)}, u32[]{:S(2)}, u32[]{:S(2)}) collective-permute-start(bf16[128,2048]{1,0:T(8,128)(2,1)S(1)} %collective-permute-done.2.refs_1_), channel_id=1, source_target_pairs={{1,3},{3,5},{5,7},{7,6},{8,10},{10,12},{12,14},{14,15},{16,17},{17... | collective-permute-start | bytes 1572872 | tf_op jit(solution)/shard_map/ppermute | solution.py:414
  24.2 12.9 %collective-permute-start.9 = (bf16[128,2048]{1,0:T(8,128)(2,1)S(1)}, bf16[128,2048]{1,0:T(8,128)(2,1)S(1)}, u32[]{:S(2)}, u32[]{:S(2)}) collective-permute-start(bf16[128,2048]{1,0:T(8,128)(2,1)S(1)} %collective-permute-done.5.refs_1_), channel_id=1, source_target_pairs={{1,3},{3,5},{5,7},{7,6},{10,12},{12,14},{14,15},{15,13},{16,17},{1... | collective-permute-start | bytes 1572872 | tf_op jit(solution)/shard_map/ppermute | solution.py:414
  27.6 11.5 %collective-permute-start.8 = (bf16[128,2048]{1,0:T(8,128)(2,1)}, bf16[128,2048]{1,0:T(8,128)(2,1)S(1)}, u32[]{:S(2)}, u32[]{:S(2)}) collective-permute-start(bf16[128,2048]{1,0:T(8,128)(2,1)} %collective-permute-done.3.refs_1_), channel_id=1, source_target_pairs={{8,16}} | collective-permute-start | bytes 1572872 | tf_op jit(solution)/shard_map/ppermute | solution.py:430
  29.9 11.2 %collective-permute-start.7 = (bf16[128,2048]{1,0:T(8,128)(2,1)S(1)}, bf16[128,2048]{1,0:T(8,128)(2,1)S(1)}, u32[]{:S(2)}, u32[]{:S(2)}) collective-permute-start(bf16[128,2048]{1,0:T(8,128)(2,1)S(1)} %collective-permute-done.4.refs_1_), channel_id=1, source_target_pairs={{3,5},{5,7},{6,20},{7,6},{10,12},{12,14},{14,15},{15,13},{16,17},{... | collective-permute-start | bytes 1572872 | tf_op jit(solution)/shard_map/ppermute | solution.py:414
  33.2 10.5 %collective-permute-start.13 = (bf16[128,2048]{1,0:T(8,128)(2,1)S(1)}, bf16[128,2048]{1,0:T(8,128)(2,1)S(1)}, u32[]{:S(2)}, u32[]{:S(2)}) collective-permute-start(bf16[128,2048]{1,0:T(8,128)(2,1)S(1)} %get-tuple-element.112.kv_ref), channel_id=1, source_target_pairs={{8,16},{9,17},{10,18},{13,21},{14,22},{15,23}} | collective-permute-start | bytes 1572872 | tf_op jit(solution)/shard_map/ppermute | solution.py:435
  34.5 9.2 %collective-permute-start.12 = (bf16[128,2048]{1,0:T(8,128)(2,1)S(1)}, bf16[128,2048]{1,0:T(8,128)(2,1)S(1)}, u32[]{:S(2)}, u32[]{:S(2)}) collective-permute-start(bf16[128,2048]{1,0:T(8,128)(2,1)S(1)} %collective-permute-done.2.refs_1_), channel_id=1, source_target_pairs={{21,28}} | collective-permute-start | bytes 1572872 | tf_op jit(solution)/shard_map/ppermute | solution.py:434
  37.2 11.1 %collective-permute-start.11 = (bf16[128,2048]{1,0:T(8,128)(2,1)S(1)}, bf16[128,2048]{1,0:T(8,128)(2,1)S(1)}, u32[]{:S(2)}, u32[]{:S(2)}) collective-permute-start(bf16[128,2048]{1,0:T(8,128)(2,1)S(1)} %collective-permute-done.9.refs_1_), channel_id=1, source_target_pairs={{3,5},{5,7},{6,4},{7,6},{12,14},{13,19},{14,15},{15,13},{16,25},{1... | collective-permute-start | bytes 1572872 | tf_op jit(solution)/shard_map/ppermute | solution.py:414
  41.3 7.0 %collective-permute-start.10 = (bf16[128,4608]{1,0:T(8,128)(2,1)S(1)}, bf16[128,4608]{1,0:T(8,128)(2,1)S(1)}, u32[]{:S(2)}, u32[]{:S(2)}) collective-permute-start(bf16[128,4608]{1,0:T(8,128)(2,1)S(1)} %get-tuple-element.109), channel_id=1, source_target_pairs={{0,8},{1,9},{2,10},{3,11},{4,12},{5,13},{6,14},{7,15},{8,0},{9,1},... | collective-permute-start | bytes 3538952 | tf_op jit(solution)/shard_map/ppermute | solution.py:444
